TPU v7x, 32 devices: a whole 2x2x4 slice. The times are simulated.
32 devices in a mesh: grp: 2 (over x), node: 16 (over z, y, core).
Axes of the slice: x: 2, y: 2, z: 4, core: 2. Of those that a mesh axis runs over, the one named last changes fastest.
Arguments:
- blocks: float32 [3072, 128, 128], P(('grp', 'node')), parts along dimension 0, may hold values from 0.001 to 0.03
- block_row: int32 [3072], P(('grp', 'node')), parts along dimension 0, may hold values from 0 to 127, as said below
- block_patch: int32 [3072], P(('grp', 'node')), parts along dimension 0, may hold values from 0 to 7
- block_count: int32 [32], P(('grp', 'node')), parts along dimension 0, may hold values from 48 to 96, as said below
- row_map: int32 [256], P('grp'), parts along dimension 0, may hold values from 0 to 127, as said below
- sinogram: float32 [8, 16384], P('grp', 'node'), parts along dimension 0, may hold values from -96 to 96
- start: float32 [8, 16384], P('grp', 'node'), parts along dimension 0, may hold values from -6 to 6
Outputs:
- image: float32 [8, 16384], P('grp', 'node'), parts along dimension 0
- weighted: float32 [8, 16384], P('grp', 'node'), parts along dimension 0
There are 2 independent parts, one for each index of `grp`. A program takes and returns all parts, laid end to end along the dimension named above; each array names one. Nothing has to cross between parts.
Inputs may be any that keep to these rules, and one draw needn't show every extreme that they name: `block_row`: of the 96 slots of one device, at most 6 have rows whose sinogram positions lie in one device's range (8 e to 8 e + 7); in every draw some device's range receives exactly 6 slots from every device. Slots from block_count on of a device are not part of the matrix; some device uses all 96. `row_map`: A permutation of the row blocks.
All inputs are finite; a program needn't handle non-finite values.
Results may differ from a plain program's by a relative error of at most 0.0001.
Values sent between devices are 32-bit elements; how exact they have to be, the bound alone decides.
No kernel may reach another device: no remote copies, remote signals or barrier semaphores. Data moves between devices by JAX's collectives and lax.ppermute only.
A program may use at most 64 MiB of HBM per device.

v0:
```python
import jax
import jax.numpy as jnp
from jax import lax
from jax.sharding import PartitionSpec as P

ITERS = 2


relax_factor = 1.9


def body(blocks, block_row, block_patch, block_count, row_map, sinogram, start):
    highest = lax.Precision.HIGHEST
    nodes = lax.axis_size("node")
    count_blocks = blocks.shape[0]
    width = blocks.shape[1]
    slices = start.shape[0]
    patches = start.shape[1] // width
    row_blocks = sinogram.shape[1] // width
    total_rows = row_map.shape[0]
    half_pairs = count_blocks // 2
    capacity = 2 * ((half_pairs + nodes - 1) // nodes)
    live = (jnp.arange(count_blocks, dtype=jnp.int32) < block_count[0]).astype(jnp.float32)
    matches = block_row[:, None] == jnp.arange(total_rows, dtype=jnp.int32)[None, :]
    position = jnp.sum(jnp.where(matches, row_map[None, :], 0), axis=1)
    target = position // row_blocks
    local_row = position % row_blocks
    dest_hot = (target[:, None] == jnp.arange(nodes, dtype=jnp.int32)[None, :]).astype(jnp.int32)
    earlier = jnp.cumsum(dest_hot, axis=0) - dest_hot
    slot_id = target * capacity + jnp.sum(earlier * dest_hot, axis=1)
    labels = (
        jnp.zeros((nodes * capacity,), jnp.int32)
        .at[slot_id]
        .set(local_row)
        .reshape(nodes, capacity)
    )
    patch_hot = (jnp.arange(patches, dtype=jnp.int32)[:, None] == block_patch[None, :]).astype(
        jnp.float32
    )
    col_totals = jnp.einsum(
        "pj,jc->pc", patch_hot * live[None, :], jnp.sum(blocks, axis=1), precision=highest
    )
    col_weight = 1.0 / (col_totals + 1.0)
    row_sums = jnp.sum(blocks, axis=2) * live[:, None]
    row_weight = None
    image = start.reshape(slices, patches, width)
    measured = sinogram.reshape(slices, row_blocks, width)
    weighted = measured
    for sweep_index in range(ITERS):
        pieces = jnp.einsum("pj,spc->jsc", patch_hot, image, precision=highest)
        partial_value = (
            jnp.einsum("jsc,jrc->jsr", pieces, blocks, precision=highest) * live[:, None, None]
        )
        payload = partial_value
        if sweep_index == 0:
            payload = jnp.concatenate([partial_value, row_sums[:, None, :]], axis=1)
        buffer = (
            jnp.zeros((nodes * capacity,) + payload.shape[1:], jnp.float32).at[slot_id].set(payload)
        )
        received = lax.all_to_all(
            buffer.reshape((nodes, capacity) + payload.shape[1:]),
            "node",
            split_axis=0,
            concat_axis=0,
            tiled=True,
        )
        got_labels = lax.all_to_all(labels, "node", split_axis=0, concat_axis=0, tiled=True)
        flat_labels = got_labels.reshape(-1)
        owner_hot = (
            flat_labels[:, None] == jnp.arange(row_blocks, dtype=jnp.int32)[None, :]
        ).astype(jnp.float32)
        summed = jnp.einsum(
            "kr,ksc->src",
            owner_hot,
            received.reshape(nodes * capacity, -1, width),
            precision=highest,
        )
        if sweep_index == 0:
            row_weight = 1.0 / (summed[slices] + 1.0)
            summed = summed[:slices]
        weighted = row_weight[None] * (measured - summed)
        whole = lax.all_gather(
            weighted.reshape(slices, row_blocks * width), "node", axis=1, tiled=True
        )
        fetched = jnp.moveaxis(
            jnp.take(whole.reshape(slices, total_rows, width), position, axis=1), 1, 0
        )
        back = jnp.einsum("jsr,jrc->jsc", fetched, blocks, precision=highest) * live[:, None, None]
        update = jnp.einsum("pj,jsc->spc", patch_hot, back, precision=highest)
        image = image + relax_factor * col_weight[None] * update
    return (image.reshape(slices, patches * width), weighted.reshape(slices, row_blocks * width))


def solution(mesh):
    placed = (
        P(("grp", "node"), None, None),
        P(("grp", "node")),
        P(("grp", "node")),
        P(("grp", "node")),
        P("grp"),
        P("grp", "node"),
        P("grp", "node"),
    )
    return jax.shard_map(
        body,
        mesh=mesh,
        in_specs=placed,
        out_specs=(P("grp", "node"), P("grp", "node")),
        check_vma=False,
    )
```

profile of v0, /device:TPU:0, one launch (start us, length us, event | category | flops | bytes accessed | tf_op | source)
XLA Modules:
  0.0 132.0 jit_solution(17812372028083572689)
XLA Ops:
  0.7 0.9 select_reduce_fusion.1
  1.6 0.1 reduce_window_sum.11
  1.8 0.2 select_reduce_fusion
  2.0 0.9 scatter_custom_fusion.1
  2.8 0.7 all_to_all.14
  3.5 7.4 %all-to-all-start.1 = ((s32[16,1,6]{2,1,0:T(1,128)}), s32[16,1,6]{2,1,0:T(1,128)S(1)}, u32[]{:S(2)}, u32[]{:S(2)}) async-start(s32[16,1,6]{2,1,0:T(1,128)} %bitcast.7), calls=%async_computation.1 | async-start | bytes 16384 | tf_op jit(solution)/shard_map/all_to_all | solution.py:67
  11.7 4.6 %fusion.54 = (f32[96,128]{1,0:T(8,128)S(1)}, f32[96,128]{1,0:T(8,128)S(1)}) fusion(f32[96,128,128]{2,1,0:T(8,128)} %param.9), kind=kLoop, calls=%fused_computation.91 | loop fusion | flops 3121152 | bytes 6389760 | tf_op jit(solution)/shard_map/reduce_sum | solution.py:41
  16.4 0.3 fusion.24
  16.7 9.9 %convolution_multiply_fusion.3 = f32[96,4,128]{2,1,0:T(4,128)S(1)} fusion(f32[96,128,128]{2,1,0:T(8,128)S(1)} %copy-done, f32[96,4,128]{2,0,1:T(8,128)S(1)} %fusion.24, f32[96]{0:T(128)S(1)} %compare_convert_fusion), kind=kOutput, calls=%fused_computation.8 | convolution fusion | flops 75546624 | bytes 6685056 | tf_op jit(solution)/shard_map/jsc,jrc->jsr/dot_general | solution.py:52
  26.6 0.2 broadcast_multiply_fusion
  26.9 3.4 %scatter_fusion = f32[96,5,128]{2,1,0:T(8,128)S(1)} fusion(f32[96,5,128]{2,1,0:T(8,128)S(1)} %broadcast_in_dim.22, s32[96]{0:T(128)S(1)} %fusion.48, f32[96,5,128]{2,1,0:T(8,128)S(1)} %pad_maximum_fusion), kind=kCustom, calls=%fused_computation.2 | custom fusion | bytes 737664 | tf_op jit(solution)/shard_map/scatter | solution.py:58
  30.3 0.8 copy.26
  31.0 6.0 %all-to-all-start = ((f32[16,6,5,128]{3,1,2,0:T(8,128)}), f32[16,6,5,128]{3,1,2,0:T(8,128)S(1)}, u32[]{:S(2)}, u32[]{:S(2)}) async-start(f32[16,6,5,128]{3,1,2,0:T(8,128)} %copy.26), calls=%async_computation | async-start | bytes 655360 | tf_op jit(solution)/shard_map/all_to_all | solution.py:60
  37.1 0.1 fusion.9
  37.2 0.5 broadcast.205
  37.8 0.7 reduce.3
  38.5 9.6 %all-to-all-done = f32[16,6,5,128]{3,1,2,0:T(8,128)S(1)} async-done(((f32[16,6,5,128]{3,1,2,0:T(8,128)}), f32[16,6,5,128]{3,1,2,0:T(8,128)S(1)}, u32[]{:S(2)}, u32[]{:S(2)}) %all-to-all-start) | async-done | bytes 245792 | tf_op jit(solution)/shard_map/all_to_all | solution.py:60
  48.2 0.2 convolution_bitcast_fusion
  48.5 19.8 %all_gather.6 = f32[4,16384]{1,0:T(4,128)S(1)} all-gather(f32[4,1024]{1,0:T(4,128)S(1)} %bitcast.116), channel_id=1, replica_groups=mesh['grp'=2,'node'=16] {'node'}, dimensions={1}, use_global_device_ids=true | all-gather | bytes 278528 | tf_op jit(solution)/shard_map/all_gather | solution.py:82
  68.3 0.7 gather_fusion
  69.0 7.4 %convolution_multiply_fusion.2 = f32[96,4,128]{2,1,0:T(4,128)S(1)} fusion(f32[96,128,128]{2,1,0:T(8,128)} %param.9, f32[96,4,128]{2,1,0:T(4,128)S(1)} %gather_fusion, f32[96]{0:T(128)S(1)} %compare_convert_fusion, pred[96]{0:T(512)(128)(4,1)S(1)} %compare_and_fusion), kind=kOutput, calls=%fused_computation.7 | convolution fusion | flops 75595776 | bytes 6685152 | tf_op jit(solution)/shard_map/jsr,jrc->jsc/dot_general | solution.py:88
  76.4 0.2 fusion.7
  76.6 0.3 fusion.32
  76.9 11.9 %convolution_multiply_fusion.1 = f32[96,4,128]{2,1,0:T(4,128)S(1)} fusion(f32[96,128,128]{2,1,0:T(8,128)} %param.9, f32[96,4,128]{2,0,1:T(8,128)S(1)} %fusion.32, f32[96]{0:T(128)S(1)} %compare_convert_fusion), kind=kOutput, calls=%fused_computation.6 | convolution fusion | flops 75546624 | bytes 6685056 | tf_op jit(solution)/shard_map/jsc,jrc->jsr/dot_general | solution.py:52
  88.8 3.4 %scatter_fusion.1 = f32[96,4,128]{2,1,0:T(4,128)S(1)} fusion(f32[96,4,128]{2,1,0:T(4,128)S(1)} %broadcast_in_dim.25, s32[96]{0:T(128)S(1)} %fusion.48, f32[96,4,128]{2,1,0:T(4,128)S(1)} %convolution_multiply_fusion.1), kind=kCustom, calls=%fused_computation.4 | custom fusion | bytes 590208 | tf_op jit(solution)/shard_map/scatter | solution.py:58
  92.2 11.6 %all_to_all.20 = f32[16,6,4,128]{3,2,1,0:T(4,128)S(1)} all-to-all(f32[16,6,4,128]{3,2,1,0:T(4,128)S(1)} %bitcast.105), channel_id=1, replica_groups=mesh['grp'=2,'node'=16] {'node'}, dimensions={0} | all-to-all | bytes 393216 | tf_op jit(solution)/shard_map/all_to_all | solution.py:60
  103.8 0.2 fusion.5
  104.0 19.1 %all_gather.7 = f32[4,16384]{1,0:T(4,128)S(1)} all-gather(f32[4,1024]{1,0:T(4,128)S(1)} %bitcast.114), channel_id=1, replica_groups=mesh['grp'=2,'node'=16] {'node'}, dimensions={1}, use_global_device_ids=true | all-gather | bytes 278528 | tf_op jit(solution)/shard_map/all_gather | solution.py:82
  123.1 0.7 gather_fusion.1
  123.8 7.4 %convolution_multiply_fusion = f32[96,4,128]{2,1,0:T(4,128)S(1)} fusion(f32[96,128,128]{2,1,0:T(8,128)} %param.9, f32[96,4,128]{2,1,0:T(4,128)S(1)} %gather_fusion.1, f32[96]{0:T(128)S(1)} %compare_convert_fusion, pred[96]{0:T(512)(128)(4,1)S(1)} %compare_and_fusion), kind=kOutput, calls=%fused_computation.5 | convolution fusion | flops 75595776 | bytes 6685152 | tf_op jit(solution)/shard_map/jsr,jrc->jsc/dot_general | solution.py:88
  131.2 0.2 fusion.2
  131.4 0.6 copy.60
  (27 shorter events, 0.5 us)
Async XLA Ops:
  0.6 15.8 %copy-start.2 = (f32[4,1024]{1,0:T(4,128)S(1)}, f32[4,1024]{1,0:T(4,128)}, u32[]{:S(2)}) copy-start(f32[4,1024]{1,0:T(4,128)} %param.15) | copy-start | bytes 49156
  0.6 15.8 %copy-start.4 = (s32[96]{0:T(128)S(1)}, s32[96]{0:T(128)}, u32[]{:S(2)}) copy-start(s32[96]{0:T(128)} %param.11) | copy-start | bytes 1156
  3.5 27.5 %all-to-all-start.1 = ((s32[16,1,6]{2,1,0:T(1,128)}), s32[16,1,6]{2,1,0:T(1,128)S(1)}, u32[]{:S(2)}, u32[]{:S(2)}) async-start(s32[16,1,6]{2,1,0:T(1,128)} %bitcast.7), calls=%async_computation.1 | async-start | bytes 16384 | tf_op jit(solution)/shard_map/all_to_all | solution.py:67
  10.9 5.8 %copy-start = (f32[96,128,128]{2,1,0:T(8,128)S(1)}, f32[96,128,128]{2,1,0:T(8,128)}, u32[]{:S(2)}) copy-start(f32[96,128,128]{2,1,0:T(8,128)} %param.9) | copy-start | bytes 18874372
  16.4 32.1 %copy-start.1 = (f32[4,1024]{1,0:T(4,128)S(1)}, f32[4,1024]{1,0:T(4,128)}, u32[]{:S(2)}) copy-start(f32[4,1024]{1,0:T(4,128)} %param.14) | copy-start | bytes 49156
  31.0 17.1 %all-to-all-start = ((f32[16,6,5,128]{3,1,2,0:T(8,128)}), f32[16,6,5,128]{3,1,2,0:T(8,128)S(1)}, u32[]{:S(2)}, u32[]{:S(2)}) async-start(f32[16,6,5,128]{3,1,2,0:T(8,128)} %copy.26), calls=%async_computation | async-start | bytes 655360 | tf_op jit(solution)/shard_map/all_to_all | solution.py:60
  104.0 28.0 %copy-start.3 = (f32[1,4,8,128]{3,1,2,0:T(4,128)}, f32[1,4,8,128]{3,1,2,0:T(4,128)S(1)}, u32[]{:S(2)}) copy-start(f32[1,4,8,128]{3,1,2,0:T(4,128)S(1)} %copy.61) | copy-start | bytes 49156
where the time goes:
time: 132 us
  blocking collectives  50.5 us (38%)
  matrix products  38 us (29%)
  starting transfers between devices  13.4 us (10%)
  local copies, waits for them, and re-layouts  11.9 us (9%)
  waiting for transfers between devices  9.63 us (7%)
  other arithmetic  6.86 us (5%)
  between operations  1.71 us (1%)
    all_gather x2, blocking collectives, body(): lax.all_gather(weighted.reshape(slices, row_blocks * width), 'node', axis...  38.9 us
    dot_general x2, matrix products, body(): jnp.einsum('jsc,jrc->jsr', pieces, blocks, precision=highest)  21.7 us
    dot_general x2, matrix products, body(): jnp.einsum('jsr,jrc->jsc', fetched, blocks, precision=highest)  14.8 us
    all_to_all x1, blocking collectives, body(): lax.all_to_all(buffer.reshape((nodes, capacity) + payload.shape[1:]), 'no...  11.6 us
    all_to_all x1, waiting for transfers between devices, body(): lax.all_to_all(buffer.reshape((nodes, capacity) + payload.shape[1:]), 'no...  9.63 us
    all_to_all x1, starting transfers between devices, body(): lax.all_to_all(labels, 'node', split_axis=0, concat_axis=0, tiled=True)  7.39 us
    scatter x2, local copies, waits for them, and re-layouts, body(): jnp.zeros((nodes * capacity,) + payload.shape[1:], jnp.float32).at[slot_id]  6.74 us
    all_to_all x1, starting transfers between devices, body(): lax.all_to_all(buffer.reshape((nodes, capacity) + payload.shape[1:]), 'no...  6.01 us
  transfers between devices with their start and end apart: 2, of which 1 were waited for; matrix products, arithmetic and copies ran while one was open for 16% of the time, Pallas kernels for 0%

commit v1 on v0

v1 whole, which is shorter than its diff:
```python
import functools

import jax
import jax.numpy as jnp
from jax import lax
from jax.experimental import pallas as pl
from jax.experimental.pallas import tpu as pltpu
from jax.sharding import PartitionSpec as P

ITERS = 2
CHUNKS = 8
GROUP = 8

relax_factor = 1.9

f32 = jnp.float32
bf16 = jnp.bfloat16


def split(value):
    high = value.astype(bf16).astype(f32)
    return high, value - high


def forward_terms(lhs_of, pair_of, slots):
    terms = []
    for j in slots:
        both = lax.dot_general(
            lhs_of(j).astype(bf16),
            pair_of(j),
            (((1,), (1,)), ((), ())),
            preferred_element_type=f32,
        )
        width = both.shape[1] // 2
        terms.append(both[:, :width] + both[:, width:])
    return terms


def backward_terms(lhs_of, pair_of, slots):
    terms = []
    for j in slots:
        lhs = lhs_of(j).astype(bf16)
        terms.append(
            jnp.dot(
                jnp.concatenate([lhs, lhs], axis=1),
                pair_of(j),
                preferred_element_type=f32,
            )
        )
    return terms


def at8(index):
    return pl.ds(pl.multiple_of(index * 8, 8), 8)


def first_kernel(
    slices,
    rows_ref,
    patch_ref,
    count_ref,
    map_ref,
    blocks_ref,
    start_ref,
    sino_ref,
    mine_ref,
    other_ref,
    col_ref,
    pair_ref,
    stage,
    lhs,
    acc,
    sums,
    cols,
    sems,
):
    count_blocks, width, _ = blocks_ref.shape
    total_rows = map_ref.shape[0]
    half = total_rows // 2
    patches = start_ref.shape[1] // width
    own = sino_ref.shape[1] // width
    node = lax.axis_index("node")
    core = lax.rem(node, 2)
    step = count_blocks // CHUNKS

    def copy(k):
        part = pl.ds(k * step, step)
        return pltpu.make_async_copy(blocks_ref.at[part], stage.at[part], sems.at[k])

    for k in range(CHUNKS):
        copy(k).start()
    acc[...] = jnp.zeros_like(acc)
    sums[...] = jnp.zeros_like(sums)
    cols[...] = jnp.zeros_like(cols)
    lhs[...] = jnp.zeros_like(lhs)
    for p in range(patches):
        high, low = split(start_ref[:, p * width : (p + 1) * width])
        lhs[p * 16 : p * 16 + slices, :] = high
        lhs[p * 16 + slices : p * 16 + 2 * slices, :] = low
        lhs[p * 16 + 8 : p * 16 + 9, :] = jnp.ones((1, width), f32)
    for r in range(own):
        acc[pl.ds((node * own + r) * 8, slices), :] = -sino_ref[:, r * width : (r + 1) * width]

    count = count_ref[0]

    def visit(base, size):
        slots = [base + i for i in range(size)]
        for j in slots:
            block = stage[j]
            block = jnp.where(j < count, block, 0.0)
            high = block.astype(bf16)
            pair_ref[j, :width, :] = high
            pair_ref[j, width:, :] = (block - high.astype(f32)).astype(bf16)
            part = jnp.sum(block.reshape(width // 8, 8, width), axis=0)
            cols[at8(patch_ref[j]), :] += part
        terms = forward_terms(
            lambda j: lhs[pl.ds(pl.multiple_of(patch_ref[j] * 16, 16), 16), :],
            lambda j: pair_ref[j],
            slots,
        )
        for j, term in zip(slots, terms):
            place = at8(map_ref[rows_ref[j]])
            acc[place, :] += term[:8]
            sums[place, :] += term[8:]

    for k in range(CHUNKS):
        copy(k).wait()
        size = min(GROUP, step)

        @pl.loop(0, step // size)
        def _(i):
            visit(k * step + i * size, size)

        for rest in range(step // size * size, step):
            visit(k * step + rest, 1)

    for ref, side in ((mine_ref, core), (other_ref, 1 - core)):
        base = side * half * 8
        for s in range(slices):
            ref[s] = (
                acc[pl.ds(base + s, half, stride=8), :]
                + acc[pl.ds(base + s + slices, half, stride=8), :]
            )
        ref[slices] = sums[pl.ds(base, half, stride=8), :]
    for p in range(patches):
        total = jnp.sum(cols[p * 8 : (p + 1) * 8, :], axis=0, keepdims=True)
        col_ref[p : p + 1, :] = relax_factor / (total + 1.0)


def weigh(slices, mine_ref, other_ref, weight_of, lhs, full, core, half):
    for ref, side in ((mine_ref, core), (other_ref, 1 - core)):
        weight = weight_of(ref, side)
        for s in range(slices):
            value = -weight * ref[s]
            high, low = split(value)
            lhs[pl.ds(side * half * 8 + s, half, stride=8), :] = high
            lhs[pl.ds(side * half * 8 + slices + s, half, stride=8), :] = low
            if full is not None:
                full[s, pl.ds(pl.multiple_of(side * half, 8), half), :] = value


def back_loop(count_blocks, rows_ref, patch_ref, map_ref, pair_ref, lhs, update):
    update[...] = jnp.zeros_like(update)

    @pl.loop(0, count_blocks // GROUP)
    def _(i):
        slots = [i * GROUP + g for g in range(GROUP)]
        terms = backward_terms(
            lambda j: lhs[at8(map_ref[rows_ref[j]]), :], lambda j: pair_ref[j], slots
        )
        for j, term in zip(slots, terms):
            update[at8(patch_ref[j]), :] += term


def middle_kernel(
    slices,
    rows_ref,
    patch_ref,
    map_ref,
    pair_ref,
    mine_ref,
    other_ref,
    col_ref,
    start_ref,
    sino_ref,
    next_mine_ref,
    next_other_ref,
    weight_ref,
    image_ref,
    lhs,
    update,
    acc,
    image_lhs,
):
    count_blocks, _, width = pair_ref.shape
    total_rows = map_ref.shape[0]
    half = total_rows // 2
    patches = start_ref.shape[1] // width
    own = sino_ref.shape[1] // width
    node = lax.axis_index("node")
    core = lax.rem(node, 2)

    def weight_of(ref, side):
        weight = 1.0 / (ref[slices] + 1.0)
        weight_ref[pl.ds(pl.multiple_of(side * half, 8), half), :] = weight
        return weight

    weigh(slices, mine_ref, other_ref, weight_of, lhs, None, core, half)
    back_loop(count_blocks, rows_ref, patch_ref, map_ref, pair_ref, lhs, update)
    for p in range(patches):
        total = update[p * 8 : p * 8 + slices, :] + update[p * 8 + slices : p * 8 + 2 * slices, :]
        value = start_ref[:, p * width : (p + 1) * width] + col_ref[p : p + 1, :] * total
        image_ref[:, p * width : (p + 1) * width] = value
        high, low = split(value)
        image_lhs[p * 8 : p * 8 + slices, :] = high
        image_lhs[p * 8 + slices : p * 8 + 2 * slices, :] = low
    acc[...] = jnp.zeros_like(acc)
    for r in range(own):
        acc[pl.ds((node * own + r) * 8, slices), :] = -sino_ref[:, r * width : (r + 1) * width]

    @pl.loop(0, count_blocks // GROUP)
    def _(i):
        slots = [i * GROUP + g for g in range(GROUP)]
        terms = forward_terms(
            lambda j: image_lhs[at8(patch_ref[j]), :], lambda j: pair_ref[j], slots
        )
        for j, term in zip(slots, terms):
            acc[at8(map_ref[rows_ref[j]]), :] += term

    for ref, side in ((next_mine_ref, core), (next_other_ref, 1 - core)):
        base = side * half * 8
        for s in range(slices):
            ref[s] = (
                acc[pl.ds(base + s, half, stride=8), :]
                + acc[pl.ds(base + s + slices, half, stride=8), :]
            )


def last_kernel(
    slices,
    rows_ref,
    patch_ref,
    map_ref,
    pair_ref,
    mine_ref,
    other_ref,
    col_ref,
    prior_ref,
    weight_ref,
    image_ref,
    weighted_ref,
    lhs,
    full,
    update,
):
    count_blocks, _, width = pair_ref.shape
    half = map_ref.shape[0] // 2
    patches = prior_ref.shape[1] // width
    own = weighted_ref.shape[1] // width
    node = lax.axis_index("node")
    core = lax.rem(node, 2)

    def weight_of(ref, side):
        return weight_ref[pl.ds(pl.multiple_of(side * half, 8), half), :]

    weigh(slices, mine_ref, other_ref, weight_of, lhs, full, core, half)
    back_loop(count_blocks, rows_ref, patch_ref, map_ref, pair_ref, lhs, update)
    for p in range(patches):
        total = update[p * 8 : p * 8 + slices, :] + update[p * 8 + slices : p * 8 + 2 * slices, :]
        image_ref[:, p * width : (p + 1) * width] = (
            prior_ref[:, p * width : (p + 1) * width] + col_ref[p : p + 1, :] * total
        )
    for s in range(slices):
        for r in range(own):
            weighted_ref[s : s + 1, r * width : (r + 1) * width] = full[
                s, pl.ds(node * own + r, 1), :
            ]


def exchange(value, distance, nodes):
    return lax.ppermute(value, "node", [(i, i ^ distance) for i in range(nodes)])


def body(blocks, block_row, block_patch, block_count, row_map, sinogram, start):
    nodes = lax.axis_size("node")
    count_blocks, width, _ = blocks.shape
    slices = start.shape[0]
    patches = start.shape[1] // width
    total_rows = row_map.shape[0]
    half = total_rows // 2
    smem = pl.BlockSpec(memory_space=pltpu.SMEM)
    vmem = pl.BlockSpec(memory_space=pltpu.VMEM)
    params = pltpu.CompilerParams(vmem_limit_bytes=32 * 1024 * 1024)

    def sum_over_nodes(mine, other):
        value = mine + exchange(other, 1, nodes)
        distance = 2
        while distance < nodes:
            value = value + exchange(value, distance, nodes)
            distance *= 2
        return value, exchange(value, 1, nodes)

    mine, other, col, pair = pl.pallas_call(
        functools.partial(first_kernel, slices),
        out_shape=(
            jax.ShapeDtypeStruct((slices + 1, half, width), f32),
            jax.ShapeDtypeStruct((slices + 1, half, width), f32),
            jax.ShapeDtypeStruct((patches, width), f32),
            pltpu.VMEM((count_blocks, 2 * width, width), bf16),
        ),
        in_specs=[smem] * 4 + [pl.BlockSpec(memory_space=pl.ANY), vmem, vmem],
        out_specs=(vmem,) * 4,
        scratch_shapes=[
            pltpu.VMEM(blocks.shape, f32),
            pltpu.VMEM((patches * 16, width), f32),
            pltpu.VMEM((total_rows * 8, width), f32),
            pltpu.VMEM((total_rows * 8, width), f32),
            pltpu.VMEM((patches * 8, width), f32),
            pltpu.SemaphoreType.DMA((CHUNKS,)),
        ],
        compiler_params=params,
        name="first",
    )(block_row, block_patch, block_count, row_map, blocks, start, sinogram)
    mine, other = sum_over_nodes(mine, other)
    held = pltpu.with_memory_space_constraint(pair, pltpu.VMEM)
    mine, other, weight, image = pl.pallas_call(
        functools.partial(middle_kernel, slices),
        out_shape=(
            jax.ShapeDtypeStruct((slices, half, width), f32),
            jax.ShapeDtypeStruct((slices, half, width), f32),
            jax.ShapeDtypeStruct((total_rows, width), f32),
            jax.ShapeDtypeStruct(start.shape, f32),
        ),
        in_specs=[smem] * 3 + [vmem] * 6,
        out_specs=(vmem,) * 4,
        scratch_shapes=[
            pltpu.VMEM((total_rows * 8, width), f32),
            pltpu.VMEM((patches * 8, width), f32),
            pltpu.VMEM((total_rows * 8, width), f32),
            pltpu.VMEM((patches * 8, width), f32),
        ],
        compiler_params=params,
        name="middle",
    )(block_row, block_patch, row_map, held, mine, other, col, start, sinogram)
    mine, other = sum_over_nodes(mine, other)
    held = pltpu.with_memory_space_constraint(pair, pltpu.VMEM)
    image, weighted = pl.pallas_call(
        functools.partial(last_kernel, slices),
        out_shape=(
            jax.ShapeDtypeStruct(start.shape, f32),
            jax.ShapeDtypeStruct(sinogram.shape, f32),
        ),
        in_specs=[smem] * 3 + [vmem] * 6,
        out_specs=(vmem,) * 2,
        scratch_shapes=[
            pltpu.VMEM((total_rows * 8, width), f32),
            pltpu.VMEM((slices, total_rows, width), f32),
            pltpu.VMEM((patches * 8, width), f32),
        ],
        compiler_params=params,
        name="last",
    )(block_row, block_patch, row_map, held, mine, other, col, image, weight)
    return image, weighted


def solution(mesh):
    placed = (
        P(("grp", "node"), None, None),
        P(("grp", "node")),
        P(("grp", "node")),
        P(("grp", "node")),
        P("grp"),
        P("grp", "node"),
        P("grp", "node"),
    )
    return jax.shard_map(
        body,
        mesh=mesh,
        in_specs=placed,
        out_specs=(P("grp", "node"), P("grp", "node")),
        check_vma=False,
    )
```

time: 132 us -> 68.6 us (0.52)
  blocking collectives: 50.5 us -> 0 us
  matrix products: 38 us -> 0 us
  waiting for transfers between devices: 9.63 us -> 35 us
  Pallas kernels: 0 us -> 14.2 us
  other arithmetic: 6.86 us -> 0.16 us
  local copies, waits for them, and re-layouts: 11.9 us -> 6.18 us
  starting transfers between devices: 13.4 us -> 11.4 us
    all_gather x2 -> x0, blocking collectives: 38.9 us -> none  [body(): lax.all_gather(weighted.reshape(slices, row_blocks * width), 'node', axis...]
    dot_general x11 -> x0, matrix products: 38 us -> none  [the longest x2 21.7 us: body(): jnp.einsum('jsc,jrc->jsr', pieces, blocks, precision=highest)]
    ppermute x0 -> x10, waiting for transfers between devices: none -> 35 us  [exchange(): lax.ppermute(value, 'node', [(i, i ^ distance) for i in range(nodes)])]
    pallas_call x0 -> x3, Pallas kernels: none -> 14.2 us  [the longest x1 6.08 us: body(): pl.pallas_call(functools.partial(middle_kernel, slices), out_shape=(jax.S...]
    all_to_all x2 -> x0, starting transfers between devices: 13.4 us -> none  [the longest x1 7.39 us: body(): lax.all_to_all(labels, 'node', split_axis=0, concat_axis=0, tiled=True)]
    all_to_all x1 -> x0, blocking collectives: 11.6 us -> none  [body(): lax.all_to_all(buffer.reshape((nodes, capacity) + payload.shape[1:]), 'no...]
    ppermute x0 -> x10, starting transfers between devices: none -> 11.4 us  [exchange(): lax.ppermute(value, 'node', [(i, i ^ distance) for i in range(nodes)])]
    all_to_all x2 -> x0, waiting for transfers between devices: 9.63 us -> none  [the longest x1 9.63 us: body(): lax.all_to_all(buffer.reshape((nodes, capacity) + payload.shape[1:]), 'no...]
  transfers between devices with their start and end apart: 2 -> 10, of which waited for: 1 -> 10; matrix products, arithmetic and copies ran while one was open for 16% -> 0% of each run, Pallas kernels for 0% -> 0%
where the time goes in v1:
time: 68.6 us; the launch traced here: 68.2 us
  waiting for transfers between devices  35 us (51%)
  Pallas kernels  14.2 us (21%)
  starting transfers between devices  11.4 us (17%)
  local copies, waits for them, and re-layouts  6.18 us (9%)
  between operations  1.35 us (2%)
    ppermute x10, waiting for transfers between devices, exchange(): lax.ppermute(value, 'node', [(i, i ^ distance) for i in range(nodes)])  35 us
    ppermute x10, starting transfers between devices, exchange(): lax.ppermute(value, 'node', [(i, i ^ distance) for i in range(nodes)])  11.4 us
    unnamed x12, local copies, waits for them, and re-layouts  6.18 us
    pallas_call x1, Pallas kernels, body(): pl.pallas_call(functools.partial(middle_kernel, slices), out_shape=(jax.S...  6.08 us
    pallas_call x1, Pallas kernels, body(): pl.pallas_call(functools.partial(first_kernel, slices), out_shape=(jax.Sh...  4.55 us
    pallas_call x1, Pallas kernels, body(): pl.pallas_call(functools.partial(last_kernel, slices), out_shape=(jax.Sha...  3.55 us
  transfers between devices with their start and end apart: 10, of which 10 were waited for; matrix products, arithmetic and copies ran while one was open for 0% of the time, Pallas kernels for 0%

profile of v1, /device:TPU:0, one launch (start us, length us, event | category | flops | bytes accessed | tf_op | source)
XLA Modules:
  0.0 68.2 jit_solution(17765934342200711063)
XLA Ops:
  1.3 0.0 copy-start
  1.3 2.8 %copy-done = f32[96,128,128]{2,1,0:T(8,128)S(1)} copy-done((f32[96,128,128]{2,1,0:T(8,128)S(1)}, f32[96,128,128]{2,1,0:T(8,128)}, u32[]{:S(2)}) %copy-start) | copy-done | bytes 6291480
  4.1 0.0 copy-start.1
  4.1 0.7 %copy-done.1 = f32[4,1024]{1,0:T(4,128)S(1)} copy-done((f32[4,1024]{1,0:T(4,128)S(1)}, f32[4,1024]{1,0:T(4,128)}, u32[]{:S(2)}) %copy-start.1) | copy-done | bytes 16408
  4.8 0.0 copy-start.2
  4.8 0.7 %copy-done.2 = f32[4,1024]{1,0:T(4,128)S(1)} copy-done((f32[4,1024]{1,0:T(4,128)S(1)}, f32[4,1024]{1,0:T(4,128)}, u32[]{:S(2)}) %copy-start.2) | copy-done | bytes 16408
  5.5 0.7 copy-done.3
  6.2 0.7 copy-done.4
  6.8 0.7 copy-done.5
  7.5 4.5 %first.1 = (f32[5,64,128]{2,1,0:T(8,128)S(1)}, f32[5,64,128]{2,1,0:T(8,128)S(1)}, f32[8,128]{1,0:T(8,128)S(1)}, bf16[96,256,128]{2,1,0:T(8,128)(2,1)S(1)}) custom-call(s32[96]{0:T(128)S(1)} %copy-done.3, s32[96]{0:T(128)S(1)} %copy-done.4, s32[1]{0:T(128)S(6)} %copy.9.count_ref, s32[128]{0:T(128)S(1)} %copy-done.5, f32[96,128,128]{2,1,0:T(8,128)S(1)} %copy-done, ...), custom_call_target="tpu_custom_call" | custom-call | tf_op jit(solution)/shard_map/first/pallas_call | solution.py:303
  12.0 0.5 collective-permute-start
  12.5 1.0 %collective-permute-done = f32[5,64,128]{2,1,0:T(8,128)S(1)} collective-permute-done((f32[5,64,128]{2,1,0:T(8,128)S(1)}, f32[5,64,128]{2,1,0:T(8,128)S(1)}, u32[]{:S(2)}, u32[]{:S(2)}) %collective-permute-start) | collective-permute-done | bytes 163872 | tf_op jit(solution)/shard_map/ppermute | solution.py:281
  13.6 2.9 %collective-permute-start.1 = (f32[5,64,128]{2,1,0:T(8,128)S(1)}, f32[5,64,128]{2,1,0:T(8,128)S(1)}, u32[]{:S(2)}, u32[]{:S(2)}) collective-permute-start(f32[5,64,128]{2,1,0:T(8,128)S(1)} %add.24), channel_id=1, source_target_pairs={{0,2},{1,3},{2,0},{3,1},{4,6},{5,7},{6,4},{7,5},{8,10},{9,11},{10,... | collective-permute-start | bytes 491528 | tf_op jit(solution)/shard_map/ppermute | solution.py:281
  16.5 4.5 %collective-permute-done.1 = f32[5,64,128]{2,1,0:T(8,128)S(1)} collective-permute-done((f32[5,64,128]{2,1,0:T(8,128)S(1)}, f32[5,64,128]{2,1,0:T(8,128)S(1)}, u32[]{:S(2)}, u32[]{:S(2)}) %collective-permute-start.1) | collective-permute-done | bytes 163872 | tf_op jit(solution)/shard_map/ppermute | solution.py:281
  21.1 1.9 %collective-permute-start.2 = (f32[5,64,128]{2,1,0:T(8,128)S(1)}, f32[5,64,128]{2,1,0:T(8,128)S(1)}, u32[]{:S(2)}, u32[]{:S(2)}) collective-permute-start(f32[5,64,128]{2,1,0:T(8,128)S(1)} %add.25), channel_id=1, source_target_pairs={{0,4},{1,5},{2,6},{3,7},{4,0},{5,1},{6,2},{7,3},{8,12},{9,13},{10,... | collective-permute-start | bytes 491528 | tf_op jit(solution)/shard_map/ppermute | solution.py:281
  22.9 3.9 %collective-permute-done.2 = f32[5,64,128]{2,1,0:T(8,128)S(1)} collective-permute-done((f32[5,64,128]{2,1,0:T(8,128)S(1)}, f32[5,64,128]{2,1,0:T(8,128)S(1)}, u32[]{:S(2)}, u32[]{:S(2)}) %collective-permute-start.2) | collective-permute-done | bytes 163872 | tf_op jit(solution)/shard_map/ppermute | solution.py:281
  26.9 2.6 %collective-permute-start.3 = (f32[5,64,128]{2,1,0:T(8,128)S(1)}, f32[5,64,128]{2,1,0:T(8,128)S(1)}, u32[]{:S(2)}, u32[]{:S(2)}) collective-permute-start(f32[5,64,128]{2,1,0:T(8,128)S(1)} %add.26), channel_id=1, source_target_pairs={{0,8},{1,9},{2,10},{3,11},{4,12},{5,13},{6,14},{7,15},{8,0},{9,1},... | collective-permute-start | bytes 491528 | tf_op jit(solution)/shard_map/ppermute | solution.py:281
  29.4 6.7 %collective-permute-done.3 = f32[5,64,128]{2,1,0:T(8,128)S(1)} collective-permute-done((f32[5,64,128]{2,1,0:T(8,128)S(1)}, f32[5,64,128]{2,1,0:T(8,128)S(1)}, u32[]{:S(2)}, u32[]{:S(2)}) %collective-permute-start.3) | collective-permute-done | bytes 163872 | tf_op jit(solution)/shard_map/ppermute | solution.py:281
  36.2 0.1 collective-permute-start.4
  36.3 1.4 %collective-permute-done.4.other_ref = f32[5,64,128]{2,1,0:T(8,128)S(1)} collective-permute-done((f32[5,64,128]{2,1,0:T(8,128)S(1)}, f32[5,64,128]{2,1,0:T(8,128)S(1)}, u32[]{:S(2)}, u32[]{:S(2)}) %collective-permute-start.4) | collective-permute-done | bytes 163872 | tf_op jit(solution)/shard_map/ppermute | solution.py:281
  37.7 6.1 %middle.1 = (f32[4,64,128]{2,1,0:T(8,128)S(1)}, f32[4,64,128]{2,1,0:T(8,128)S(1)}, f32[128,128]{1,0:T(8,128)S(1)}, f32[4,1024]{1,0:T(4,128)S(1)}) custom-call(s32[96]{0:T(128)S(1)} %copy-done.3, s32[96]{0:T(128)S(1)} %copy-done.4, s32[128]{0:T(128)S(1)} %copy-done.5, bf16[96,256,128]{2,1,0:T(8,128)(2,1)S(1)} %get-tuple-element.10.pair_ref, ...), custom_call_target="tpu_custom_call" | custom-call | tf_op jit(solution)/shard_map/middle/pallas_call | solution.py:326
  43.8 0.2 collective-permute-start.5
  44.0 1.2 %collective-permute-done.5 = f32[4,64,128]{2,1,0:T(8,128)S(1)} collective-permute-done((f32[4,64,128]{2,1,0:T(8,128)S(1)}, f32[4,64,128]{2,1,0:T(8,128)S(1)}, u32[]{:S(2)}, u32[]{:S(2)}) %collective-permute-start.5) | collective-permute-done | bytes 131104 | tf_op jit(solution)/shard_map/ppermute | solution.py:281
  45.2 1.2 %collective-permute-start.6 = (f32[4,64,128]{2,1,0:T(8,128)S(1)}, f32[4,64,128]{2,1,0:T(8,128)S(1)}, u32[]{:S(2)}, u32[]{:S(2)}) collective-permute-start(f32[4,64,128]{2,1,0:T(8,128)S(1)} %add.28), channel_id=1, source_target_pairs={{0,2},{1,3},{2,0},{3,1},{4,6},{5,7},{6,4},{7,5},{8,10},{9,11},{10,... | collective-permute-start | bytes 393224 | tf_op jit(solution)/shard_map/ppermute | solution.py:281
  46.4 4.5 %collective-permute-done.6 = f32[4,64,128]{2,1,0:T(8,128)S(1)} collective-permute-done((f32[4,64,128]{2,1,0:T(8,128)S(1)}, f32[4,64,128]{2,1,0:T(8,128)S(1)}, u32[]{:S(2)}, u32[]{:S(2)}) %collective-permute-start.6) | collective-permute-done | bytes 131104 | tf_op jit(solution)/shard_map/ppermute | solution.py:281
  50.8 0.3 collective-permute-start.7
  51.1 4.7 %collective-permute-done.7 = f32[4,64,128]{2,1,0:T(8,128)S(1)} collective-permute-done((f32[4,64,128]{2,1,0:T(8,128)S(1)}, f32[4,64,128]{2,1,0:T(8,128)S(1)}, u32[]{:S(2)}, u32[]{:S(2)}) %collective-permute-start.7) | collective-permute-done | bytes 131104 | tf_op jit(solution)/shard_map/ppermute | solution.py:281
  55.9 1.7 %collective-permute-start.8 = (f32[4,64,128]{2,1,0:T(8,128)S(1)}, f32[4,64,128]{2,1,0:T(8,128)S(1)}, u32[]{:S(2)}, u32[]{:S(2)}) collective-permute-start(f32[4,64,128]{2,1,0:T(8,128)S(1)} %add.30), channel_id=1, source_target_pairs={{0,8},{1,9},{2,10},{3,11},{4,12},{5,13},{6,14},{7,15},{8,0},{9,1},... | collective-permute-start | bytes 393224 | tf_op jit(solution)/shard_map/ppermute | solution.py:281
  57.6 5.6 %collective-permute-done.8 = f32[4,64,128]{2,1,0:T(8,128)S(1)} collective-permute-done((f32[4,64,128]{2,1,0:T(8,128)S(1)}, f32[4,64,128]{2,1,0:T(8,128)S(1)}, u32[]{:S(2)}, u32[]{:S(2)}) %collective-permute-start.8) | collective-permute-done | bytes 131104 | tf_op jit(solution)/shard_map/ppermute | solution.py:281
  63.3 0.1 collective-permute-start.9
  63.3 1.3 %collective-permute-done.9.other_ref = f32[4,64,128]{2,1,0:T(8,128)S(1)} collective-permute-done((f32[4,64,128]{2,1,0:T(8,128)S(1)}, f32[4,64,128]{2,1,0:T(8,128)S(1)}, u32[]{:S(2)}, u32[]{:S(2)}) %collective-permute-start.9) | collective-permute-done | bytes 131104 | tf_op jit(solution)/shard_map/ppermute | solution.py:281
  64.7 3.6 %last.1 = (f32[4,1024]{1,0:T(4,128)}, f32[4,1024]{1,0:T(4,128)}) custom-call(s32[96]{0:T(128)S(1)} %copy-done.3, s32[96]{0:T(128)S(1)} %copy-done.4, s32[128]{0:T(128)S(1)} %copy-done.5, bf16[96,256,128]{2,1,0:T(8,128)(2,1)S(1)} %get-tuple-element.10.pair_ref, f32[4,64,128]{2,1,0:T(8,128)S(1)} %add.31.mine_ref, ...), custom_call_target="tpu_custom_call" | custom-call | tf_op jit(solution)/shard_map/last/pallas_call | solution.py:347
  (11 shorter events, 0.2 us)
Async XLA Ops:
  1.3 2.8 %copy-start = (f32[96,128,128]{2,1,0:T(8,128)S(1)}, f32[96,128,128]{2,1,0:T(8,128)}, u32[]{:S(2)}) copy-start(f32[96,128,128]{2,1,0:T(8,128)} %blocks_ref.1) | copy-start | bytes 18874372
  4.1 0.7 %copy-start.1 = (f32[4,1024]{1,0:T(4,128)S(1)}, f32[4,1024]{1,0:T(4,128)}, u32[]{:S(2)}) copy-start(f32[4,1024]{1,0:T(4,128)} %start_ref.3) | copy-start | bytes 49156
  4.8 0.7 %copy-start.2 = (f32[4,1024]{1,0:T(4,128)S(1)}, f32[4,1024]{1,0:T(4,128)}, u32[]{:S(2)}) copy-start(f32[4,1024]{1,0:T(4,128)} %sino_ref.3) | copy-start | bytes 49156
  5.5 0.7 copy-start.3
  6.2 0.7 copy-start.4
  6.8 0.7 copy-start.5
  12.0 1.5 %collective-permute-start = (f32[5,64,128]{2,1,0:T(8,128)S(1)}, f32[5,64,128]{2,1,0:T(8,128)S(1)}, u32[]{:S(2)}, u32[]{:S(2)}) collective-permute-start(f32[5,64,128]{2,1,0:T(8,128)S(1)} %get-tuple-element.12), channel_id=1, source_target_pairs={{0,1},{1,0},{2,3},{3,2},{4,5},{5,4},{6,7},{7,6},{8,9},{9,8},{10,11... | collective-permute-start | bytes 491528 | tf_op jit(solution)/shard_map/ppermute | solution.py:281
  13.6 7.5 %collective-permute-start.1 = (f32[5,64,128]{2,1,0:T(8,128)S(1)}, f32[5,64,128]{2,1,0:T(8,128)S(1)}, u32[]{:S(2)}, u32[]{:S(2)}) collective-permute-start(f32[5,64,128]{2,1,0:T(8,128)S(1)} %add.24), channel_id=1, source_target_pairs={{0,2},{1,3},{2,0},{3,1},{4,6},{5,7},{6,4},{7,5},{8,10},{9,11},{10,... | collective-permute-start | bytes 491528 | tf_op jit(solution)/shard_map/ppermute | solution.py:281
  21.1 5.8 %collective-permute-start.2 = (f32[5,64,128]{2,1,0:T(8,128)S(1)}, f32[5,64,128]{2,1,0:T(8,128)S(1)}, u32[]{:S(2)}, u32[]{:S(2)}) collective-permute-start(f32[5,64,128]{2,1,0:T(8,128)S(1)} %add.25), channel_id=1, source_target_pairs={{0,4},{1,5},{2,6},{3,7},{4,0},{5,1},{6,2},{7,3},{8,12},{9,13},{10,... | collective-permute-start | bytes 491528 | tf_op jit(solution)/shard_map/ppermute | solution.py:281
  26.9 9.3 %collective-permute-start.3 = (f32[5,64,128]{2,1,0:T(8,128)S(1)}, f32[5,64,128]{2,1,0:T(8,128)S(1)}, u32[]{:S(2)}, u32[]{:S(2)}) collective-permute-start(f32[5,64,128]{2,1,0:T(8,128)S(1)} %add.26), channel_id=1, source_target_pairs={{0,8},{1,9},{2,10},{3,11},{4,12},{5,13},{6,14},{7,15},{8,0},{9,1},... | collective-permute-start | bytes 491528 | tf_op jit(solution)/shard_map/ppermute | solution.py:281
  36.2 1.5 %collective-permute-start.4 = (f32[5,64,128]{2,1,0:T(8,128)S(1)}, f32[5,64,128]{2,1,0:T(8,128)S(1)}, u32[]{:S(2)}, u32[]{:S(2)}) collective-permute-start(f32[5,64,128]{2,1,0:T(8,128)S(1)} %add.27.mine_ref), channel_id=1, source_target_pairs={{0,1},{1,0},{2,3},{3,2},{4,5},{5,4},{6,7},{7,6},{8,9},{9,8},{10,11... | collective-permute-start | bytes 491528 | tf_op jit(solution)/shard_map/ppermute | solution.py:281
  43.8 1.4 %collective-permute-start.5 = (f32[4,64,128]{2,1,0:T(8,128)S(1)}, f32[4,64,128]{2,1,0:T(8,128)S(1)}, u32[]{:S(2)}, u32[]{:S(2)}) collective-permute-start(f32[4,64,128]{2,1,0:T(8,128)S(1)} %get-tuple-element.15), channel_id=1, source_target_pairs={{0,1},{1,0},{2,3},{3,2},{4,5},{5,4},{6,7},{7,6},{8,9},{9,8},{10,11... | collective-permute-start | bytes 393224 | tf_op jit(solution)/shard_map/ppermute | solution.py:281
  45.2 5.6 %collective-permute-start.6 = (f32[4,64,128]{2,1,0:T(8,128)S(1)}, f32[4,64,128]{2,1,0:T(8,128)S(1)}, u32[]{:S(2)}, u32[]{:S(2)}) collective-permute-start(f32[4,64,128]{2,1,0:T(8,128)S(1)} %add.28), channel_id=1, source_target_pairs={{0,2},{1,3},{2,0},{3,1},{4,6},{5,7},{6,4},{7,5},{8,10},{9,11},{10,... | collective-permute-start | bytes 393224 | tf_op jit(solution)/shard_map/ppermute | solution.py:281
  50.8 5.0 %collective-permute-start.7 = (f32[4,64,128]{2,1,0:T(8,128)S(1)}, f32[4,64,128]{2,1,0:T(8,128)S(1)}, u32[]{:S(2)}, u32[]{:S(2)}) collective-permute-start(f32[4,64,128]{2,1,0:T(8,128)S(1)} %add.29), channel_id=1, source_target_pairs={{0,4},{1,5},{2,6},{3,7},{4,0},{5,1},{6,2},{7,3},{8,12},{9,13},{10,... | collective-permute-start | bytes 393224 | tf_op jit(solution)/shard_map/ppermute | solution.py:281
  55.9 7.3 %collective-permute-start.8 = (f32[4,64,128]{2,1,0:T(8,128)S(1)}, f32[4,64,128]{2,1,0:T(8,128)S(1)}, u32[]{:S(2)}, u32[]{:S(2)}) collective-permute-start(f32[4,64,128]{2,1,0:T(8,128)S(1)} %add.30), channel_id=1, source_target_pairs={{0,8},{1,9},{2,10},{3,11},{4,12},{5,13},{6,14},{7,15},{8,0},{9,1},... | collective-permute-start | bytes 393224 | tf_op jit(solution)/shard_map/ppermute | solution.py:281
  63.3 1.4 %collective-permute-start.9 = (f32[4,64,128]{2,1,0:T(8,128)S(1)}, f32[4,64,128]{2,1,0:T(8,128)S(1)}, u32[]{:S(2)}, u32[]{:S(2)}) collective-permute-start(f32[4,64,128]{2,1,0:T(8,128)S(1)} %add.31.mine_ref), channel_id=1, source_target_pairs={{0,1},{1,0},{2,3},{3,2},{4,5},{5,4},{6,7},{7,6},{8,9},{9,8},{10,11... | collective-permute-start | bytes 393224 | tf_op jit(solution)/shard_map/ppermute | solution.py:281

commit v2 on v1

v2 whole, which is shorter than its diff:
```python
import functools

import jax
import jax.numpy as jnp
from jax import lax
from jax.experimental import pallas as pl
from jax.experimental.pallas import tpu as pltpu
from jax.sharding import PartitionSpec as P

CHUNKS = 8
CHAINS = 1

relax_factor = 1.9

f32 = jnp.float32
bf16 = jnp.bfloat16


def split(value):
    high = value.astype(bf16).astype(f32)
    return high, value - high


def forward_term(lhs, pair):
    both = lax.dot_general(
        lhs.astype(bf16), pair, (((1,), (1,)), ((), ())), preferred_element_type=f32
    )
    width = both.shape[1] // 2
    return both[:, :width] + both[:, width:]


def backward_term(lhs, pair):
    lhs = lhs.astype(bf16)
    return jnp.dot(
        jnp.concatenate([lhs, lhs], axis=1), pair, preferred_element_type=f32
    )


def at8(index):
    return pl.ds(pl.multiple_of(index * 8, 8), 8)


def minus_measured(acc, sino_ref, width, node):
    own = sino_ref.shape[1] // width
    slices = sino_ref.shape[0]
    for r in range(own):
        acc[pl.ds((node * own + r) * 8, slices), :] = -sino_ref[:, r * width : (r + 1) * width]


def write_halves(acc, slices, core, half, mine_ref, other_ref):
    for ref, side in ((mine_ref, core), (other_ref, 1 - core)):
        base = side * half * 8
        for s in range(slices):
            ref[s] = (
                acc[pl.ds(base + s, half, stride=8), :]
                + acc[pl.ds(base + s + slices, half, stride=8), :]
            )


def fill_lhs(lhs, p, stride, value, slices):
    high, low = split(value)
    lhs[p * stride : p * stride + slices, :] = high
    lhs[p * stride + slices : p * stride + 2 * slices, :] = low


def first_kernel(
    lo,
    slices,
    rows_hbm,
    patch_hbm,
    count_ref,
    map_hbm,
    blocks_ref,
    start_hbm,
    sino_hbm,
    mine_ref,
    other_ref,
    col_ref,
    pair_ref,
    index_ref,
    rows_ref,
    patch_ref,
    map_ref,
    start_ref,
    sino_ref,
    stage,
    lhs,
    acc,
    sums,
    cols,
    sems,
    small_sems,
):
    count_blocks, width, _ = blocks_ref.shape
    total_rows = map_ref.shape[0]
    half = total_rows // 2
    patches = start_ref.shape[1] // width
    node = lax.axis_index("node")
    core = lax.rem(node, 2)
    step = count_blocks // CHUNKS

    def copy(k):
        part = pl.ds(k * step, step)
        return pltpu.make_async_copy(blocks_ref.at[part], stage.at[part], sems.at[k])

    small = [
        pltpu.make_async_copy(src, dst, small_sems.at[i])
        for i, (src, dst) in enumerate(
            (
                (start_hbm, start_ref),
                (sino_hbm, sino_ref),
                (rows_hbm, rows_ref),
                (patch_hbm, patch_ref),
                (map_hbm, map_ref),
            )
        )
    ]
    copy(0).start()
    for one in small:
        one.start()
    for k in range(1, CHUNKS):
        copy(k).start()
    acc[...] = jnp.zeros_like(acc)
    sums[...] = jnp.zeros_like(sums)
    cols[...] = jnp.zeros_like(cols)
    lhs[...] = jnp.zeros_like(lhs)
    for one in small:
        one.wait()
    for p in range(patches):
        fill_lhs(lhs, p, 16, start_ref[lo : lo + slices, p * width : (p + 1) * width], slices)
        lhs[p * 16 + 8 : p * 16 + 9, :] = jnp.ones((1, width), f32)
    minus_measured(acc, sino_ref.at[lo : lo + slices], width, node)
    count = count_ref[0]

    for k in range(CHUNKS):
        copy(k).wait()
        slots = range(k * step, (k + 1) * step)
        places = []
        terms = []
        for j in slots:
            position = map_ref[rows_ref[j]]
            patch = patch_ref[j]
            index_ref[0, j] = position
            index_ref[1, j] = patch
            places.append(at8(position))
            block = jnp.where(j < count, stage[j], 0.0)
            high = block.astype(bf16)
            pair = jnp.concatenate([high, (block - high.astype(f32)).astype(bf16)], axis=0)
            pair_ref[j] = pair
            cols[at8(patch), :] += jnp.sum(block.reshape(width // 8, 8, width), axis=0)
            terms.append(
                forward_term(lhs[pl.ds(pl.multiple_of(patch * 16, 16), 16), :], pair)
            )
        for place, term in zip(places, terms):
            acc[place, :] += term[:8]
            sums[place, :] += term[8:]

    write_halves(acc, slices, core, half, mine_ref, other_ref)
    for ref, side in ((mine_ref, core), (other_ref, 1 - core)):
        ref[slices] = sums[pl.ds(side * half * 8, half, stride=8), :]
    for p in range(patches):
        total = jnp.sum(cols[p * 8 : (p + 1) * 8, :], axis=0, keepdims=True)
        col_ref[p : p + 1, :] = relax_factor / (total + 1.0)


def weigh(slices, mine_ref, other_ref, weight_of, lhs, full, core, half):
    for ref, side in ((mine_ref, core), (other_ref, 1 - core)):
        weight = weight_of(ref, side)
        for s in range(slices):
            value = -weight * ref[s]
            high, low = split(value)
            lhs[pl.ds(side * half * 8 + s, half, stride=8), :] = high
            lhs[pl.ds(side * half * 8 + slices + s, half, stride=8), :] = low
            if full is not None:
                full[s, pl.ds(pl.multiple_of(side * half, 8), half), :] = value


def backward(index_ref, pair_ref, lhs, update):
    update[...] = jnp.zeros_like(update)
    terms = []
    for j in range(pair_ref.shape[0]):
        terms.append(backward_term(lhs[at8(index_ref[0, j]), :], pair_ref[j]))
    for j, term in enumerate(terms):
        update[at8(index_ref[1, j]), :] += term


def forward(index_ref, pair_ref, lhs, acc):
    terms = []
    for j in range(pair_ref.shape[0]):
        terms.append(forward_term(lhs[at8(index_ref[1, j]), :], pair_ref[j]))
    for j, term in enumerate(terms):
        acc[at8(index_ref[0, j]), :] += term


def second_kernel(
    lo, slices, index_ref, pair_ref, start_ref, sino_ref, mine_ref, other_ref, acc, image_lhs
):
    width = pair_ref.shape[2]
    half = mine_ref.shape[1]
    patches = start_ref.shape[1] // width
    node = lax.axis_index("node")
    image_lhs[...] = jnp.zeros_like(image_lhs)
    for p in range(patches):
        fill_lhs(image_lhs, p, 8, start_ref[lo : lo + slices, p * width : (p + 1) * width], slices)
    acc[...] = jnp.zeros_like(acc)
    minus_measured(acc, sino_ref.at[lo : lo + slices], width, node)
    forward(index_ref, pair_ref, image_lhs, acc)
    write_halves(acc, slices, lax.rem(node, 2), half, mine_ref, other_ref)


def middle_kernel(
    lo,
    slices,
    index_ref,
    pair_ref,
    mine_ref,
    other_ref,
    col_ref,
    start_ref,
    sino_ref,
    *rest,
):
    given, rest = (rest[:1], rest[1:]) if lo else ((), rest)
    next_mine_ref, next_other_ref, image_ref = rest[:3]
    made, rest = (rest[3:4], rest[4:]) if not lo else ((), rest[3:])
    lhs, update, acc, image_lhs = rest
    width = pair_ref.shape[2]
    half = mine_ref.shape[1]
    patches = start_ref.shape[1] // width
    node = lax.axis_index("node")
    core = lax.rem(node, 2)

    def weight_of(ref, side):
        part = pl.ds(pl.multiple_of(side * half, 8), half)
        if given:
            return given[0][part, :]
        weight = 1.0 / (ref[slices] + 1.0)
        made[0][part, :] = weight
        return weight

    if slices < 4:
        lhs[...] = jnp.zeros_like(lhs)
        image_lhs[...] = jnp.zeros_like(image_lhs)
    weigh(slices, mine_ref, other_ref, weight_of, lhs, None, core, half)
    backward(index_ref, pair_ref, lhs, update)
    for p in range(patches):
        total = update[p * 8 : p * 8 + slices, :] + update[p * 8 + slices : p * 8 + 2 * slices, :]
        value = (
            start_ref[lo : lo + slices, p * width : (p + 1) * width]
            + col_ref[p : p + 1, :] * total
        )
        image_ref[:, p * width : (p + 1) * width] = value
        fill_lhs(image_lhs, p, 8, value, slices)
    acc[...] = jnp.zeros_like(acc)
    minus_measured(acc, sino_ref.at[lo : lo + slices], width, node)
    forward(index_ref, pair_ref, image_lhs, acc)
    write_halves(acc, slices, core, half, next_mine_ref, next_other_ref)


def last_kernel(
    lo,
    slices,
    index_ref,
    pair_ref,
    mine_ref,
    other_ref,
    col_ref,
    prior_ref,
    weight_ref,
    *rest,
):
    earlier, rest = (rest[:2], rest[2:]) if lo else ((), rest)
    image_ref, weighted_ref, lhs, full, update = rest
    width = pair_ref.shape[2]
    half = mine_ref.shape[1]
    patches = prior_ref.shape[1] // width
    own = weighted_ref.shape[1] // width
    node = lax.axis_index("node")
    core = lax.rem(node, 2)

    def weight_of(ref, side):
        return weight_ref[pl.ds(pl.multiple_of(side * half, 8), half), :]

    if slices < 4:
        lhs[...] = jnp.zeros_like(lhs)
    if earlier:
        image_ref[:lo, :] = earlier[0][...]
        weighted_ref[:lo, :] = earlier[1][...]
    weigh(slices, mine_ref, other_ref, weight_of, lhs, full, core, half)
    for s in range(slices):
        for r in range(own):
            weighted_ref[lo + s : lo + s + 1, r * width : (r + 1) * width] = full[
                s, pl.ds(node * own + r, 1), :
            ]
    backward(index_ref, pair_ref, lhs, update)
    for p in range(patches):
        total = update[p * 8 : p * 8 + slices, :] + update[p * 8 + slices : p * 8 + 2 * slices, :]
        image_ref[lo : lo + slices, p * width : (p + 1) * width] = (
            prior_ref[:, p * width : (p + 1) * width] + col_ref[p : p + 1, :] * total
        )


def exchange(value, distance, nodes):
    return lax.ppermute(value, "node", [(i, i ^ distance) for i in range(nodes)])


def body(blocks, block_row, block_patch, block_count, row_map, sinogram, start):
    nodes = lax.axis_size("node")
    count_blocks, width, _ = blocks.shape
    all_slices, pixels = start.shape
    slices = all_slices // CHAINS
    patches = pixels // width
    total_rows = row_map.shape[0]
    half = total_rows // 2
    hbm = pl.BlockSpec(memory_space=pltpu.HBM)
    smem = pl.BlockSpec(memory_space=pltpu.SMEM)
    vmem = pl.BlockSpec(memory_space=pltpu.VMEM)
    params = pltpu.CompilerParams(vmem_limit_bytes=28 * 1024 * 1024)
    small_params = pltpu.CompilerParams(vmem_limit_bytes=20 * 1024 * 1024)

    def in_hbm(value):
        return pltpu.with_memory_space_constraint(value, pltpu.HBM)

    def array(*shape):
        return jax.ShapeDtypeStruct(shape, f32)

    def sum_over_nodes(mine, other):
        value = mine + exchange(other, 1, nodes)
        distance = 2
        while distance < nodes:
            value = value + exchange(value, distance, nodes)
            distance *= 2
        return value, exchange(value, 1, nodes)

    acc_shape = pltpu.VMEM((total_rows * 8, width), f32)
    patch_shape = pltpu.VMEM((patches * 8, width), f32)

    mine, other, col, pair, index = pl.pallas_call(
        functools.partial(first_kernel, 0, slices),
        out_shape=(
            array(slices + 1, half, width),
            array(slices + 1, half, width),
            array(patches, width),
            pltpu.VMEM((count_blocks, 2 * width, width), bf16),
            pltpu.SMEM((2, count_blocks), jnp.int32),
        ),
        in_specs=[hbm] * 2 + [smem] + [hbm] * 4,
        out_specs=(vmem,) * 4 + (smem,),
        scratch_shapes=[
            pltpu.SMEM(block_row.shape, jnp.int32),
            pltpu.SMEM(block_patch.shape, jnp.int32),
            pltpu.SMEM(row_map.shape, jnp.int32),
            pltpu.VMEM(start.shape, f32),
            pltpu.VMEM(sinogram.shape, f32),
            pltpu.VMEM(blocks.shape, f32),
            pltpu.VMEM((patches * 16, width), f32),
            acc_shape,
            acc_shape,
            patch_shape,
            pltpu.SemaphoreType.DMA((CHUNKS,)),
            pltpu.SemaphoreType.DMA((5,)),
        ],
        compiler_params=params,
        name="first",
    )(
        in_hbm(block_row),
        in_hbm(block_patch),
        block_count,
        *map(in_hbm, (row_map, blocks, start, sinogram)),
    )

    def held():
        return (
            pltpu.with_memory_space_constraint(index, pltpu.SMEM),
            pltpu.with_memory_space_constraint(pair, pltpu.VMEM),
        )

    terms = [(mine, other)]
    for chain in range(1, CHAINS):
        terms.append(
            pl.pallas_call(
                functools.partial(second_kernel, chain * slices, slices),
                out_shape=(array(slices, half, width),) * 2,
                in_specs=[smem] + [vmem] * 3,
                out_specs=(vmem,) * 2,
                scratch_shapes=[acc_shape, patch_shape],
                compiler_params=small_params,
                name="second",
            )(*held(), start, sinogram)
        )
    images = []
    weight = None
    for chain in range(CHAINS):
        given = (weight,) if chain else ()
        got = pl.pallas_call(
            functools.partial(middle_kernel, chain * slices, slices),
            out_shape=(
                array(slices, half, width),
                array(slices, half, width),
                array(slices, pixels),
            )
            + (() if chain else (array(total_rows, width),)),
            in_specs=[smem] + [vmem] * (6 + len(given)),
            out_specs=(vmem,) * (3 if chain else 4),
            scratch_shapes=[acc_shape, patch_shape, acc_shape, patch_shape],
            compiler_params=small_params,
            name="middle",
        )(*held(), *sum_over_nodes(*terms[chain]), col, start, sinogram, *given)
        terms[chain] = got[:2]
        images.append(got[2])
        if not chain:
            weight = got[3]
    results = ()
    for chain in range(CHAINS):
        upto = (chain + 1) * slices
        results = pl.pallas_call(
            functools.partial(last_kernel, chain * slices, slices),
            out_shape=(array(upto, pixels), array(upto, sinogram.shape[1])),
            in_specs=[smem] + [vmem] * (6 + len(results)),
            out_specs=(vmem,) * 2,
            scratch_shapes=[
                acc_shape,
                pltpu.VMEM((slices, total_rows, width), f32),
                patch_shape,
            ],
            compiler_params=small_params,
            name="last",
        )(*held(), *sum_over_nodes(*terms[chain]), col, images[chain], weight, *results)
    return results


def solution(mesh):
    placed = (
        P(("grp", "node"), None, None),
        P(("grp", "node")),
        P(("grp", "node")),
        P(("grp", "node")),
        P("grp"),
        P("grp", "node"),
        P("grp", "node"),
    )
    return jax.shard_map(
        body,
        mesh=mesh,
        in_specs=placed,
        out_specs=(P("grp", "node"), P("grp", "node")),
        check_vma=False,
    )
```

time: 68.6 us -> 57.3 us (0.84)
  local copies, waits for them, and re-layouts: 6.18 us -> 0.01 us
  Pallas kernels: 14.2 us -> 9.25 us
    unnamed x12 -> x4, local copies, waits for them, and re-layouts: 6.18 us -> 0.01 us
    pallas_call x3, Pallas kernels: 14.2 us -> 9.25 us  [the longest x1 4.64 us: body(): pl.pallas_call(functools.partial(first_kernel, 0, slices), out_shape=(arr...]
where the time goes in v2:
time: 57.3 us; the launch traced here: 57.2 us
  waiting for transfers between devices  35 us (61%)
  starting transfers between devices  11.3 us (20%)
  Pallas kernels  9.25 us (16%)
  between operations  1.37 us (2%)
    ppermute x10, waiting for transfers between devices, exchange(): lax.ppermute(value, 'node', [(i, i ^ distance) for i in range(nodes)])  35 us
    ppermute x10, starting transfers between devices, exchange(): lax.ppermute(value, 'node', [(i, i ^ distance) for i in range(nodes)])  11.3 us
    pallas_call x1, Pallas kernels, body(): pl.pallas_call(functools.partial(first_kernel, 0, slices), out_shape=(arr...  4.64 us
    pallas_call x1, Pallas kernels, body(): pl.pallas_call(functools.partial(middle_kernel, chain * slices, slices),...  2.9 us
    pallas_call x1, Pallas kernels, body(): pl.pallas_call(functools.partial(last_kernel, chain * slices, slices), ou...  1.7 us
  transfers between devices with their start and end apart: 10, of which 10 were waited for; matrix products, arithmetic and copies ran while one was open for 0% of the time, Pallas kernels for 0%

profile of v2, /device:TPU:0, one launch (start us, length us, event | category | flops | bytes accessed | tf_op | source)
XLA Modules:
  0.0 57.2 jit_solution(13943560210632751304)
XLA Ops:
  0.6 0.0 copy-start
  0.6 0.0 copy-start.1
  1.3 4.6 %first.1 = (f32[5,64,128]{2,1,0:T(8,128)S(1)}, f32[5,64,128]{2,1,0:T(8,128)S(1)}, f32[8,128]{1,0:T(8,128)S(1)}, bf16[96,256,128]{2,1,0:T(8,128)(2,1)S(1)}, s32[2,96]{1,0:T(2,128)S(4)}) custom-call(s32[96]{0:T(128)} %rows_hbm.1, s32[96]{0:T(128)} %patch_hbm.1, s32[1]{0:T(128)S(6)} %copy.9.count_ref, s32[128]{0:T(128)} %map_hbm.1, f32[96,128,128]{2,1,0:T(8,128)} %blocks_ref.1, ...), custom_call_target="tpu_custom_call" | custom-call | tf_op jit(solution)/shard_map/first/pallas_call | solution.py:338
  6.0 0.5 collective-permute-start
  6.5 1.0 %collective-permute-done = f32[5,64,128]{2,1,0:T(8,128)S(1)} collective-permute-done((f32[5,64,128]{2,1,0:T(8,128)S(1)}, f32[5,64,128]{2,1,0:T(8,128)S(1)}, u32[]{:S(2)}, u32[]{:S(2)}) %collective-permute-start) | collective-permute-done | bytes 163872 | tf_op jit(solution)/shard_map/ppermute | solution.py:304
  7.5 3.0 %collective-permute-start.1 = (f32[5,64,128]{2,1,0:T(8,128)S(1)}, f32[5,64,128]{2,1,0:T(8,128)S(1)}, u32[]{:S(2)}, u32[]{:S(2)}) collective-permute-start(f32[5,64,128]{2,1,0:T(8,128)S(1)} %add.24), channel_id=1, source_target_pairs={{0,2},{1,3},{2,0},{3,1},{4,6},{5,7},{6,4},{7,5},{8,10},{9,11},{10,... | collective-permute-start | bytes 491528 | tf_op jit(solution)/shard_map/ppermute | solution.py:304
  10.5 4.5 %collective-permute-done.1 = f32[5,64,128]{2,1,0:T(8,128)S(1)} collective-permute-done((f32[5,64,128]{2,1,0:T(8,128)S(1)}, f32[5,64,128]{2,1,0:T(8,128)S(1)}, u32[]{:S(2)}, u32[]{:S(2)}) %collective-permute-start.1) | collective-permute-done | bytes 163872 | tf_op jit(solution)/shard_map/ppermute | solution.py:304
  15.0 1.9 %collective-permute-start.2 = (f32[5,64,128]{2,1,0:T(8,128)S(1)}, f32[5,64,128]{2,1,0:T(8,128)S(1)}, u32[]{:S(2)}, u32[]{:S(2)}) collective-permute-start(f32[5,64,128]{2,1,0:T(8,128)S(1)} %add.25), channel_id=1, source_target_pairs={{0,4},{1,5},{2,6},{3,7},{4,0},{5,1},{6,2},{7,3},{8,12},{9,13},{10,... | collective-permute-start | bytes 491528 | tf_op jit(solution)/shard_map/ppermute | solution.py:304
  16.9 3.9 %collective-permute-done.2 = f32[5,64,128]{2,1,0:T(8,128)S(1)} collective-permute-done((f32[5,64,128]{2,1,0:T(8,128)S(1)}, f32[5,64,128]{2,1,0:T(8,128)S(1)}, u32[]{:S(2)}, u32[]{:S(2)}) %collective-permute-start.2) | collective-permute-done | bytes 163872 | tf_op jit(solution)/shard_map/ppermute | solution.py:304
  20.8 2.6 %collective-permute-start.3 = (f32[5,64,128]{2,1,0:T(8,128)S(1)}, f32[5,64,128]{2,1,0:T(8,128)S(1)}, u32[]{:S(2)}, u32[]{:S(2)}) collective-permute-start(f32[5,64,128]{2,1,0:T(8,128)S(1)} %add.26), channel_id=1, source_target_pairs={{0,8},{1,9},{2,10},{3,11},{4,12},{5,13},{6,14},{7,15},{8,0},{9,1},... | collective-permute-start | bytes 491528 | tf_op jit(solution)/shard_map/ppermute | solution.py:304
  23.4 6.8 %collective-permute-done.3 = f32[5,64,128]{2,1,0:T(8,128)S(1)} collective-permute-done((f32[5,64,128]{2,1,0:T(8,128)S(1)}, f32[5,64,128]{2,1,0:T(8,128)S(1)}, u32[]{:S(2)}, u32[]{:S(2)}) %collective-permute-start.3) | collective-permute-done | bytes 163872 | tf_op jit(solution)/shard_map/ppermute | solution.py:304
  30.2 0.1 collective-permute-start.4
  30.3 1.4 %collective-permute-done.4.other_ref = f32[5,64,128]{2,1,0:T(8,128)S(1)} collective-permute-done((f32[5,64,128]{2,1,0:T(8,128)S(1)}, f32[5,64,128]{2,1,0:T(8,128)S(1)}, u32[]{:S(2)}, u32[]{:S(2)}) %collective-permute-start.4) | collective-permute-done | bytes 163872 | tf_op jit(solution)/shard_map/ppermute | solution.py:304
  31.6 0.0 copy-done
  31.6 0.0 copy-done.1
  31.6 2.9 %middle.1 = (f32[4,64,128]{2,1,0:T(8,128)S(1)}, f32[4,64,128]{2,1,0:T(8,128)S(1)}, f32[4,1024]{1,0:T(4,128)S(1)}, f32[128,128]{1,0:T(8,128)S(1)}) custom-call(s32[2,96]{1,0:T(2,128)S(4)} %get-tuple-element.11.index_ref, bf16[96,256,128]{2,1,0:T(8,128)(2,1)S(1)} %get-tuple-element.12.pair_ref, f32[5,64,128]{2,1,0:T(8,128)S(1)} %add.27.mine_ref, ...), custom_call_target="tpu_custom_call" | custom-call | tf_op jit(solution)/shard_map/middle/pallas_call | solution.py:395
  34.6 0.2 collective-permute-start.5
  34.8 1.2 %collective-permute-done.5 = f32[4,64,128]{2,1,0:T(8,128)S(1)} collective-permute-done((f32[4,64,128]{2,1,0:T(8,128)S(1)}, f32[4,64,128]{2,1,0:T(8,128)S(1)}, u32[]{:S(2)}, u32[]{:S(2)}) %collective-permute-start.5) | collective-permute-done | bytes 131104 | tf_op jit(solution)/shard_map/ppermute | solution.py:304
  36.0 1.1 %collective-permute-start.6 = (f32[4,64,128]{2,1,0:T(8,128)S(1)}, f32[4,64,128]{2,1,0:T(8,128)S(1)}, u32[]{:S(2)}, u32[]{:S(2)}) collective-permute-start(f32[4,64,128]{2,1,0:T(8,128)S(1)} %add.28), channel_id=1, source_target_pairs={{0,2},{1,3},{2,0},{3,1},{4,6},{5,7},{6,4},{7,5},{8,10},{9,11},{10,... | collective-permute-start | bytes 393224 | tf_op jit(solution)/shard_map/ppermute | solution.py:304
  37.1 4.5 %collective-permute-done.6 = f32[4,64,128]{2,1,0:T(8,128)S(1)} collective-permute-done((f32[4,64,128]{2,1,0:T(8,128)S(1)}, f32[4,64,128]{2,1,0:T(8,128)S(1)}, u32[]{:S(2)}, u32[]{:S(2)}) %collective-permute-start.6) | collective-permute-done | bytes 131104 | tf_op jit(solution)/shard_map/ppermute | solution.py:304
  41.6 0.3 collective-permute-start.7
  41.9 4.7 %collective-permute-done.7 = f32[4,64,128]{2,1,0:T(8,128)S(1)} collective-permute-done((f32[4,64,128]{2,1,0:T(8,128)S(1)}, f32[4,64,128]{2,1,0:T(8,128)S(1)}, u32[]{:S(2)}, u32[]{:S(2)}) %collective-permute-start.7) | collective-permute-done | bytes 131104 | tf_op jit(solution)/shard_map/ppermute | solution.py:304
  46.7 1.7 %collective-permute-start.8 = (f32[4,64,128]{2,1,0:T(8,128)S(1)}, f32[4,64,128]{2,1,0:T(8,128)S(1)}, u32[]{:S(2)}, u32[]{:S(2)}) collective-permute-start(f32[4,64,128]{2,1,0:T(8,128)S(1)} %add.30), channel_id=1, source_target_pairs={{0,8},{1,9},{2,10},{3,11},{4,12},{5,13},{6,14},{7,15},{8,0},{9,1},... | collective-permute-start | bytes 393224 | tf_op jit(solution)/shard_map/ppermute | solution.py:304
  48.4 5.7 %collective-permute-done.8 = f32[4,64,128]{2,1,0:T(8,128)S(1)} collective-permute-done((f32[4,64,128]{2,1,0:T(8,128)S(1)}, f32[4,64,128]{2,1,0:T(8,128)S(1)}, u32[]{:S(2)}, u32[]{:S(2)}) %collective-permute-start.8) | collective-permute-done | bytes 131104 | tf_op jit(solution)/shard_map/ppermute | solution.py:304
  54.0 0.1 collective-permute-start.9
  54.1 1.3 %collective-permute-done.9.other_ref = f32[4,64,128]{2,1,0:T(8,128)S(1)} collective-permute-done((f32[4,64,128]{2,1,0:T(8,128)S(1)}, f32[4,64,128]{2,1,0:T(8,128)S(1)}, u32[]{:S(2)}, u32[]{:S(2)}) %collective-permute-start.9) | collective-permute-done | bytes 131104 | tf_op jit(solution)/shard_map/ppermute | solution.py:304
  55.5 1.7 %last.1 = (f32[4,1024]{1,0:T(4,128)}, f32[4,1024]{1,0:T(4,128)}) custom-call(s32[2,96]{1,0:T(2,128)S(4)} %get-tuple-element.11.index_ref, bf16[96,256,128]{2,1,0:T(8,128)(2,1)S(1)} %get-tuple-element.12.pair_ref, f32[4,64,128]{2,1,0:T(8,128)S(1)} %add.31.mine_ref, f32[4,64,128]{2,1,0:T(8,128)S(1)} %collective-permute-done.9.other_ref, ...), custom_call_target="tpu_custom_call" | custom-call | tf_op jit(solution)/shard_map/last/pallas_call | solution.py:416
  (8 shorter events, 0.2 us)
Async XLA Ops:
  0.6 31.0 %copy-start = (f32[4,1024]{1,0:T(4,128)S(1)}, f32[4,1024]{1,0:T(4,128)}, u32[]{:S(2)}) copy-start(f32[4,1024]{1,0:T(4,128)} %start_ref.1) | copy-start | bytes 49156
  0.6 31.0 %copy-start.1 = (f32[4,1024]{1,0:T(4,128)S(1)}, f32[4,1024]{1,0:T(4,128)}, u32[]{:S(2)}) copy-start(f32[4,1024]{1,0:T(4,128)} %sino_ref.1) | copy-start | bytes 49156
  6.0 1.5 %collective-permute-start = (f32[5,64,128]{2,1,0:T(8,128)S(1)}, f32[5,64,128]{2,1,0:T(8,128)S(1)}, u32[]{:S(2)}, u32[]{:S(2)}) collective-permute-start(f32[5,64,128]{2,1,0:T(8,128)S(1)} %get-tuple-element.14), channel_id=1, source_target_pairs={{0,1},{1,0},{2,3},{3,2},{4,5},{5,4},{6,7},{7,6},{8,9},{9,8},{10,11... | collective-permute-start | bytes 491528 | tf_op jit(solution)/shard_map/ppermute | solution.py:304
  7.5 7.5 %collective-permute-start.1 = (f32[5,64,128]{2,1,0:T(8,128)S(1)}, f32[5,64,128]{2,1,0:T(8,128)S(1)}, u32[]{:S(2)}, u32[]{:S(2)}) collective-permute-start(f32[5,64,128]{2,1,0:T(8,128)S(1)} %add.24), channel_id=1, source_target_pairs={{0,2},{1,3},{2,0},{3,1},{4,6},{5,7},{6,4},{7,5},{8,10},{9,11},{10,... | collective-permute-start | bytes 491528 | tf_op jit(solution)/shard_map/ppermute | solution.py:304
  15.0 5.8 %collective-permute-start.2 = (f32[5,64,128]{2,1,0:T(8,128)S(1)}, f32[5,64,128]{2,1,0:T(8,128)S(1)}, u32[]{:S(2)}, u32[]{:S(2)}) collective-permute-start(f32[5,64,128]{2,1,0:T(8,128)S(1)} %add.25), channel_id=1, source_target_pairs={{0,4},{1,5},{2,6},{3,7},{4,0},{5,1},{6,2},{7,3},{8,12},{9,13},{10,... | collective-permute-start | bytes 491528 | tf_op jit(solution)/shard_map/ppermute | solution.py:304
  20.8 9.3 %collective-permute-start.3 = (f32[5,64,128]{2,1,0:T(8,128)S(1)}, f32[5,64,128]{2,1,0:T(8,128)S(1)}, u32[]{:S(2)}, u32[]{:S(2)}) collective-permute-start(f32[5,64,128]{2,1,0:T(8,128)S(1)} %add.26), channel_id=1, source_target_pairs={{0,8},{1,9},{2,10},{3,11},{4,12},{5,13},{6,14},{7,15},{8,0},{9,1},... | collective-permute-start | bytes 491528 | tf_op jit(solution)/shard_map/ppermute | solution.py:304
  30.2 1.5 %collective-permute-start.4 = (f32[5,64,128]{2,1,0:T(8,128)S(1)}, f32[5,64,128]{2,1,0:T(8,128)S(1)}, u32[]{:S(2)}, u32[]{:S(2)}) collective-permute-start(f32[5,64,128]{2,1,0:T(8,128)S(1)} %add.27.mine_ref), channel_id=1, source_target_pairs={{0,1},{1,0},{2,3},{3,2},{4,5},{5,4},{6,7},{7,6},{8,9},{9,8},{10,11... | collective-permute-start | bytes 491528 | tf_op jit(solution)/shard_map/ppermute | solution.py:304
  34.6 1.4 %collective-permute-start.5 = (f32[4,64,128]{2,1,0:T(8,128)S(1)}, f32[4,64,128]{2,1,0:T(8,128)S(1)}, u32[]{:S(2)}, u32[]{:S(2)}) collective-permute-start(f32[4,64,128]{2,1,0:T(8,128)S(1)} %get-tuple-element.17), channel_id=1, source_target_pairs={{0,1},{1,0},{2,3},{3,2},{4,5},{5,4},{6,7},{7,6},{8,9},{9,8},{10,11... | collective-permute-start | bytes 393224 | tf_op jit(solution)/shard_map/ppermute | solution.py:304
  36.0 5.6 %collective-permute-start.6 = (f32[4,64,128]{2,1,0:T(8,128)S(1)}, f32[4,64,128]{2,1,0:T(8,128)S(1)}, u32[]{:S(2)}, u32[]{:S(2)}) collective-permute-start(f32[4,64,128]{2,1,0:T(8,128)S(1)} %add.28), channel_id=1, source_target_pairs={{0,2},{1,3},{2,0},{3,1},{4,6},{5,7},{6,4},{7,5},{8,10},{9,11},{10,... | collective-permute-start | bytes 393224 | tf_op jit(solution)/shard_map/ppermute | solution.py:304
  41.6 5.0 %collective-permute-start.7 = (f32[4,64,128]{2,1,0:T(8,128)S(1)}, f32[4,64,128]{2,1,0:T(8,128)S(1)}, u32[]{:S(2)}, u32[]{:S(2)}) collective-permute-start(f32[4,64,128]{2,1,0:T(8,128)S(1)} %add.29), channel_id=1, source_target_pairs={{0,4},{1,5},{2,6},{3,7},{4,0},{5,1},{6,2},{7,3},{8,12},{9,13},{10,... | collective-permute-start | bytes 393224 | tf_op jit(solution)/shard_map/ppermute | solution.py:304
  46.7 7.3 %collective-permute-start.8 = (f32[4,64,128]{2,1,0:T(8,128)S(1)}, f32[4,64,128]{2,1,0:T(8,128)S(1)}, u32[]{:S(2)}, u32[]{:S(2)}) collective-permute-start(f32[4,64,128]{2,1,0:T(8,128)S(1)} %add.30), channel_id=1, source_target_pairs={{0,8},{1,9},{2,10},{3,11},{4,12},{5,13},{6,14},{7,15},{8,0},{9,1},... | collective-permute-start | bytes 393224 | tf_op jit(solution)/shard_map/ppermute | solution.py:304
  54.0 1.4 %collective-permute-start.9 = (f32[4,64,128]{2,1,0:T(8,128)S(1)}, f32[4,64,128]{2,1,0:T(8,128)S(1)}, u32[]{:S(2)}, u32[]{:S(2)}) collective-permute-start(f32[4,64,128]{2,1,0:T(8,128)S(1)} %add.31.mine_ref), channel_id=1, source_target_pairs={{0,1},{1,0},{2,3},{3,2},{4,5},{5,4},{6,7},{7,6},{8,9},{9,8},{10,11... | collective-permute-start | bytes 393224 | tf_op jit(solution)/shard_map/ppermute | solution.py:304

commit v3 on v2

--- a/solution.py
+++ b/solution.py
@@ -7,7 +7,7 @@
 from jax.experimental.pallas import tpu as pltpu
 from jax.sharding import PartitionSpec as P
 
-CHUNKS = 8
+CHUNKS = 4
 CHAINS = 1
 
 relax_factor = 1.9
@@ -40,11 +40,12 @@
     return pl.ds(pl.multiple_of(index * 8, 8), 8)
 
 
-def minus_measured(acc, sino_ref, width, node):
+def minus_measured(acc, sino_ref, lo, slices, width, node):
     own = sino_ref.shape[1] // width
-    slices = sino_ref.shape[0]
     for r in range(own):
-        acc[pl.ds((node * own + r) * 8, slices), :] = -sino_ref[:, r * width : (r + 1) * width]
+        acc[pl.ds((node * own + r) * 8, slices), :] = -sino_ref[
+            lo : lo + slices, r * width : (r + 1) * width
+        ]
 
 
 def write_halves(acc, slices, core, half, mine_ref, other_ref):
@@ -68,7 +69,7 @@
     slices,
     rows_hbm,
     patch_hbm,
-    count_ref,
+    count_hbm,
     map_hbm,
     blocks_ref,
     start_hbm,
@@ -80,6 +81,7 @@
     index_ref,
     rows_ref,
     patch_ref,
+    count_ref,
     map_ref,
     start_ref,
     sino_ref,
@@ -111,6 +113,7 @@
                 (sino_hbm, sino_ref),
                 (rows_hbm, rows_ref),
                 (patch_hbm, patch_ref),
+                (count_hbm, count_ref),
                 (map_hbm, map_ref),
             )
         )
@@ -129,7 +132,7 @@
     for p in range(patches):
         fill_lhs(lhs, p, 16, start_ref[lo : lo + slices, p * width : (p + 1) * width], slices)
         lhs[p * 16 + 8 : p * 16 + 9, :] = jnp.ones((1, width), f32)
-    minus_measured(acc, sino_ref.at[lo : lo + slices], width, node)
+    minus_measured(acc, sino_ref, lo, slices, width, node)
     count = count_ref[0]
 
     for k in range(CHUNKS):
@@ -138,12 +141,13 @@
         places = []
         terms = []
         for j in slots:
-            position = map_ref[rows_ref[j]]
-            patch = patch_ref[j]
+            live = j < count
+            position = jnp.where(live, map_ref[rows_ref[j]], total_rows)
+            patch = jnp.where(live, patch_ref[j], patches)
             index_ref[0, j] = position
             index_ref[1, j] = patch
             places.append(at8(position))
-            block = jnp.where(j < count, stage[j], 0.0)
+            block = stage[j]
             high = block.astype(bf16)
             pair = jnp.concatenate([high, (block - high.astype(f32)).astype(bf16)], axis=0)
             pair_ref[j] = pair
@@ -203,7 +207,7 @@
     for p in range(patches):
         fill_lhs(image_lhs, p, 8, start_ref[lo : lo + slices, p * width : (p + 1) * width], slices)
     acc[...] = jnp.zeros_like(acc)
-    minus_measured(acc, sino_ref.at[lo : lo + slices], width, node)
+    minus_measured(acc, sino_ref, lo, slices, width, node)
     forward(index_ref, pair_ref, image_lhs, acc)
     write_halves(acc, slices, lax.rem(node, 2), half, mine_ref, other_ref)
 
@@ -241,6 +245,8 @@
     if slices < 4:
         lhs[...] = jnp.zeros_like(lhs)
         image_lhs[...] = jnp.zeros_like(image_lhs)
+    lhs[2 * half * 8 :, :] = jnp.zeros((8, width), f32)
+    image_lhs[patches * 8 :, :] = jnp.zeros((8, width), f32)
     weigh(slices, mine_ref, other_ref, weight_of, lhs, None, core, half)
     backward(index_ref, pair_ref, lhs, update)
     for p in range(patches):
@@ -252,7 +258,7 @@
         image_ref[:, p * width : (p + 1) * width] = value
         fill_lhs(image_lhs, p, 8, value, slices)
     acc[...] = jnp.zeros_like(acc)
-    minus_measured(acc, sino_ref.at[lo : lo + slices], width, node)
+    minus_measured(acc, sino_ref, lo, slices, width, node)
     forward(index_ref, pair_ref, image_lhs, acc)
     write_halves(acc, slices, core, half, next_mine_ref, next_other_ref)
 
@@ -286,6 +292,7 @@
     if earlier:
         image_ref[:lo, :] = earlier[0][...]
         weighted_ref[:lo, :] = earlier[1][...]
+    lhs[2 * half * 8 :, :] = jnp.zeros((8, width), f32)
     weigh(slices, mine_ref, other_ref, weight_of, lhs, full, core, half)
     for s in range(slices):
         for r in range(own):
@@ -332,8 +339,8 @@
             distance *= 2
         return value, exchange(value, 1, nodes)
 
-    acc_shape = pltpu.VMEM((total_rows * 8, width), f32)
-    patch_shape = pltpu.VMEM((patches * 8, width), f32)
+    acc_shape = pltpu.VMEM((total_rows * 8 + 8, width), f32)
+    patch_shape = pltpu.VMEM((patches * 8 + 8, width), f32)
 
     mine, other, col, pair, index = pl.pallas_call(
         functools.partial(first_kernel, 0, slices),
@@ -344,21 +351,22 @@
             pltpu.VMEM((count_blocks, 2 * width, width), bf16),
             pltpu.SMEM((2, count_blocks), jnp.int32),
         ),
-        in_specs=[hbm] * 2 + [smem] + [hbm] * 4,
+        in_specs=[hbm] * 2 + [pl.BlockSpec(memory_space=pl.ANY)] + [hbm] * 4,
         out_specs=(vmem,) * 4 + (smem,),
         scratch_shapes=[
             pltpu.SMEM(block_row.shape, jnp.int32),
             pltpu.SMEM(block_patch.shape, jnp.int32),
+            pltpu.SMEM(block_count.shape, jnp.int32),
             pltpu.SMEM(row_map.shape, jnp.int32),
             pltpu.VMEM(start.shape, f32),
             pltpu.VMEM(sinogram.shape, f32),
             pltpu.VMEM(blocks.shape, f32),
-            pltpu.VMEM((patches * 16, width), f32),
+            pltpu.VMEM((patches * 16 + 16, width), f32),
             acc_shape,
             acc_shape,
             patch_shape,
             pltpu.SemaphoreType.DMA((CHUNKS,)),
-            pltpu.SemaphoreType.DMA((5,)),
+            pltpu.SemaphoreType.DMA((6,)),
         ],
         compiler_params=params,
         name="first",

time: 57.3 us -> 56.8 us (level)
  Pallas kernels: 9.25 us -> 8.53 us
    pallas_call x1, Pallas kernels: 4.64 us -> 3.89 us  [body(): pl.pallas_call(functools.partial(first_kernel, 0, slices), out_shape=(arr...]
where the time goes in v3:
time: 56.8 us; the launch traced here: 56.5 us
  waiting for transfers between devices  34.7 us (61%)
  starting transfers between devices  11.7 us (21%)
  Pallas kernels  8.53 us (15%)
  between operations  1.37 us (2%)
    ppermute x10, waiting for transfers between devices, exchange(): lax.ppermute(value, 'node', [(i, i ^ distance) for i in range(nodes)])  34.7 us
    ppermute x10, starting transfers between devices, exchange(): lax.ppermute(value, 'node', [(i, i ^ distance) for i in range(nodes)])  11.7 us
    pallas_call x1, Pallas kernels, body(): pl.pallas_call(functools.partial(first_kernel, 0, slices), out_shape=(arr...  3.89 us
    pallas_call x1, Pallas kernels, body(): pl.pallas_call(functools.partial(middle_kernel, chain * slices, slices),...  2.93 us
    pallas_call x1, Pallas kernels, body(): pl.pallas_call(functools.partial(last_kernel, chain * slices, slices), ou...  1.71 us
  transfers between devices with their start and end apart: 10, of which 10 were waited for; matrix products, arithmetic and copies ran while one was open for 0% of the time, Pallas kernels for 0%

profile of v3, /device:TPU:0, one launch (start us, length us, event | category | flops | bytes accessed | tf_op | source)
XLA Modules:
  0.0 56.5 jit_solution(16224779687752350166)
XLA Ops:
  0.6 0.0 copy-start
  0.6 0.0 copy-start.1
  1.3 3.9 %first.1 = (f32[5,64,128]{2,1,0:T(8,128)S(1)}, f32[5,64,128]{2,1,0:T(8,128)S(1)}, f32[8,128]{1,0:T(8,128)S(1)}, bf16[96,256,128]{2,1,0:T(8,128)(2,1)S(1)}, s32[2,96]{1,0:T(2,128)S(4)}) custom-call(s32[96]{0:T(128)} %rows_hbm.1, s32[96]{0:T(128)} %patch_hbm.1, s32[1]{0:T(128)S(6)} %copy.9.count_hbm, s32[128]{0:T(128)} %map_hbm.1, f32[96,128,128]{2,1,0:T(8,128)} %blocks_ref.1, ...), custom_call_target="tpu_custom_call" | custom-call | tf_op jit(solution)/shard_map/first/pallas_call | solution.py:345
  5.2 0.5 collective-permute-start
  5.7 1.0 %collective-permute-done = f32[5,64,128]{2,1,0:T(8,128)S(1)} collective-permute-done((f32[5,64,128]{2,1,0:T(8,128)S(1)}, f32[5,64,128]{2,1,0:T(8,128)S(1)}, u32[]{:S(2)}, u32[]{:S(2)}) %collective-permute-start) | collective-permute-done | bytes 163872 | tf_op jit(solution)/shard_map/ppermute | solution.py:311
  6.8 3.0 %collective-permute-start.1 = (f32[5,64,128]{2,1,0:T(8,128)S(1)}, f32[5,64,128]{2,1,0:T(8,128)S(1)}, u32[]{:S(2)}, u32[]{:S(2)}) collective-permute-start(f32[5,64,128]{2,1,0:T(8,128)S(1)} %add.24), channel_id=1, source_target_pairs={{0,2},{1,3},{2,0},{3,1},{4,6},{5,7},{6,4},{7,5},{8,10},{9,11},{10,... | collective-permute-start | bytes 491528 | tf_op jit(solution)/shard_map/ppermute | solution.py:311
  9.8 4.5 %collective-permute-done.1 = f32[5,64,128]{2,1,0:T(8,128)S(1)} collective-permute-done((f32[5,64,128]{2,1,0:T(8,128)S(1)}, f32[5,64,128]{2,1,0:T(8,128)S(1)}, u32[]{:S(2)}, u32[]{:S(2)}) %collective-permute-start.1) | collective-permute-done | bytes 163872 | tf_op jit(solution)/shard_map/ppermute | solution.py:311
  14.3 1.8 %collective-permute-start.2 = (f32[5,64,128]{2,1,0:T(8,128)S(1)}, f32[5,64,128]{2,1,0:T(8,128)S(1)}, u32[]{:S(2)}, u32[]{:S(2)}) collective-permute-start(f32[5,64,128]{2,1,0:T(8,128)S(1)} %add.25), channel_id=1, source_target_pairs={{0,4},{1,5},{2,6},{3,7},{4,0},{5,1},{6,2},{7,3},{8,12},{9,13},{10,... | collective-permute-start | bytes 491528 | tf_op jit(solution)/shard_map/ppermute | solution.py:311
  16.2 4.0 %collective-permute-done.2 = f32[5,64,128]{2,1,0:T(8,128)S(1)} collective-permute-done((f32[5,64,128]{2,1,0:T(8,128)S(1)}, f32[5,64,128]{2,1,0:T(8,128)S(1)}, u32[]{:S(2)}, u32[]{:S(2)}) %collective-permute-start.2) | collective-permute-done | bytes 163872 | tf_op jit(solution)/shard_map/ppermute | solution.py:311
  20.1 2.6 %collective-permute-start.3 = (f32[5,64,128]{2,1,0:T(8,128)S(1)}, f32[5,64,128]{2,1,0:T(8,128)S(1)}, u32[]{:S(2)}, u32[]{:S(2)}) collective-permute-start(f32[5,64,128]{2,1,0:T(8,128)S(1)} %add.26), channel_id=1, source_target_pairs={{0,8},{1,9},{2,10},{3,11},{4,12},{5,13},{6,14},{7,15},{8,0},{9,1},... | collective-permute-start | bytes 491528 | tf_op jit(solution)/shard_map/ppermute | solution.py:311
  22.7 6.7 %collective-permute-done.3 = f32[5,64,128]{2,1,0:T(8,128)S(1)} collective-permute-done((f32[5,64,128]{2,1,0:T(8,128)S(1)}, f32[5,64,128]{2,1,0:T(8,128)S(1)}, u32[]{:S(2)}, u32[]{:S(2)}) %collective-permute-start.3) | collective-permute-done | bytes 163872 | tf_op jit(solution)/shard_map/ppermute | solution.py:311
  29.5 0.1 collective-permute-start.4
  29.6 1.4 %collective-permute-done.4.other_ref = f32[5,64,128]{2,1,0:T(8,128)S(1)} collective-permute-done((f32[5,64,128]{2,1,0:T(8,128)S(1)}, f32[5,64,128]{2,1,0:T(8,128)S(1)}, u32[]{:S(2)}, u32[]{:S(2)}) %collective-permute-start.4) | collective-permute-done | bytes 163872 | tf_op jit(solution)/shard_map/ppermute | solution.py:311
  30.9 0.0 copy-done
  30.9 0.0 copy-done.1
  30.9 2.9 %middle.1 = (f32[4,64,128]{2,1,0:T(8,128)S(1)}, f32[4,64,128]{2,1,0:T(8,128)S(1)}, f32[4,1024]{1,0:T(4,128)S(1)}, f32[128,128]{1,0:T(8,128)S(1)}) custom-call(s32[2,96]{1,0:T(2,128)S(4)} %get-tuple-element.11.index_ref, bf16[96,256,128]{2,1,0:T(8,128)(2,1)S(1)} %get-tuple-element.12.pair_ref, f32[5,64,128]{2,1,0:T(8,128)S(1)} %add.27.mine_ref, ...), custom_call_target="tpu_custom_call" | custom-call | tf_op jit(solution)/shard_map/middle/pallas_call | solution.py:403
  33.9 0.2 collective-permute-start.5
  34.1 1.2 %collective-permute-done.5 = f32[4,64,128]{2,1,0:T(8,128)S(1)} collective-permute-done((f32[4,64,128]{2,1,0:T(8,128)S(1)}, f32[4,64,128]{2,1,0:T(8,128)S(1)}, u32[]{:S(2)}, u32[]{:S(2)}) %collective-permute-start.5) | collective-permute-done | bytes 131104 | tf_op jit(solution)/shard_map/ppermute | solution.py:311
  35.3 1.2 %collective-permute-start.6 = (f32[4,64,128]{2,1,0:T(8,128)S(1)}, f32[4,64,128]{2,1,0:T(8,128)S(1)}, u32[]{:S(2)}, u32[]{:S(2)}) collective-permute-start(f32[4,64,128]{2,1,0:T(8,128)S(1)} %add.28), channel_id=1, source_target_pairs={{0,2},{1,3},{2,0},{3,1},{4,6},{5,7},{6,4},{7,5},{8,10},{9,11},{10,... | collective-permute-start | bytes 393224 | tf_op jit(solution)/shard_map/ppermute | solution.py:311
  36.5 4.4 %collective-permute-done.6 = f32[4,64,128]{2,1,0:T(8,128)S(1)} collective-permute-done((f32[4,64,128]{2,1,0:T(8,128)S(1)}, f32[4,64,128]{2,1,0:T(8,128)S(1)}, u32[]{:S(2)}, u32[]{:S(2)}) %collective-permute-start.6) | collective-permute-done | bytes 131104 | tf_op jit(solution)/shard_map/ppermute | solution.py:311
  40.9 0.4 collective-permute-start.7
  41.3 4.6 %collective-permute-done.7 = f32[4,64,128]{2,1,0:T(8,128)S(1)} collective-permute-done((f32[4,64,128]{2,1,0:T(8,128)S(1)}, f32[4,64,128]{2,1,0:T(8,128)S(1)}, u32[]{:S(2)}, u32[]{:S(2)}) %collective-permute-start.7) | collective-permute-done | bytes 131104 | tf_op jit(solution)/shard_map/ppermute | solution.py:311
  46.0 1.9 %collective-permute-start.8 = (f32[4,64,128]{2,1,0:T(8,128)S(1)}, f32[4,64,128]{2,1,0:T(8,128)S(1)}, u32[]{:S(2)}, u32[]{:S(2)}) collective-permute-start(f32[4,64,128]{2,1,0:T(8,128)S(1)} %add.30), channel_id=1, source_target_pairs={{0,8},{1,9},{2,10},{3,11},{4,12},{5,13},{6,14},{7,15},{8,0},{9,1},... | collective-permute-start | bytes 393224 | tf_op jit(solution)/shard_map/ppermute | solution.py:311
  47.9 5.5 %collective-permute-done.8 = f32[4,64,128]{2,1,0:T(8,128)S(1)} collective-permute-done((f32[4,64,128]{2,1,0:T(8,128)S(1)}, f32[4,64,128]{2,1,0:T(8,128)S(1)}, u32[]{:S(2)}, u32[]{:S(2)}) %collective-permute-start.8) | collective-permute-done | bytes 131104 | tf_op jit(solution)/shard_map/ppermute | solution.py:311
  53.4 0.1 collective-permute-start.9
  53.4 1.3 %collective-permute-done.9.other_ref = f32[4,64,128]{2,1,0:T(8,128)S(1)} collective-permute-done((f32[4,64,128]{2,1,0:T(8,128)S(1)}, f32[4,64,128]{2,1,0:T(8,128)S(1)}, u32[]{:S(2)}, u32[]{:S(2)}) %collective-permute-start.9) | collective-permute-done | bytes 131104 | tf_op jit(solution)/shard_map/ppermute | solution.py:311
  54.8 1.7 %last.1 = (f32[4,1024]{1,0:T(4,128)}, f32[4,1024]{1,0:T(4,128)}) custom-call(s32[2,96]{1,0:T(2,128)S(4)} %get-tuple-element.11.index_ref, bf16[96,256,128]{2,1,0:T(8,128)(2,1)S(1)} %get-tuple-element.12.pair_ref, f32[4,64,128]{2,1,0:T(8,128)S(1)} %add.31.mine_ref, f32[4,64,128]{2,1,0:T(8,128)S(1)} %collective-permute-done.9.other_ref, ...), custom_call_target="tpu_custom_call" | custom-call | tf_op jit(solution)/shard_map/last/pallas_call | solution.py:424
  (8 shorter events, 0.2 us)
Async XLA Ops:
  0.6 30.3 %copy-start = (f32[4,1024]{1,0:T(4,128)S(1)}, f32[4,1024]{1,0:T(4,128)}, u32[]{:S(2)}) copy-start(f32[4,1024]{1,0:T(4,128)} %start_ref.1) | copy-start | bytes 49156
  0.6 30.3 %copy-start.1 = (f32[4,1024]{1,0:T(4,128)S(1)}, f32[4,1024]{1,0:T(4,128)}, u32[]{:S(2)}) copy-start(f32[4,1024]{1,0:T(4,128)} %sino_ref.1) | copy-start | bytes 49156
  5.2 1.6 %collective-permute-start = (f32[5,64,128]{2,1,0:T(8,128)S(1)}, f32[5,64,128]{2,1,0:T(8,128)S(1)}, u32[]{:S(2)}, u32[]{:S(2)}) collective-permute-start(f32[5,64,128]{2,1,0:T(8,128)S(1)} %get-tuple-element.14), channel_id=1, source_target_pairs={{0,1},{1,0},{2,3},{3,2},{4,5},{5,4},{6,7},{7,6},{8,9},{9,8},{10,11... | collective-permute-start | bytes 491528 | tf_op jit(solution)/shard_map/ppermute | solution.py:311
  6.8 7.5 %collective-permute-start.1 = (f32[5,64,128]{2,1,0:T(8,128)S(1)}, f32[5,64,128]{2,1,0:T(8,128)S(1)}, u32[]{:S(2)}, u32[]{:S(2)}) collective-permute-start(f32[5,64,128]{2,1,0:T(8,128)S(1)} %add.24), channel_id=1, source_target_pairs={{0,2},{1,3},{2,0},{3,1},{4,6},{5,7},{6,4},{7,5},{8,10},{9,11},{10,... | collective-permute-start | bytes 491528 | tf_op jit(solution)/shard_map/ppermute | solution.py:311
  14.3 5.8 %collective-permute-start.2 = (f32[5,64,128]{2,1,0:T(8,128)S(1)}, f32[5,64,128]{2,1,0:T(8,128)S(1)}, u32[]{:S(2)}, u32[]{:S(2)}) collective-permute-start(f32[5,64,128]{2,1,0:T(8,128)S(1)} %add.25), channel_id=1, source_target_pairs={{0,4},{1,5},{2,6},{3,7},{4,0},{5,1},{6,2},{7,3},{8,12},{9,13},{10,... | collective-permute-start | bytes 491528 | tf_op jit(solution)/shard_map/ppermute | solution.py:311
  20.1 9.3 %collective-permute-start.3 = (f32[5,64,128]{2,1,0:T(8,128)S(1)}, f32[5,64,128]{2,1,0:T(8,128)S(1)}, u32[]{:S(2)}, u32[]{:S(2)}) collective-permute-start(f32[5,64,128]{2,1,0:T(8,128)S(1)} %add.26), channel_id=1, source_target_pairs={{0,8},{1,9},{2,10},{3,11},{4,12},{5,13},{6,14},{7,15},{8,0},{9,1},... | collective-permute-start | bytes 491528 | tf_op jit(solution)/shard_map/ppermute | solution.py:311
  29.5 1.5 %collective-permute-start.4 = (f32[5,64,128]{2,1,0:T(8,128)S(1)}, f32[5,64,128]{2,1,0:T(8,128)S(1)}, u32[]{:S(2)}, u32[]{:S(2)}) collective-permute-start(f32[5,64,128]{2,1,0:T(8,128)S(1)} %add.27.mine_ref), channel_id=1, source_target_pairs={{0,1},{1,0},{2,3},{3,2},{4,5},{5,4},{6,7},{7,6},{8,9},{9,8},{10,11... | collective-permute-start | bytes 491528 | tf_op jit(solution)/shard_map/ppermute | solution.py:311
  33.9 1.4 %collective-permute-start.5 = (f32[4,64,128]{2,1,0:T(8,128)S(1)}, f32[4,64,128]{2,1,0:T(8,128)S(1)}, u32[]{:S(2)}, u32[]{:S(2)}) collective-permute-start(f32[4,64,128]{2,1,0:T(8,128)S(1)} %get-tuple-element.17), channel_id=1, source_target_pairs={{0,1},{1,0},{2,3},{3,2},{4,5},{5,4},{6,7},{7,6},{8,9},{9,8},{10,11... | collective-permute-start | bytes 393224 | tf_op jit(solution)/shard_map/ppermute | solution.py:311
  35.3 5.6 %collective-permute-start.6 = (f32[4,64,128]{2,1,0:T(8,128)S(1)}, f32[4,64,128]{2,1,0:T(8,128)S(1)}, u32[]{:S(2)}, u32[]{:S(2)}) collective-permute-start(f32[4,64,128]{2,1,0:T(8,128)S(1)} %add.28), channel_id=1, source_target_pairs={{0,2},{1,3},{2,0},{3,1},{4,6},{5,7},{6,4},{7,5},{8,10},{9,11},{10,... | collective-permute-start | bytes 393224 | tf_op jit(solution)/shard_map/ppermute | solution.py:311
  40.9 5.0 %collective-permute-start.7 = (f32[4,64,128]{2,1,0:T(8,128)S(1)}, f32[4,64,128]{2,1,0:T(8,128)S(1)}, u32[]{:S(2)}, u32[]{:S(2)}) collective-permute-start(f32[4,64,128]{2,1,0:T(8,128)S(1)} %add.29), channel_id=1, source_target_pairs={{0,4},{1,5},{2,6},{3,7},{4,0},{5,1},{6,2},{7,3},{8,12},{9,13},{10,... | collective-permute-start | bytes 393224 | tf_op jit(solution)/shard_map/ppermute | solution.py:311
  46.0 7.3 %collective-permute-start.8 = (f32[4,64,128]{2,1,0:T(8,128)S(1)}, f32[4,64,128]{2,1,0:T(8,128)S(1)}, u32[]{:S(2)}, u32[]{:S(2)}) collective-permute-start(f32[4,64,128]{2,1,0:T(8,128)S(1)} %add.30), channel_id=1, source_target_pairs={{0,8},{1,9},{2,10},{3,11},{4,12},{5,13},{6,14},{7,15},{8,0},{9,1},... | collective-permute-start | bytes 393224 | tf_op jit(solution)/shard_map/ppermute | solution.py:311
  53.4 1.4 %collective-permute-start.9 = (f32[4,64,128]{2,1,0:T(8,128)S(1)}, f32[4,64,128]{2,1,0:T(8,128)S(1)}, u32[]{:S(2)}, u32[]{:S(2)}) collective-permute-start(f32[4,64,128]{2,1,0:T(8,128)S(1)} %add.31.mine_ref), channel_id=1, source_target_pairs={{0,1},{1,0},{2,3},{3,2},{4,5},{5,4},{6,7},{7,6},{8,9},{9,8},{10,11... | collective-permute-start | bytes 393224 | tf_op jit(solution)/shard_map/ppermute | solution.py:311

commit v4 on v3

--- a/solution.py
+++ b/solution.py
@@ -331,13 +331,20 @@
     def array(*shape):
         return jax.ShapeDtypeStruct(shape, f32)
 
+    distances = [2**k for k in range(1, nodes.bit_length() - 1)]
+    swapped = distances[1::-1] + distances[2:]
+
     def sum_over_nodes(mine, other):
-        value = mine + exchange(other, 1, nodes)
-        distance = 2
-        while distance < nodes:
-            value = value + exchange(value, distance, nodes)
-            distance *= 2
-        return value, exchange(value, 1, nodes)
+        cut = 2
+        values = [
+            m + exchange(o, 1, nodes)
+            for m, o in ((mine[:cut], other[:cut]), (mine[cut:], other[cut:]))
+        ]
+        for pair in zip(distances, swapped):
+            got = [exchange(v, d, nodes) for v, d in zip(values, pair)]
+            values = [v + g for v, g in zip(values, got)]
+        others = [exchange(v, 1, nodes) for v in values]
+        return jnp.concatenate(values), jnp.concatenate(others)
 
     acc_shape = pltpu.VMEM((total_rows * 8 + 8, width), f32)
     patch_shape = pltpu.VMEM((patches * 8 + 8, width), f32)

time: 56.8 us -> 52.4 us (0.923)
  waiting for transfers between devices: 34.7 us -> 19.7 us
  starting transfers between devices: 11.7 us -> 22 us
    ppermute x10 -> x20, waiting for transfers between devices: 34.7 us -> 19.7 us  [exchange(): lax.ppermute(value, 'node', [(i, i ^ distance) for i in range(nodes)])]
    ppermute x10 -> x20, starting transfers between devices: 11.7 us -> 22 us  [exchange(): lax.ppermute(value, 'node', [(i, i ^ distance) for i in range(nodes)])]
  transfers between devices with their start and end apart: 10 -> 20, of which waited for: 10 -> 15; matrix products, arithmetic and copies ran while one was open for 0% -> 0% of each run, Pallas kernels for 0% -> 0%
where the time goes in v4:
time: 52.4 us; the launch traced here: 52.1 us
  starting transfers between devices  22 us (42%)
  waiting for transfers between devices  19.7 us (38%)
  Pallas kernels  8.68 us (17%)
  between operations  1.47 us (3%)
    ppermute x20, starting transfers between devices, exchange(): lax.ppermute(value, 'node', [(i, i ^ distance) for i in range(nodes)])  22 us
    ppermute x20, waiting for transfers between devices, exchange(): lax.ppermute(value, 'node', [(i, i ^ distance) for i in range(nodes)])  19.7 us
    pallas_call x1, Pallas kernels, body(): pl.pallas_call(functools.partial(first_kernel, 0, slices), out_shape=(arr...  3.94 us
    pallas_call x1, Pallas kernels, body(): pl.pallas_call(functools.partial(middle_kernel, chain * slices, slices),...  2.99 us
    pallas_call x1, Pallas kernels, body(): pl.pallas_call(functools.partial(last_kernel, chain * slices, slices), ou...  1.74 us
  transfers between devices with their start and end apart: 20, of which 15 were waited for; matrix products, arithmetic and copies ran while one was open for 0% of the time, Pallas kernels for 0%

profile of v4, /device:TPU:0, one launch (start us, length us, event | category | flops | bytes accessed | tf_op | source)
XLA Modules:
  0.0 52.1 jit_solution(7838204316069376480)
XLA Ops:
  1.3 3.9 %first.1 = (f32[5,64,128]{2,1,0:T(8,128)S(1)}, f32[5,64,128]{2,1,0:T(8,128)S(1)}, f32[8,128]{1,0:T(8,128)S(1)}, bf16[96,256,128]{2,1,0:T(8,128)(2,1)S(1)}, s32[2,96]{1,0:T(2,128)S(4)}) custom-call(s32[96]{0:T(128)} %rows_hbm.1, s32[96]{0:T(128)} %patch_hbm.1, s32[1]{0:T(128)S(6)} %copy.9.count_hbm, s32[128]{0:T(128)} %map_hbm.1, f32[96,128,128]{2,1,0:T(8,128)} %blocks_ref.1, ...), custom_call_target="tpu_custom_call" | custom-call | tf_op jit(solution)/shard_map/first/pallas_call | solution.py:352
  5.3 0.5 %collective-permute-start.4 = (f32[3,64,128]{2,1,0:T(8,128)S(1)}, f32[3,64,128]{2,1,0:T(8,128)S(1)}, u32[]{:S(2)}, u32[]{:S(2)}) collective-permute-start(f32[3,64,128]{2,1,0:T(8,128)S(1)} %slice.27), channel_id=1, source_target_pairs={{0,1},{1,0},{2,3},{3,2},{4,5},{5,4},{6,7},{7,6},{8,9},{9,8},{10,11... | collective-permute-start | bytes 294920 | tf_op jit(solution)/shard_map/ppermute | solution.py:311
  5.9 0.9 %collective-permute-done.4 = f32[3,64,128]{2,1,0:T(8,128)S(1)} collective-permute-done((f32[3,64,128]{2,1,0:T(8,128)S(1)}, f32[3,64,128]{2,1,0:T(8,128)S(1)}, u32[]{:S(2)}, u32[]{:S(2)}) %collective-permute-start.4) | collective-permute-done | bytes 98336 | tf_op jit(solution)/shard_map/ppermute | solution.py:311
  6.8 3.0 %collective-permute-start.5 = (f32[3,64,128]{2,1,0:T(8,128)S(1)}, f32[3,64,128]{2,1,0:T(8,128)S(1)}, u32[]{:S(2)}, u32[]{:S(2)}) collective-permute-start(f32[3,64,128]{2,1,0:T(8,128)S(1)} %slice_add_fusion), channel_id=1, source_target_pairs={{0,4},{1,5},{2,6},{3,7},{4,0},{5,1},{6,2},{7,3},{8,12},{9,13},{10,... | collective-permute-start | bytes 294920 | tf_op jit(solution)/shard_map/ppermute | solution.py:311
  9.7 1.6 %collective-permute-start.1 = (f32[2,64,128]{2,1,0:T(8,128)S(1)}, f32[2,64,128]{2,1,0:T(8,128)S(1)}, u32[]{:S(2)}, u32[]{:S(2)}) collective-permute-start(f32[2,64,128]{2,1,0:T(8,128)S(1)} %slice_add_fusion.3), channel_id=1, source_target_pairs={{0,2},{1,3},{2,0},{3,1},{4,6},{5,7},{6,4},{7,5},{8,10},{9,11},{10,... | collective-permute-start | bytes 196616 | tf_op jit(solution)/shard_map/ppermute | solution.py:311
  11.4 1.5 %collective-permute-done.5 = f32[3,64,128]{2,1,0:T(8,128)S(1)} collective-permute-done((f32[3,64,128]{2,1,0:T(8,128)S(1)}, f32[3,64,128]{2,1,0:T(8,128)S(1)}, u32[]{:S(2)}, u32[]{:S(2)}) %collective-permute-start.5) | collective-permute-done | bytes 98336 | tf_op jit(solution)/shard_map/ppermute | solution.py:311
  12.8 1.8 %collective-permute-start.6 = (f32[3,64,128]{2,1,0:T(8,128)S(1)}, f32[3,64,128]{2,1,0:T(8,128)S(1)}, u32[]{:S(2)}, u32[]{:S(2)}) collective-permute-start(f32[3,64,128]{2,1,0:T(8,128)S(1)} %add.53), channel_id=1, source_target_pairs={{0,2},{1,3},{2,0},{3,1},{4,6},{5,7},{6,4},{7,5},{8,10},{9,11},{10,... | collective-permute-start | bytes 294920 | tf_op jit(solution)/shard_map/ppermute | solution.py:311
  14.6 1.7 %collective-permute-start.2 = (f32[2,64,128]{2,1,0:T(8,128)S(1)}, f32[2,64,128]{2,1,0:T(8,128)S(1)}, u32[]{:S(2)}, u32[]{:S(2)}) collective-permute-start(f32[2,64,128]{2,1,0:T(8,128)S(1)} %add.49), channel_id=1, source_target_pairs={{0,4},{1,5},{2,6},{3,7},{4,0},{5,1},{6,2},{7,3},{8,12},{9,13},{10,... | collective-permute-start | bytes 196616 | tf_op jit(solution)/shard_map/ppermute | solution.py:311
  16.3 1.2 %collective-permute-done.6 = f32[3,64,128]{2,1,0:T(8,128)S(1)} collective-permute-done((f32[3,64,128]{2,1,0:T(8,128)S(1)}, f32[3,64,128]{2,1,0:T(8,128)S(1)}, u32[]{:S(2)}, u32[]{:S(2)}) %collective-permute-start.6) | collective-permute-done | bytes 98336 | tf_op jit(solution)/shard_map/ppermute | solution.py:311
  17.5 2.9 %collective-permute-start.7 = (f32[3,64,128]{2,1,0:T(8,128)S(1)}, f32[3,64,128]{2,1,0:T(8,128)S(1)}, u32[]{:S(2)}, u32[]{:S(2)}) collective-permute-start(f32[3,64,128]{2,1,0:T(8,128)S(1)} %add.54), channel_id=1, source_target_pairs={{0,8},{1,9},{2,10},{3,11},{4,12},{5,13},{6,14},{7,15},{8,0},{9,1},... | collective-permute-start | bytes 294920 | tf_op jit(solution)/shard_map/ppermute | solution.py:311
  20.4 1.6 %collective-permute-start.3 = (f32[2,64,128]{2,1,0:T(8,128)S(1)}, f32[2,64,128]{2,1,0:T(8,128)S(1)}, u32[]{:S(2)}, u32[]{:S(2)}) collective-permute-start(f32[2,64,128]{2,1,0:T(8,128)S(1)} %add.50), channel_id=1, source_target_pairs={{0,8},{1,9},{2,10},{3,11},{4,12},{5,13},{6,14},{7,15},{8,0},{9,1},... | collective-permute-start | bytes 196616 | tf_op jit(solution)/shard_map/ppermute | solution.py:311
  22.1 4.8 %collective-permute-done.3 = f32[2,64,128]{2,1,0:T(8,128)S(1)} collective-permute-done((f32[2,64,128]{2,1,0:T(8,128)S(1)}, f32[2,64,128]{2,1,0:T(8,128)S(1)}, u32[]{:S(2)}, u32[]{:S(2)}) %collective-permute-start.3) | collective-permute-done | bytes 65568 | tf_op jit(solution)/shard_map/ppermute | solution.py:311
  27.0 0.5 %collective-permute-start.9 = (f32[3,64,128]{2,1,0:T(8,128)S(1)}, f32[3,64,128]{2,1,0:T(8,128)S(1)}, u32[]{:S(2)}, u32[]{:S(2)}) collective-permute-start(f32[3,64,128]{2,1,0:T(8,128)S(1)} %add.55), channel_id=1, source_target_pairs={{0,1},{1,0},{2,3},{3,2},{4,5},{5,4},{6,7},{7,6},{8,9},{9,8},{10,11... | collective-permute-start | bytes 294920 | tf_op jit(solution)/shard_map/ppermute | solution.py:311
  27.6 0.6 %collective-permute-done.8 = f32[2,64,128]{2,1,0:T(8,128)S(1)} collective-permute-done((f32[2,64,128]{2,1,0:T(8,128)S(1)}, f32[2,64,128]{2,1,0:T(8,128)S(1)}, u32[]{:S(2)}, u32[]{:S(2)}) %collective-permute-start.8) | collective-permute-done | bytes 65568 | tf_op jit(solution)/shard_map/ppermute | solution.py:311
  28.2 0.3 collective-permute-done.9
  28.6 3.0 %middle.1 = (f32[4,64,128]{2,1,0:T(8,128)S(1)}, f32[4,64,128]{2,1,0:T(8,128)S(1)}, f32[4,1024]{1,0:T(4,128)S(1)}, f32[128,128]{1,0:T(8,128)S(1)}) custom-call(s32[2,96]{1,0:T(2,128)S(4)} %get-tuple-element.11.index_ref, bf16[96,256,128]{2,1,0:T(8,128)(2,1)S(1)} %get-tuple-element.12.pair_ref, f32[5,64,128]{2,1,0:T(8,128)S(1)} %pad_maximum_fusion.mine_ref, ...), custom_call_target="tpu_custom_call" | custom-call | tf_op jit(solution)/shard_map/middle/pallas_call | solution.py:410
  31.6 0.4 collective-permute-start.10
  32.2 0.8 %collective-permute-done.10 = f32[2,64,128]{2,1,0:T(8,128)S(1)} collective-permute-done((f32[2,64,128]{2,1,0:T(8,128)S(1)}, f32[2,64,128]{2,1,0:T(8,128)S(1)}, u32[]{:S(2)}, u32[]{:S(2)}) %collective-permute-start.10) | collective-permute-done | bytes 65568 | tf_op jit(solution)/shard_map/ppermute | solution.py:311
  32.9 0.4 collective-permute-done.14
  33.3 0.7 %collective-permute-start.11 = (f32[2,64,128]{2,1,0:T(8,128)S(1)}, f32[2,64,128]{2,1,0:T(8,128)S(1)}, u32[]{:S(2)}, u32[]{:S(2)}) collective-permute-start(f32[2,64,128]{2,1,0:T(8,128)S(1)} %get-tuple-element.20), channel_id=1, source_target_pairs={{0,2},{1,3},{2,0},{3,1},{4,6},{5,7},{6,4},{7,5},{8,10},{9,11},{10,... | collective-permute-start | bytes 196616 | tf_op jit(solution)/shard_map/ppermute | solution.py:311
  33.9 1.3 %collective-permute-start.15 = (f32[2,64,128]{2,1,0:T(8,128)S(1)}, f32[2,64,128]{2,1,0:T(8,128)S(1)}, u32[]{:S(2)}, u32[]{:S(2)}) collective-permute-start(f32[2,64,128]{2,1,0:T(8,128)S(1)} %get-tuple-element.21), channel_id=1, source_target_pairs={{0,4},{1,5},{2,6},{3,7},{4,0},{5,1},{6,2},{7,3},{8,12},{9,13},{10,... | collective-permute-start | bytes 196616 | tf_op jit(solution)/shard_map/ppermute | solution.py:311
  35.2 2.4 %collective-permute-done.11 = f32[2,64,128]{2,1,0:T(8,128)S(1)} collective-permute-done((f32[2,64,128]{2,1,0:T(8,128)S(1)}, f32[2,64,128]{2,1,0:T(8,128)S(1)}, u32[]{:S(2)}, u32[]{:S(2)}) %collective-permute-start.11) | collective-permute-done | bytes 65568 | tf_op jit(solution)/shard_map/ppermute | solution.py:311
  37.6 0.4 collective-permute-start.12
  38.2 1.5 %collective-permute-start.16 = (f32[2,64,128]{2,1,0:T(8,128)S(1)}, f32[2,64,128]{2,1,0:T(8,128)S(1)}, u32[]{:S(2)}, u32[]{:S(2)}) collective-permute-start(f32[2,64,128]{2,1,0:T(8,128)S(1)} %add.61), channel_id=1, source_target_pairs={{0,2},{1,3},{2,0},{3,1},{4,6},{5,7},{6,4},{7,5},{8,10},{9,11},{10,... | collective-permute-start | bytes 196616 | tf_op jit(solution)/shard_map/ppermute | solution.py:311
  39.7 2.2 %collective-permute-done.12 = f32[2,64,128]{2,1,0:T(8,128)S(1)} collective-permute-done((f32[2,64,128]{2,1,0:T(8,128)S(1)}, f32[2,64,128]{2,1,0:T(8,128)S(1)}, u32[]{:S(2)}, u32[]{:S(2)}) %collective-permute-start.12) | collective-permute-done | bytes 65568 | tf_op jit(solution)/shard_map/ppermute | solution.py:311
  42.0 1.6 %collective-permute-start.13 = (f32[2,64,128]{2,1,0:T(8,128)S(1)}, f32[2,64,128]{2,1,0:T(8,128)S(1)}, u32[]{:S(2)}, u32[]{:S(2)}) collective-permute-start(f32[2,64,128]{2,1,0:T(8,128)S(1)} %add.58), channel_id=1, source_target_pairs={{0,8},{1,9},{2,10},{3,11},{4,12},{5,13},{6,14},{7,15},{8,0},{9,1},... | collective-permute-start | bytes 196616 | tf_op jit(solution)/shard_map/ppermute | solution.py:311
  43.6 2.1 %collective-permute-start.17 = (f32[2,64,128]{2,1,0:T(8,128)S(1)}, f32[2,64,128]{2,1,0:T(8,128)S(1)}, u32[]{:S(2)}, u32[]{:S(2)}) collective-permute-start(f32[2,64,128]{2,1,0:T(8,128)S(1)} %add.62), channel_id=1, source_target_pairs={{0,8},{1,9},{2,10},{3,11},{4,12},{5,13},{6,14},{7,15},{8,0},{9,1},... | collective-permute-start | bytes 196616 | tf_op jit(solution)/shard_map/ppermute | solution.py:311
  45.7 2.6 %collective-permute-done.13 = f32[2,64,128]{2,1,0:T(8,128)S(1)} collective-permute-done((f32[2,64,128]{2,1,0:T(8,128)S(1)}, f32[2,64,128]{2,1,0:T(8,128)S(1)}, u32[]{:S(2)}, u32[]{:S(2)}) %collective-permute-start.13) | collective-permute-done | bytes 65568 | tf_op jit(solution)/shard_map/ppermute | solution.py:311
  48.4 0.6 %collective-permute-done.17 = f32[2,64,128]{2,1,0:T(8,128)S(1)} collective-permute-done((f32[2,64,128]{2,1,0:T(8,128)S(1)}, f32[2,64,128]{2,1,0:T(8,128)S(1)}, u32[]{:S(2)}, u32[]{:S(2)}) %collective-permute-start.17) | collective-permute-done | bytes 65568 | tf_op jit(solution)/shard_map/ppermute | solution.py:311
  49.1 0.5 collective-permute-done.18
  49.7 0.7 %collective-permute-done.19 = f32[2,64,128]{2,1,0:T(8,128)S(1)} collective-permute-done((f32[2,64,128]{2,1,0:T(8,128)S(1)}, f32[2,64,128]{2,1,0:T(8,128)S(1)}, u32[]{:S(2)}, u32[]{:S(2)}) %collective-permute-start.19) | collective-permute-done | bytes 65568 | tf_op jit(solution)/shard_map/ppermute | solution.py:311
  50.4 1.7 %last.1 = (f32[4,1024]{1,0:T(4,128)}, f32[4,1024]{1,0:T(4,128)}) custom-call(s32[2,96]{1,0:T(2,128)S(4)} %get-tuple-element.11.index_ref, bf16[96,256,128]{2,1,0:T(8,128)(2,1)S(1)} %get-tuple-element.12.pair_ref, f32[4,64,128]{2,1,0:T(8,128)S(1)} %pad_maximum_fusion.2.mine_ref, f32[4,64,128]{2,1,0:T(8,128)S(1)} %pad_maximum_fusion.3.other_ref, ...), custom_call_target="tpu_custom_call" | custom-call | tf_op jit(solution)/shard_map/last/pallas_call | solution.py:431
  (37 shorter events, 0.9 us)
Async XLA Ops:
  0.6 27.9 %copy-start = (f32[4,1024]{1,0:T(4,128)S(1)}, f32[4,1024]{1,0:T(4,128)}, u32[]{:S(2)}) copy-start(f32[4,1024]{1,0:T(4,128)} %start_ref.1) | copy-start | bytes 49156
  0.6 27.9 %copy-start.1 = (f32[4,1024]{1,0:T(4,128)S(1)}, f32[4,1024]{1,0:T(4,128)}, u32[]{:S(2)}) copy-start(f32[4,1024]{1,0:T(4,128)} %sino_ref.1) | copy-start | bytes 49156
  5.3 1.5 %collective-permute-start.4 = (f32[3,64,128]{2,1,0:T(8,128)S(1)}, f32[3,64,128]{2,1,0:T(8,128)S(1)}, u32[]{:S(2)}, u32[]{:S(2)}) collective-permute-start(f32[3,64,128]{2,1,0:T(8,128)S(1)} %slice.27), channel_id=1, source_target_pairs={{0,1},{1,0},{2,3},{3,2},{4,5},{5,4},{6,7},{7,6},{8,9},{9,8},{10,11... | collective-permute-start | bytes 294920 | tf_op jit(solution)/shard_map/ppermute | solution.py:311
  5.8 3.9 %collective-permute-start = (f32[2,64,128]{2,1,0:T(8,128)S(1)}, f32[2,64,128]{2,1,0:T(8,128)S(1)}, u32[]{:S(2)}, u32[]{:S(2)}) collective-permute-start(f32[2,64,128]{2,1,0:T(8,128)S(1)} %slice.25), channel_id=1, source_target_pairs={{0,1},{1,0},{2,3},{3,2},{4,5},{5,4},{6,7},{7,6},{8,9},{9,8},{10,11... | collective-permute-start | bytes 196616 | tf_op jit(solution)/shard_map/ppermute | solution.py:311
  6.8 6.1 %collective-permute-start.5 = (f32[3,64,128]{2,1,0:T(8,128)S(1)}, f32[3,64,128]{2,1,0:T(8,128)S(1)}, u32[]{:S(2)}, u32[]{:S(2)}) collective-permute-start(f32[3,64,128]{2,1,0:T(8,128)S(1)} %slice_add_fusion), channel_id=1, source_target_pairs={{0,4},{1,5},{2,6},{3,7},{4,0},{5,1},{6,2},{7,3},{8,12},{9,13},{10,... | collective-permute-start | bytes 294920 | tf_op jit(solution)/shard_map/ppermute | solution.py:311
  9.7 4.9 %collective-permute-start.1 = (f32[2,64,128]{2,1,0:T(8,128)S(1)}, f32[2,64,128]{2,1,0:T(8,128)S(1)}, u32[]{:S(2)}, u32[]{:S(2)}) collective-permute-start(f32[2,64,128]{2,1,0:T(8,128)S(1)} %slice_add_fusion.3), channel_id=1, source_target_pairs={{0,2},{1,3},{2,0},{3,1},{4,6},{5,7},{6,4},{7,5},{8,10},{9,11},{10,... | collective-permute-start | bytes 196616 | tf_op jit(solution)/shard_map/ppermute | solution.py:311
  12.8 4.7 %collective-permute-start.6 = (f32[3,64,128]{2,1,0:T(8,128)S(1)}, f32[3,64,128]{2,1,0:T(8,128)S(1)}, u32[]{:S(2)}, u32[]{:S(2)}) collective-permute-start(f32[3,64,128]{2,1,0:T(8,128)S(1)} %add.53), channel_id=1, source_target_pairs={{0,2},{1,3},{2,0},{3,1},{4,6},{5,7},{6,4},{7,5},{8,10},{9,11},{10,... | collective-permute-start | bytes 294920 | tf_op jit(solution)/shard_map/ppermute | solution.py:311
  14.6 5.8 %collective-permute-start.2 = (f32[2,64,128]{2,1,0:T(8,128)S(1)}, f32[2,64,128]{2,1,0:T(8,128)S(1)}, u32[]{:S(2)}, u32[]{:S(2)}) collective-permute-start(f32[2,64,128]{2,1,0:T(8,128)S(1)} %add.49), channel_id=1, source_target_pairs={{0,4},{1,5},{2,6},{3,7},{4,0},{5,1},{6,2},{7,3},{8,12},{9,13},{10,... | collective-permute-start | bytes 196616 | tf_op jit(solution)/shard_map/ppermute | solution.py:311
  17.5 9.5 %collective-permute-start.7 = (f32[3,64,128]{2,1,0:T(8,128)S(1)}, f32[3,64,128]{2,1,0:T(8,128)S(1)}, u32[]{:S(2)}, u32[]{:S(2)}) collective-permute-start(f32[3,64,128]{2,1,0:T(8,128)S(1)} %add.54), channel_id=1, source_target_pairs={{0,8},{1,9},{2,10},{3,11},{4,12},{5,13},{6,14},{7,15},{8,0},{9,1},... | collective-permute-start | bytes 294920 | tf_op jit(solution)/shard_map/ppermute | solution.py:311
  20.4 6.5 %collective-permute-start.3 = (f32[2,64,128]{2,1,0:T(8,128)S(1)}, f32[2,64,128]{2,1,0:T(8,128)S(1)}, u32[]{:S(2)}, u32[]{:S(2)}) collective-permute-start(f32[2,64,128]{2,1,0:T(8,128)S(1)} %add.50), channel_id=1, source_target_pairs={{0,8},{1,9},{2,10},{3,11},{4,12},{5,13},{6,14},{7,15},{8,0},{9,1},... | collective-permute-start | bytes 196616 | tf_op jit(solution)/shard_map/ppermute | solution.py:311
  26.9 1.3 %collective-permute-start.8 = (f32[2,64,128]{2,1,0:T(8,128)S(1)}, f32[2,64,128]{2,1,0:T(8,128)S(1)}, u32[]{:S(2)}, u32[]{:S(2)}) collective-permute-start(f32[2,64,128]{2,1,0:T(8,128)S(1)} %add.51), channel_id=1, source_target_pairs={{0,1},{1,0},{2,3},{3,2},{4,5},{5,4},{6,7},{7,6},{8,9},{9,8},{10,11... | collective-permute-start | bytes 196616 | tf_op jit(solution)/shard_map/ppermute | solution.py:311
  27.0 1.5 %collective-permute-start.9 = (f32[3,64,128]{2,1,0:T(8,128)S(1)}, f32[3,64,128]{2,1,0:T(8,128)S(1)}, u32[]{:S(2)}, u32[]{:S(2)}) collective-permute-start(f32[3,64,128]{2,1,0:T(8,128)S(1)} %add.55), channel_id=1, source_target_pairs={{0,1},{1,0},{2,3},{3,2},{4,5},{5,4},{6,7},{7,6},{8,9},{9,8},{10,11... | collective-permute-start | bytes 294920 | tf_op jit(solution)/shard_map/ppermute | solution.py:311
  31.6 1.3 %collective-permute-start.10 = (f32[2,64,128]{2,1,0:T(8,128)S(1)}, f32[2,64,128]{2,1,0:T(8,128)S(1)}, u32[]{:S(2)}, u32[]{:S(2)}) collective-permute-start(f32[2,64,128]{2,1,0:T(8,128)S(1)} %get-tuple-element.22), channel_id=1, source_target_pairs={{0,1},{1,0},{2,3},{3,2},{4,5},{5,4},{6,7},{7,6},{8,9},{9,8},{10,11... | collective-permute-start | bytes 196616 | tf_op jit(solution)/shard_map/ppermute | solution.py:311
  32.0 1.3 %collective-permute-start.14 = (f32[2,64,128]{2,1,0:T(8,128)S(1)}, f32[2,64,128]{2,1,0:T(8,128)S(1)}, u32[]{:S(2)}, u32[]{:S(2)}) collective-permute-start(f32[2,64,128]{2,1,0:T(8,128)S(1)} %get-tuple-element.23), channel_id=1, source_target_pairs={{0,1},{1,0},{2,3},{3,2},{4,5},{5,4},{6,7},{7,6},{8,9},{9,8},{10,11... | collective-permute-start | bytes 196616 | tf_op jit(solution)/shard_map/ppermute | solution.py:311
  33.3 4.3 %collective-permute-start.11 = (f32[2,64,128]{2,1,0:T(8,128)S(1)}, f32[2,64,128]{2,1,0:T(8,128)S(1)}, u32[]{:S(2)}, u32[]{:S(2)}) collective-permute-start(f32[2,64,128]{2,1,0:T(8,128)S(1)} %get-tuple-element.20), channel_id=1, source_target_pairs={{0,2},{1,3},{2,0},{3,1},{4,6},{5,7},{6,4},{7,5},{8,10},{9,11},{10,... | collective-permute-start | bytes 196616 | tf_op jit(solution)/shard_map/ppermute | solution.py:311
  33.9 4.3 %collective-permute-start.15 = (f32[2,64,128]{2,1,0:T(8,128)S(1)}, f32[2,64,128]{2,1,0:T(8,128)S(1)}, u32[]{:S(2)}, u32[]{:S(2)}) collective-permute-start(f32[2,64,128]{2,1,0:T(8,128)S(1)} %get-tuple-element.21), channel_id=1, source_target_pairs={{0,4},{1,5},{2,6},{3,7},{4,0},{5,1},{6,2},{7,3},{8,12},{9,13},{10,... | collective-permute-start | bytes 196616 | tf_op jit(solution)/shard_map/ppermute | solution.py:311
  37.6 4.3 %collective-permute-start.12 = (f32[2,64,128]{2,1,0:T(8,128)S(1)}, f32[2,64,128]{2,1,0:T(8,128)S(1)}, u32[]{:S(2)}, u32[]{:S(2)}) collective-permute-start(f32[2,64,128]{2,1,0:T(8,128)S(1)} %add.57), channel_id=1, source_target_pairs={{0,4},{1,5},{2,6},{3,7},{4,0},{5,1},{6,2},{7,3},{8,12},{9,13},{10,... | collective-permute-start | bytes 196616 | tf_op jit(solution)/shard_map/ppermute | solution.py:311
  38.2 5.4 %collective-permute-start.16 = (f32[2,64,128]{2,1,0:T(8,128)S(1)}, f32[2,64,128]{2,1,0:T(8,128)S(1)}, u32[]{:S(2)}, u32[]{:S(2)}) collective-permute-start(f32[2,64,128]{2,1,0:T(8,128)S(1)} %add.61), channel_id=1, source_target_pairs={{0,2},{1,3},{2,0},{3,1},{4,6},{5,7},{6,4},{7,5},{8,10},{9,11},{10,... | collective-permute-start | bytes 196616 | tf_op jit(solution)/shard_map/ppermute | solution.py:311
  42.0 6.3 %collective-permute-start.13 = (f32[2,64,128]{2,1,0:T(8,128)S(1)}, f32[2,64,128]{2,1,0:T(8,128)S(1)}, u32[]{:S(2)}, u32[]{:S(2)}) collective-permute-start(f32[2,64,128]{2,1,0:T(8,128)S(1)} %add.58), channel_id=1, source_target_pairs={{0,8},{1,9},{2,10},{3,11},{4,12},{5,13},{6,14},{7,15},{8,0},{9,1},... | collective-permute-start | bytes 196616 | tf_op jit(solution)/shard_map/ppermute | solution.py:311
  43.6 5.4 %collective-permute-start.17 = (f32[2,64,128]{2,1,0:T(8,128)S(1)}, f32[2,64,128]{2,1,0:T(8,128)S(1)}, u32[]{:S(2)}, u32[]{:S(2)}) collective-permute-start(f32[2,64,128]{2,1,0:T(8,128)S(1)} %add.62), channel_id=1, source_target_pairs={{0,8},{1,9},{2,10},{3,11},{4,12},{5,13},{6,14},{7,15},{8,0},{9,1},... | collective-permute-start | bytes 196616 | tf_op jit(solution)/shard_map/ppermute | solution.py:311
  48.3 1.3 %collective-permute-start.18 = (f32[2,64,128]{2,1,0:T(8,128)S(1)}, f32[2,64,128]{2,1,0:T(8,128)S(1)}, u32[]{:S(2)}, u32[]{:S(2)}) collective-permute-start(f32[2,64,128]{2,1,0:T(8,128)S(1)} %add.59), channel_id=1, source_target_pairs={{0,1},{1,0},{2,3},{3,2},{4,5},{5,4},{6,7},{7,6},{8,9},{9,8},{10,11... | collective-permute-start | bytes 196616 | tf_op jit(solution)/shard_map/ppermute | solution.py:311
  49.0 1.3 %collective-permute-start.19 = (f32[2,64,128]{2,1,0:T(8,128)S(1)}, f32[2,64,128]{2,1,0:T(8,128)S(1)}, u32[]{:S(2)}, u32[]{:S(2)}) collective-permute-start(f32[2,64,128]{2,1,0:T(8,128)S(1)} %add.63), channel_id=1, source_target_pairs={{0,1},{1,0},{2,3},{3,2},{4,5},{5,4},{6,7},{7,6},{8,9},{9,8},{10,11... | collective-permute-start | bytes 196616 | tf_op jit(solution)/shard_map/ppermute | solution.py:311

commit v5 on v4

--- a/solution.py
+++ b/solution.py
@@ -8,6 +8,7 @@
 from jax.sharding import PartitionSpec as P
 
 CHUNKS = 4
+WAYS = 4
 CHAINS = 1
 
 relax_factor = 1.9
@@ -21,15 +22,7 @@
     return high, value - high
 
 
-def forward_term(lhs, pair):
-    both = lax.dot_general(
-        lhs.astype(bf16), pair, (((1,), (1,)), ((), ())), preferred_element_type=f32
-    )
-    width = both.shape[1] // 2
-    return both[:, :width] + both[:, width:]
-
-
-def backward_term(lhs, pair):
+def product(lhs, pair):
     lhs = lhs.astype(bf16)
     return jnp.dot(
         jnp.concatenate([lhs, lhs], axis=1), pair, preferred_element_type=f32
@@ -78,6 +71,7 @@
     other_ref,
     col_ref,
     pair_ref,
+    turned_ref,
     index_ref,
     rows_ref,
     patch_ref,
@@ -89,9 +83,9 @@
     lhs,
     acc,
     sums,
-    cols,
     sems,
     small_sems,
+    *cols,
 ):
     count_blocks, width, _ = blocks_ref.shape
     total_rows = map_ref.shape[0]
@@ -125,7 +119,8 @@
         copy(k).start()
     acc[...] = jnp.zeros_like(acc)
     sums[...] = jnp.zeros_like(sums)
-    cols[...] = jnp.zeros_like(cols)
+    for one in cols:
+        one[...] = jnp.zeros_like(one)
     lhs[...] = jnp.zeros_like(lhs)
     for one in small:
         one.wait()
@@ -149,11 +144,16 @@
             places.append(at8(position))
             block = stage[j]
             high = block.astype(bf16)
-            pair = jnp.concatenate([high, (block - high.astype(f32)).astype(bf16)], axis=0)
-            pair_ref[j] = pair
-            cols[at8(patch), :] += jnp.sum(block.reshape(width // 8, 8, width), axis=0)
+            low = block - high.astype(f32)
+            pair_ref[j, :width, :] = high
+            pair_ref[j, width:, :] = low.astype(bf16)
+            other = block.T
+            high = other.astype(bf16)
+            turned = jnp.concatenate([high, (other - high.astype(f32)).astype(bf16)], axis=0)
+            turned_ref[j] = turned
+            cols[j % WAYS][at8(patch), :] += jnp.sum(block.reshape(width // 8, 8, width), axis=0)
             terms.append(
-                forward_term(lhs[pl.ds(pl.multiple_of(patch * 16, 16), 16), :], pair)
+                product(lhs[pl.ds(pl.multiple_of(patch * 16, 16), 16), :], turned)
             )
         for place, term in zip(places, terms):
             acc[place, :] += term[:8]
@@ -163,7 +163,10 @@
     for ref, side in ((mine_ref, core), (other_ref, 1 - core)):
         ref[slices] = sums[pl.ds(side * half * 8, half, stride=8), :]
     for p in range(patches):
-        total = jnp.sum(cols[p * 8 : (p + 1) * 8, :], axis=0, keepdims=True)
+        total = cols[0][at8(p), :]
+        for one in cols[1:]:
+            total = total + one[at8(p), :]
+        total = jnp.sum(total, axis=0, keepdims=True)
         col_ref[p : p + 1, :] = relax_factor / (total + 1.0)
 
 
@@ -179,37 +182,29 @@
                 full[s, pl.ds(pl.multiple_of(side * half, 8), half), :] = value
 
 
+def patch_total(update, p, slices):
+    total = update[0][at8(p), :]
+    for one in update[1:]:
+        total = total + one[at8(p), :]
+    return total[:slices] + total[slices : 2 * slices]
+
+
 def backward(index_ref, pair_ref, lhs, update):
-    update[...] = jnp.zeros_like(update)
+    for one in update:
+        one[...] = jnp.zeros_like(one)
     terms = []
     for j in range(pair_ref.shape[0]):
-        terms.append(backward_term(lhs[at8(index_ref[0, j]), :], pair_ref[j]))
+        terms.append(product(lhs[at8(index_ref[0, j]), :], pair_ref[j]))
     for j, term in enumerate(terms):
-        update[at8(index_ref[1, j]), :] += term
-
-
-def forward(index_ref, pair_ref, lhs, acc):
+        update[j % WAYS][at8(index_ref[1, j]), :] += term
+
+
+def forward(index_ref, turned_ref, lhs, acc):
     terms = []
-    for j in range(pair_ref.shape[0]):
-        terms.append(forward_term(lhs[at8(index_ref[1, j]), :], pair_ref[j]))
+    for j in range(turned_ref.shape[0]):
+        terms.append(product(lhs[at8(index_ref[1, j]), :], turned_ref[j]))
     for j, term in enumerate(terms):
         acc[at8(index_ref[0, j]), :] += term
-
-
-def second_kernel(
-    lo, slices, index_ref, pair_ref, start_ref, sino_ref, mine_ref, other_ref, acc, image_lhs
-):
-    width = pair_ref.shape[2]
-    half = mine_ref.shape[1]
-    patches = start_ref.shape[1] // width
-    node = lax.axis_index("node")
-    image_lhs[...] = jnp.zeros_like(image_lhs)
-    for p in range(patches):
-        fill_lhs(image_lhs, p, 8, start_ref[lo : lo + slices, p * width : (p + 1) * width], slices)
-    acc[...] = jnp.zeros_like(acc)
-    minus_measured(acc, sino_ref, lo, slices, width, node)
-    forward(index_ref, pair_ref, image_lhs, acc)
-    write_halves(acc, slices, lax.rem(node, 2), half, mine_ref, other_ref)
 
 
 def middle_kernel(
@@ -217,6 +212,7 @@
     slices,
     index_ref,
     pair_ref,
+    turned_ref,
     mine_ref,
     other_ref,
     col_ref,
@@ -227,7 +223,8 @@
     given, rest = (rest[:1], rest[1:]) if lo else ((), rest)
     next_mine_ref, next_other_ref, image_ref = rest[:3]
     made, rest = (rest[3:4], rest[4:]) if not lo else ((), rest[3:])
-    lhs, update, acc, image_lhs = rest
+    lhs, acc, image_lhs = rest[:3]
+    update = rest[3:]
     width = pair_ref.shape[2]
     half = mine_ref.shape[1]
     patches = start_ref.shape[1] // width
@@ -250,7 +247,7 @@
     weigh(slices, mine_ref, other_ref, weight_of, lhs, None, core, half)
     backward(index_ref, pair_ref, lhs, update)
     for p in range(patches):
-        total = update[p * 8 : p * 8 + slices, :] + update[p * 8 + slices : p * 8 + 2 * slices, :]
+        total = patch_total(update, p, slices)
         value = (
             start_ref[lo : lo + slices, p * width : (p + 1) * width]
             + col_ref[p : p + 1, :] * total
@@ -259,7 +256,7 @@
         fill_lhs(image_lhs, p, 8, value, slices)
     acc[...] = jnp.zeros_like(acc)
     minus_measured(acc, sino_ref, lo, slices, width, node)
-    forward(index_ref, pair_ref, image_lhs, acc)
+    forward(index_ref, turned_ref, image_lhs, acc)
     write_halves(acc, slices, core, half, next_mine_ref, next_other_ref)
 
 
@@ -276,7 +273,8 @@
     *rest,
 ):
     earlier, rest = (rest[:2], rest[2:]) if lo else ((), rest)
-    image_ref, weighted_ref, lhs, full, update = rest
+    image_ref, weighted_ref, lhs, full = rest[:4]
+    update = rest[4:]
     width = pair_ref.shape[2]
     half = mine_ref.shape[1]
     patches = prior_ref.shape[1] // width
@@ -301,7 +299,7 @@
             ]
     backward(index_ref, pair_ref, lhs, update)
     for p in range(patches):
-        total = update[p * 8 : p * 8 + slices, :] + update[p * 8 + slices : p * 8 + 2 * slices, :]
+        total = patch_total(update, p, slices)
         image_ref[lo : lo + slices, p * width : (p + 1) * width] = (
             prior_ref[:, p * width : (p + 1) * width] + col_ref[p : p + 1, :] * total
         )
@@ -349,17 +347,18 @@
     acc_shape = pltpu.VMEM((total_rows * 8 + 8, width), f32)
     patch_shape = pltpu.VMEM((patches * 8 + 8, width), f32)
 
-    mine, other, col, pair, index = pl.pallas_call(
+    mine, other, col, pair, turned, index = pl.pallas_call(
         functools.partial(first_kernel, 0, slices),
         out_shape=(
             array(slices + 1, half, width),
             array(slices + 1, half, width),
             array(patches, width),
             pltpu.VMEM((count_blocks, 2 * width, width), bf16),
+            pltpu.VMEM((count_blocks, 2 * width, width), bf16),
             pltpu.SMEM((2, count_blocks), jnp.int32),
         ),
         in_specs=[hbm] * 2 + [pl.BlockSpec(memory_space=pl.ANY)] + [hbm] * 4,
-        out_specs=(vmem,) * 4 + (smem,),
+        out_specs=(vmem,) * 5 + (smem,),
         scratch_shapes=[
             pltpu.SMEM(block_row.shape, jnp.int32),
             pltpu.SMEM(block_patch.shape, jnp.int32),
@@ -371,10 +370,10 @@
             pltpu.VMEM((patches * 16 + 16, width), f32),
             acc_shape,
             acc_shape,
-            patch_shape,
             pltpu.SemaphoreType.DMA((CHUNKS,)),
             pltpu.SemaphoreType.DMA((6,)),
-        ],
+        ]
+        + [patch_shape] * WAYS,
         compiler_params=params,
         name="first",
     )(
@@ -391,18 +390,6 @@
         )
 
     terms = [(mine, other)]
-    for chain in range(1, CHAINS):
-        terms.append(
-            pl.pallas_call(
-                functools.partial(second_kernel, chain * slices, slices),
-                out_shape=(array(slices, half, width),) * 2,
-                in_specs=[smem] + [vmem] * 3,
-                out_specs=(vmem,) * 2,
-                scratch_shapes=[acc_shape, patch_shape],
-                compiler_params=small_params,
-                name="second",
-            )(*held(), start, sinogram)
-        )
     images = []
     weight = None
     for chain in range(CHAINS):
@@ -415,12 +402,16 @@
                 array(slices, pixels),
             )
             + (() if chain else (array(total_rows, width),)),
-            in_specs=[smem] + [vmem] * (6 + len(given)),
+            in_specs=[smem] + [vmem] * (7 + len(given)),
             out_specs=(vmem,) * (3 if chain else 4),
-            scratch_shapes=[acc_shape, patch_shape, acc_shape, patch_shape],
+            scratch_shapes=[acc_shape, acc_shape, patch_shape] + [patch_shape] * WAYS,
             compiler_params=small_params,
             name="middle",
-        )(*held(), *sum_over_nodes(*terms[chain]), col, start, sinogram, *given)
+        )(
+            *held(),
+            pltpu.with_memory_space_constraint(turned, pltpu.VMEM),
+            *sum_over_nodes(*terms[chain]),
+            col, start, sinogram, *given)
         terms[chain] = got[:2]
         images.append(got[2])
         if not chain:
@@ -436,8 +427,8 @@
             scratch_shapes=[
                 acc_shape,
                 pltpu.VMEM((slices, total_rows, width), f32),
-                patch_shape,
-            ],
+            ]
+            + [patch_shape] * WAYS,
             compiler_params=small_params,
             name="last",
         )(*held(), *sum_over_nodes(*terms[chain]), col, images[chain], weight, *results)

time: 52.4 us -> 51.6 us (0.985)
  starting transfers between devices: 22 us -> 21.2 us
  waiting for transfers between devices: 19.7 us -> 20.5 us
  Pallas kernels: 8.68 us -> 7.88 us
    pallas_call x1, Pallas kernels: 2.99 us -> 2.12 us  [body(): pl.pallas_call(functools.partial(middle_kernel, chain * slices, slices),...]
    ppermute x20, waiting for transfers between devices: 19.7 us -> 20.5 us  [exchange(): lax.ppermute(value, 'node', [(i, i ^ distance) for i in range(nodes)])]
    ppermute x20, starting transfers between devices: 22 us -> 21.2 us  [exchange(): lax.ppermute(value, 'node', [(i, i ^ distance) for i in range(nodes)])]
where the time goes in v5:
time: 51.6 us; the launch traced here: 51.4 us
  starting transfers between devices  21.2 us (41%)
  waiting for transfers between devices  20.5 us (40%)
  Pallas kernels  7.88 us (15%)
  between operations  1.48 us (3%)
    ppermute x20, starting transfers between devices, exchange(): lax.ppermute(value, 'node', [(i, i ^ distance) for i in range(nodes)])  21.2 us
    ppermute x20, waiting for transfers between devices, exchange(): lax.ppermute(value, 'node', [(i, i ^ distance) for i in range(nodes)])  20.5 us
    pallas_call x1, Pallas kernels, body(): pl.pallas_call(functools.partial(first_kernel, 0, slices), out_shape=(arr...  4.06 us
    pallas_call x1, Pallas kernels, body(): pl.pallas_call(functools.partial(middle_kernel, chain * slices, slices),...  2.12 us
    pallas_call x1, Pallas kernels, body(): pl.pallas_call(functools.partial(last_kernel, chain * slices, slices), ou...  1.7 us
  transfers between devices with their start and end apart: 20, of which 15 were waited for; matrix products, arithmetic and copies ran while one was open for 0% of the time, Pallas kernels for 0%

profile of v5, /device:TPU:0, one launch (start us, length us, event | category | flops | bytes accessed | tf_op | source)
XLA Modules:
  0.0 51.4 jit_solution(9045631204043557005)
XLA Ops:
  1.3 4.1 %first.1 = (f32[5,64,128]{2,1,0:T(8,128)S(1)}, f32[5,64,128]{2,1,0:T(8,128)S(1)}, f32[8,128]{1,0:T(8,128)S(1)}, bf16[96,256,128]{2,1,0:T(8,128)(2,1)S(1)}, bf16[...) custom-call(s32[96]{0:T(128)} %rows_hbm.1, s32[96]{0:T(128)} %patch_hbm.1, s32[1]{0:T(128)S(6)} %copy.9.count_hbm, ...), custom_call_target="tpu_custom_call" | custom-call | tf_op jit(solution)/shard_map/first/pallas_call | solution.py:350
  5.4 0.5 %collective-permute-start.4 = (f32[3,64,128]{2,1,0:T(8,128)S(1)}, f32[3,64,128]{2,1,0:T(8,128)S(1)}, u32[]{:S(2)}, u32[]{:S(2)}) collective-permute-start(f32[3,64,128]{2,1,0:T(8,128)S(1)} %slice.27), channel_id=1, source_target_pairs={{0,1},{1,0},{2,3},{3,2},{4,5},{5,4},{6,7},{7,6},{8,9},{9,8},{10,11... | collective-permute-start | bytes 294920 | tf_op jit(solution)/shard_map/ppermute | solution.py:309
  6.0 0.9 %collective-permute-done.4 = f32[3,64,128]{2,1,0:T(8,128)S(1)} collective-permute-done((f32[3,64,128]{2,1,0:T(8,128)S(1)}, f32[3,64,128]{2,1,0:T(8,128)S(1)}, u32[]{:S(2)}, u32[]{:S(2)}) %collective-permute-start.4) | collective-permute-done | bytes 98336 | tf_op jit(solution)/shard_map/ppermute | solution.py:309
  6.9 3.0 %collective-permute-start.5 = (f32[3,64,128]{2,1,0:T(8,128)S(1)}, f32[3,64,128]{2,1,0:T(8,128)S(1)}, u32[]{:S(2)}, u32[]{:S(2)}) collective-permute-start(f32[3,64,128]{2,1,0:T(8,128)S(1)} %slice_add_fusion), channel_id=1, source_target_pairs={{0,4},{1,5},{2,6},{3,7},{4,0},{5,1},{6,2},{7,3},{8,12},{9,13},{10,... | collective-permute-start | bytes 294920 | tf_op jit(solution)/shard_map/ppermute | solution.py:309
  9.9 1.6 %collective-permute-start.1 = (f32[2,64,128]{2,1,0:T(8,128)S(1)}, f32[2,64,128]{2,1,0:T(8,128)S(1)}, u32[]{:S(2)}, u32[]{:S(2)}) collective-permute-start(f32[2,64,128]{2,1,0:T(8,128)S(1)} %slice_add_fusion.3), channel_id=1, source_target_pairs={{0,2},{1,3},{2,0},{3,1},{4,6},{5,7},{6,4},{7,5},{8,10},{9,11},{10,... | collective-permute-start | bytes 196616 | tf_op jit(solution)/shard_map/ppermute | solution.py:309
  11.5 1.5 %collective-permute-done.5 = f32[3,64,128]{2,1,0:T(8,128)S(1)} collective-permute-done((f32[3,64,128]{2,1,0:T(8,128)S(1)}, f32[3,64,128]{2,1,0:T(8,128)S(1)}, u32[]{:S(2)}, u32[]{:S(2)}) %collective-permute-start.5) | collective-permute-done | bytes 98336 | tf_op jit(solution)/shard_map/ppermute | solution.py:309
  13.0 1.7 %collective-permute-start.6 = (f32[3,64,128]{2,1,0:T(8,128)S(1)}, f32[3,64,128]{2,1,0:T(8,128)S(1)}, u32[]{:S(2)}, u32[]{:S(2)}) collective-permute-start(f32[3,64,128]{2,1,0:T(8,128)S(1)} %add.53), channel_id=1, source_target_pairs={{0,2},{1,3},{2,0},{3,1},{4,6},{5,7},{6,4},{7,5},{8,10},{9,11},{10,... | collective-permute-start | bytes 294920 | tf_op jit(solution)/shard_map/ppermute | solution.py:309
  14.8 1.6 %collective-permute-start.2 = (f32[2,64,128]{2,1,0:T(8,128)S(1)}, f32[2,64,128]{2,1,0:T(8,128)S(1)}, u32[]{:S(2)}, u32[]{:S(2)}) collective-permute-start(f32[2,64,128]{2,1,0:T(8,128)S(1)} %add.49), channel_id=1, source_target_pairs={{0,4},{1,5},{2,6},{3,7},{4,0},{5,1},{6,2},{7,3},{8,12},{9,13},{10,... | collective-permute-start | bytes 196616 | tf_op jit(solution)/shard_map/ppermute | solution.py:309
  16.4 1.3 %collective-permute-done.6 = f32[3,64,128]{2,1,0:T(8,128)S(1)} collective-permute-done((f32[3,64,128]{2,1,0:T(8,128)S(1)}, f32[3,64,128]{2,1,0:T(8,128)S(1)}, u32[]{:S(2)}, u32[]{:S(2)}) %collective-permute-start.6) | collective-permute-done | bytes 98336 | tf_op jit(solution)/shard_map/ppermute | solution.py:309
  17.7 2.8 %collective-permute-start.7 = (f32[3,64,128]{2,1,0:T(8,128)S(1)}, f32[3,64,128]{2,1,0:T(8,128)S(1)}, u32[]{:S(2)}, u32[]{:S(2)}) collective-permute-start(f32[3,64,128]{2,1,0:T(8,128)S(1)} %add.54), channel_id=1, source_target_pairs={{0,8},{1,9},{2,10},{3,11},{4,12},{5,13},{6,14},{7,15},{8,0},{9,1},... | collective-permute-start | bytes 294920 | tf_op jit(solution)/shard_map/ppermute | solution.py:309
  20.5 1.7 %collective-permute-start.3 = (f32[2,64,128]{2,1,0:T(8,128)S(1)}, f32[2,64,128]{2,1,0:T(8,128)S(1)}, u32[]{:S(2)}, u32[]{:S(2)}) collective-permute-start(f32[2,64,128]{2,1,0:T(8,128)S(1)} %add.50), channel_id=1, source_target_pairs={{0,8},{1,9},{2,10},{3,11},{4,12},{5,13},{6,14},{7,15},{8,0},{9,1},... | collective-permute-start | bytes 196616 | tf_op jit(solution)/shard_map/ppermute | solution.py:309
  22.3 4.8 %collective-permute-done.3 = f32[2,64,128]{2,1,0:T(8,128)S(1)} collective-permute-done((f32[2,64,128]{2,1,0:T(8,128)S(1)}, f32[2,64,128]{2,1,0:T(8,128)S(1)}, u32[]{:S(2)}, u32[]{:S(2)}) %collective-permute-start.3) | collective-permute-done | bytes 65568 | tf_op jit(solution)/shard_map/ppermute | solution.py:309
  27.2 0.5 %collective-permute-start.9 = (f32[3,64,128]{2,1,0:T(8,128)S(1)}, f32[3,64,128]{2,1,0:T(8,128)S(1)}, u32[]{:S(2)}, u32[]{:S(2)}) collective-permute-start(f32[3,64,128]{2,1,0:T(8,128)S(1)} %add.55), channel_id=1, source_target_pairs={{0,1},{1,0},{2,3},{3,2},{4,5},{5,4},{6,7},{7,6},{8,9},{9,8},{10,11... | collective-permute-start | bytes 294920 | tf_op jit(solution)/shard_map/ppermute | solution.py:309
  27.8 0.6 %collective-permute-done.8 = f32[2,64,128]{2,1,0:T(8,128)S(1)} collective-permute-done((f32[2,64,128]{2,1,0:T(8,128)S(1)}, f32[2,64,128]{2,1,0:T(8,128)S(1)}, u32[]{:S(2)}, u32[]{:S(2)}) %collective-permute-start.8) | collective-permute-done | bytes 65568 | tf_op jit(solution)/shard_map/ppermute | solution.py:309
  28.7 2.1 %middle.1 = (f32[4,64,128]{2,1,0:T(8,128)S(1)}, f32[4,64,128]{2,1,0:T(8,128)S(1)}, f32[4,1024]{1,0:T(4,128)S(1)}, f32[128,128]{1,0:T(8,128)S(1)}) custom-call(s32[2,96]{1,0:T(2,128)S(4)} %get-tuple-element.12.index_ref, bf16[96,256,128]{2,1,0:T(8,128)(2,1)S(1)} %get-tuple-element.13.pair_ref, bf16[96,256,128]{2,1,0:T(8,128)(2,1)S(1)} %get-tuple-element.14.turned_ref, ...), custom_call_target="tpu_custom_call" | custom-call | tf_op jit(solution)/shard_map/middle/pallas_call | solution.py:397
  30.9 0.4 collective-permute-start.10
  31.5 0.8 %collective-permute-done.10 = f32[2,64,128]{2,1,0:T(8,128)S(1)} collective-permute-done((f32[2,64,128]{2,1,0:T(8,128)S(1)}, f32[2,64,128]{2,1,0:T(8,128)S(1)}, u32[]{:S(2)}, u32[]{:S(2)}) %collective-permute-start.10) | collective-permute-done | bytes 65568 | tf_op jit(solution)/shard_map/ppermute | solution.py:309
  32.2 0.4 collective-permute-done.14
  32.6 1.4 %collective-permute-start.11 = (f32[2,64,128]{2,1,0:T(8,128)S(1)}, f32[2,64,128]{2,1,0:T(8,128)S(1)}, u32[]{:S(2)}, u32[]{:S(2)}) collective-permute-start(f32[2,64,128]{2,1,0:T(8,128)S(1)} %get-tuple-element.22), channel_id=1, source_target_pairs={{0,2},{1,3},{2,0},{3,1},{4,6},{5,7},{6,4},{7,5},{8,10},{9,11},{10,... | collective-permute-start | bytes 196616 | tf_op jit(solution)/shard_map/ppermute | solution.py:309
  34.0 0.5 %collective-permute-start.15 = (f32[2,64,128]{2,1,0:T(8,128)S(1)}, f32[2,64,128]{2,1,0:T(8,128)S(1)}, u32[]{:S(2)}, u32[]{:S(2)}) collective-permute-start(f32[2,64,128]{2,1,0:T(8,128)S(1)} %get-tuple-element.23), channel_id=1, source_target_pairs={{0,4},{1,5},{2,6},{3,7},{4,0},{5,1},{6,2},{7,3},{8,12},{9,13},{10,... | collective-permute-start | bytes 196616 | tf_op jit(solution)/shard_map/ppermute | solution.py:309
  34.5 2.4 %collective-permute-done.11 = f32[2,64,128]{2,1,0:T(8,128)S(1)} collective-permute-done((f32[2,64,128]{2,1,0:T(8,128)S(1)}, f32[2,64,128]{2,1,0:T(8,128)S(1)}, u32[]{:S(2)}, u32[]{:S(2)}) %collective-permute-start.11) | collective-permute-done | bytes 65568 | tf_op jit(solution)/shard_map/ppermute | solution.py:309
  36.9 0.4 collective-permute-start.12
  37.4 0.9 %collective-permute-done.15 = f32[2,64,128]{2,1,0:T(8,128)S(1)} collective-permute-done((f32[2,64,128]{2,1,0:T(8,128)S(1)}, f32[2,64,128]{2,1,0:T(8,128)S(1)}, u32[]{:S(2)}, u32[]{:S(2)}) %collective-permute-start.15) | collective-permute-done | bytes 65568 | tf_op jit(solution)/shard_map/ppermute | solution.py:309
  38.3 0.8 %collective-permute-start.16 = (f32[2,64,128]{2,1,0:T(8,128)S(1)}, f32[2,64,128]{2,1,0:T(8,128)S(1)}, u32[]{:S(2)}, u32[]{:S(2)}) collective-permute-start(f32[2,64,128]{2,1,0:T(8,128)S(1)} %add.61), channel_id=1, source_target_pairs={{0,2},{1,3},{2,0},{3,1},{4,6},{5,7},{6,4},{7,5},{8,10},{9,11},{10,... | collective-permute-start | bytes 196616 | tf_op jit(solution)/shard_map/ppermute | solution.py:309
  39.0 2.2 %collective-permute-done.12 = f32[2,64,128]{2,1,0:T(8,128)S(1)} collective-permute-done((f32[2,64,128]{2,1,0:T(8,128)S(1)}, f32[2,64,128]{2,1,0:T(8,128)S(1)}, u32[]{:S(2)}, u32[]{:S(2)}) %collective-permute-start.12) | collective-permute-done | bytes 65568 | tf_op jit(solution)/shard_map/ppermute | solution.py:309
  41.3 1.6 %collective-permute-start.13 = (f32[2,64,128]{2,1,0:T(8,128)S(1)}, f32[2,64,128]{2,1,0:T(8,128)S(1)}, u32[]{:S(2)}, u32[]{:S(2)}) collective-permute-start(f32[2,64,128]{2,1,0:T(8,128)S(1)} %add.58), channel_id=1, source_target_pairs={{0,8},{1,9},{2,10},{3,11},{4,12},{5,13},{6,14},{7,15},{8,0},{9,1},... | collective-permute-start | bytes 196616 | tf_op jit(solution)/shard_map/ppermute | solution.py:309
  42.9 2.1 %collective-permute-start.17 = (f32[2,64,128]{2,1,0:T(8,128)S(1)}, f32[2,64,128]{2,1,0:T(8,128)S(1)}, u32[]{:S(2)}, u32[]{:S(2)}) collective-permute-start(f32[2,64,128]{2,1,0:T(8,128)S(1)} %add.62), channel_id=1, source_target_pairs={{0,8},{1,9},{2,10},{3,11},{4,12},{5,13},{6,14},{7,15},{8,0},{9,1},... | collective-permute-start | bytes 196616 | tf_op jit(solution)/shard_map/ppermute | solution.py:309
  45.0 2.6 %collective-permute-done.13 = f32[2,64,128]{2,1,0:T(8,128)S(1)} collective-permute-done((f32[2,64,128]{2,1,0:T(8,128)S(1)}, f32[2,64,128]{2,1,0:T(8,128)S(1)}, u32[]{:S(2)}, u32[]{:S(2)}) %collective-permute-start.13) | collective-permute-done | bytes 65568 | tf_op jit(solution)/shard_map/ppermute | solution.py:309
  47.7 0.6 %collective-permute-done.17 = f32[2,64,128]{2,1,0:T(8,128)S(1)} collective-permute-done((f32[2,64,128]{2,1,0:T(8,128)S(1)}, f32[2,64,128]{2,1,0:T(8,128)S(1)}, u32[]{:S(2)}, u32[]{:S(2)}) %collective-permute-start.17) | collective-permute-done | bytes 65568 | tf_op jit(solution)/shard_map/ppermute | solution.py:309
  48.4 0.5 %collective-permute-done.18 = f32[2,64,128]{2,1,0:T(8,128)S(1)} collective-permute-done((f32[2,64,128]{2,1,0:T(8,128)S(1)}, f32[2,64,128]{2,1,0:T(8,128)S(1)}, u32[]{:S(2)}, u32[]{:S(2)}) %collective-permute-start.18) | collective-permute-done | bytes 65568 | tf_op jit(solution)/shard_map/ppermute | solution.py:309
  49.0 0.7 %collective-permute-done.19 = f32[2,64,128]{2,1,0:T(8,128)S(1)} collective-permute-done((f32[2,64,128]{2,1,0:T(8,128)S(1)}, f32[2,64,128]{2,1,0:T(8,128)S(1)}, u32[]{:S(2)}, u32[]{:S(2)}) %collective-permute-start.19) | collective-permute-done | bytes 65568 | tf_op jit(solution)/shard_map/ppermute | solution.py:309
  49.7 1.7 %last.1 = (f32[4,1024]{1,0:T(4,128)}, f32[4,1024]{1,0:T(4,128)}) custom-call(s32[2,96]{1,0:T(2,128)S(4)} %get-tuple-element.12.index_ref, bf16[96,256,128]{2,1,0:T(8,128)(2,1)S(1)} %get-tuple-element.13.pair_ref, f32[4,64,128]{2,1,0:T(8,128)S(1)} %pad_maximum_fusion.2.mine_ref, f32[4,64,128]{2,1,0:T(8,128)S(1)} %pad_maximum_fusion.3.other_ref, ...), custom_call_target="tpu_custom_call" | custom-call | tf_op jit(solution)/shard_map/last/pallas_call | solution.py:422
  (37 shorter events, 1.0 us)
Async XLA Ops:
  0.6 28.1 %copy-start = (f32[4,1024]{1,0:T(4,128)S(1)}, f32[4,1024]{1,0:T(4,128)}, u32[]{:S(2)}) copy-start(f32[4,1024]{1,0:T(4,128)} %start_ref.1) | copy-start | bytes 49156
  0.6 28.1 %copy-start.1 = (f32[4,1024]{1,0:T(4,128)S(1)}, f32[4,1024]{1,0:T(4,128)}, u32[]{:S(2)}) copy-start(f32[4,1024]{1,0:T(4,128)} %sino_ref.1) | copy-start | bytes 49156
  5.4 1.5 %collective-permute-start.4 = (f32[3,64,128]{2,1,0:T(8,128)S(1)}, f32[3,64,128]{2,1,0:T(8,128)S(1)}, u32[]{:S(2)}, u32[]{:S(2)}) collective-permute-start(f32[3,64,128]{2,1,0:T(8,128)S(1)} %slice.27), channel_id=1, source_target_pairs={{0,1},{1,0},{2,3},{3,2},{4,5},{5,4},{6,7},{7,6},{8,9},{9,8},{10,11... | collective-permute-start | bytes 294920 | tf_op jit(solution)/shard_map/ppermute | solution.py:309
  5.9 4.0 %collective-permute-start = (f32[2,64,128]{2,1,0:T(8,128)S(1)}, f32[2,64,128]{2,1,0:T(8,128)S(1)}, u32[]{:S(2)}, u32[]{:S(2)}) collective-permute-start(f32[2,64,128]{2,1,0:T(8,128)S(1)} %slice.25), channel_id=1, source_target_pairs={{0,1},{1,0},{2,3},{3,2},{4,5},{5,4},{6,7},{7,6},{8,9},{9,8},{10,11... | collective-permute-start | bytes 196616 | tf_op jit(solution)/shard_map/ppermute | solution.py:309
  6.9 6.1 %collective-permute-start.5 = (f32[3,64,128]{2,1,0:T(8,128)S(1)}, f32[3,64,128]{2,1,0:T(8,128)S(1)}, u32[]{:S(2)}, u32[]{:S(2)}) collective-permute-start(f32[3,64,128]{2,1,0:T(8,128)S(1)} %slice_add_fusion), channel_id=1, source_target_pairs={{0,4},{1,5},{2,6},{3,7},{4,0},{5,1},{6,2},{7,3},{8,12},{9,13},{10,... | collective-permute-start | bytes 294920 | tf_op jit(solution)/shard_map/ppermute | solution.py:309
  9.9 4.8 %collective-permute-start.1 = (f32[2,64,128]{2,1,0:T(8,128)S(1)}, f32[2,64,128]{2,1,0:T(8,128)S(1)}, u32[]{:S(2)}, u32[]{:S(2)}) collective-permute-start(f32[2,64,128]{2,1,0:T(8,128)S(1)} %slice_add_fusion.3), channel_id=1, source_target_pairs={{0,2},{1,3},{2,0},{3,1},{4,6},{5,7},{6,4},{7,5},{8,10},{9,11},{10,... | collective-permute-start | bytes 196616 | tf_op jit(solution)/shard_map/ppermute | solution.py:309
  13.0 4.7 %collective-permute-start.6 = (f32[3,64,128]{2,1,0:T(8,128)S(1)}, f32[3,64,128]{2,1,0:T(8,128)S(1)}, u32[]{:S(2)}, u32[]{:S(2)}) collective-permute-start(f32[3,64,128]{2,1,0:T(8,128)S(1)} %add.53), channel_id=1, source_target_pairs={{0,2},{1,3},{2,0},{3,1},{4,6},{5,7},{6,4},{7,5},{8,10},{9,11},{10,... | collective-permute-start | bytes 294920 | tf_op jit(solution)/shard_map/ppermute | solution.py:309
  14.8 5.8 %collective-permute-start.2 = (f32[2,64,128]{2,1,0:T(8,128)S(1)}, f32[2,64,128]{2,1,0:T(8,128)S(1)}, u32[]{:S(2)}, u32[]{:S(2)}) collective-permute-start(f32[2,64,128]{2,1,0:T(8,128)S(1)} %add.49), channel_id=1, source_target_pairs={{0,4},{1,5},{2,6},{3,7},{4,0},{5,1},{6,2},{7,3},{8,12},{9,13},{10,... | collective-permute-start | bytes 196616 | tf_op jit(solution)/shard_map/ppermute | solution.py:309
  17.7 9.5 %collective-permute-start.7 = (f32[3,64,128]{2,1,0:T(8,128)S(1)}, f32[3,64,128]{2,1,0:T(8,128)S(1)}, u32[]{:S(2)}, u32[]{:S(2)}) collective-permute-start(f32[3,64,128]{2,1,0:T(8,128)S(1)} %add.54), channel_id=1, source_target_pairs={{0,8},{1,9},{2,10},{3,11},{4,12},{5,13},{6,14},{7,15},{8,0},{9,1},... | collective-permute-start | bytes 294920 | tf_op jit(solution)/shard_map/ppermute | solution.py:309
  20.5 6.6 %collective-permute-start.3 = (f32[2,64,128]{2,1,0:T(8,128)S(1)}, f32[2,64,128]{2,1,0:T(8,128)S(1)}, u32[]{:S(2)}, u32[]{:S(2)}) collective-permute-start(f32[2,64,128]{2,1,0:T(8,128)S(1)} %add.50), channel_id=1, source_target_pairs={{0,8},{1,9},{2,10},{3,11},{4,12},{5,13},{6,14},{7,15},{8,0},{9,1},... | collective-permute-start | bytes 196616 | tf_op jit(solution)/shard_map/ppermute | solution.py:309
  27.1 1.3 %collective-permute-start.8 = (f32[2,64,128]{2,1,0:T(8,128)S(1)}, f32[2,64,128]{2,1,0:T(8,128)S(1)}, u32[]{:S(2)}, u32[]{:S(2)}) collective-permute-start(f32[2,64,128]{2,1,0:T(8,128)S(1)} %add.51), channel_id=1, source_target_pairs={{0,1},{1,0},{2,3},{3,2},{4,5},{5,4},{6,7},{7,6},{8,9},{9,8},{10,11... | collective-permute-start | bytes 196616 | tf_op jit(solution)/shard_map/ppermute | solution.py:309
  27.2 1.5 %collective-permute-start.9 = (f32[3,64,128]{2,1,0:T(8,128)S(1)}, f32[3,64,128]{2,1,0:T(8,128)S(1)}, u32[]{:S(2)}, u32[]{:S(2)}) collective-permute-start(f32[3,64,128]{2,1,0:T(8,128)S(1)} %add.55), channel_id=1, source_target_pairs={{0,1},{1,0},{2,3},{3,2},{4,5},{5,4},{6,7},{7,6},{8,9},{9,8},{10,11... | collective-permute-start | bytes 294920 | tf_op jit(solution)/shard_map/ppermute | solution.py:309
  30.9 1.3 %collective-permute-start.10 = (f32[2,64,128]{2,1,0:T(8,128)S(1)}, f32[2,64,128]{2,1,0:T(8,128)S(1)}, u32[]{:S(2)}, u32[]{:S(2)}) collective-permute-start(f32[2,64,128]{2,1,0:T(8,128)S(1)} %get-tuple-element.24), channel_id=1, source_target_pairs={{0,1},{1,0},{2,3},{3,2},{4,5},{5,4},{6,7},{7,6},{8,9},{9,8},{10,11... | collective-permute-start | bytes 196616 | tf_op jit(solution)/shard_map/ppermute | solution.py:309
  31.3 1.3 %collective-permute-start.14 = (f32[2,64,128]{2,1,0:T(8,128)S(1)}, f32[2,64,128]{2,1,0:T(8,128)S(1)}, u32[]{:S(2)}, u32[]{:S(2)}) collective-permute-start(f32[2,64,128]{2,1,0:T(8,128)S(1)} %get-tuple-element.25), channel_id=1, source_target_pairs={{0,1},{1,0},{2,3},{3,2},{4,5},{5,4},{6,7},{7,6},{8,9},{9,8},{10,11... | collective-permute-start | bytes 196616 | tf_op jit(solution)/shard_map/ppermute | solution.py:309
  32.6 4.3 %collective-permute-start.11 = (f32[2,64,128]{2,1,0:T(8,128)S(1)}, f32[2,64,128]{2,1,0:T(8,128)S(1)}, u32[]{:S(2)}, u32[]{:S(2)}) collective-permute-start(f32[2,64,128]{2,1,0:T(8,128)S(1)} %get-tuple-element.22), channel_id=1, source_target_pairs={{0,2},{1,3},{2,0},{3,1},{4,6},{5,7},{6,4},{7,5},{8,10},{9,11},{10,... | collective-permute-start | bytes 196616 | tf_op jit(solution)/shard_map/ppermute | solution.py:309
  34.0 4.3 %collective-permute-start.15 = (f32[2,64,128]{2,1,0:T(8,128)S(1)}, f32[2,64,128]{2,1,0:T(8,128)S(1)}, u32[]{:S(2)}, u32[]{:S(2)}) collective-permute-start(f32[2,64,128]{2,1,0:T(8,128)S(1)} %get-tuple-element.23), channel_id=1, source_target_pairs={{0,4},{1,5},{2,6},{3,7},{4,0},{5,1},{6,2},{7,3},{8,12},{9,13},{10,... | collective-permute-start | bytes 196616 | tf_op jit(solution)/shard_map/ppermute | solution.py:309
  36.9 4.3 %collective-permute-start.12 = (f32[2,64,128]{2,1,0:T(8,128)S(1)}, f32[2,64,128]{2,1,0:T(8,128)S(1)}, u32[]{:S(2)}, u32[]{:S(2)}) collective-permute-start(f32[2,64,128]{2,1,0:T(8,128)S(1)} %add.57), channel_id=1, source_target_pairs={{0,4},{1,5},{2,6},{3,7},{4,0},{5,1},{6,2},{7,3},{8,12},{9,13},{10,... | collective-permute-start | bytes 196616 | tf_op jit(solution)/shard_map/ppermute | solution.py:309
  38.3 4.6 %collective-permute-start.16 = (f32[2,64,128]{2,1,0:T(8,128)S(1)}, f32[2,64,128]{2,1,0:T(8,128)S(1)}, u32[]{:S(2)}, u32[]{:S(2)}) collective-permute-start(f32[2,64,128]{2,1,0:T(8,128)S(1)} %add.61), channel_id=1, source_target_pairs={{0,2},{1,3},{2,0},{3,1},{4,6},{5,7},{6,4},{7,5},{8,10},{9,11},{10,... | collective-permute-start | bytes 196616 | tf_op jit(solution)/shard_map/ppermute | solution.py:309
  41.3 6.3 %collective-permute-start.13 = (f32[2,64,128]{2,1,0:T(8,128)S(1)}, f32[2,64,128]{2,1,0:T(8,128)S(1)}, u32[]{:S(2)}, u32[]{:S(2)}) collective-permute-start(f32[2,64,128]{2,1,0:T(8,128)S(1)} %add.58), channel_id=1, source_target_pairs={{0,8},{1,9},{2,10},{3,11},{4,12},{5,13},{6,14},{7,15},{8,0},{9,1},... | collective-permute-start | bytes 196616 | tf_op jit(solution)/shard_map/ppermute | solution.py:309
  42.9 5.4 %collective-permute-start.17 = (f32[2,64,128]{2,1,0:T(8,128)S(1)}, f32[2,64,128]{2,1,0:T(8,128)S(1)}, u32[]{:S(2)}, u32[]{:S(2)}) collective-permute-start(f32[2,64,128]{2,1,0:T(8,128)S(1)} %add.62), channel_id=1, source_target_pairs={{0,8},{1,9},{2,10},{3,11},{4,12},{5,13},{6,14},{7,15},{8,0},{9,1},... | collective-permute-start | bytes 196616 | tf_op jit(solution)/shard_map/ppermute | solution.py:309
  47.6 1.3 %collective-permute-start.18 = (f32[2,64,128]{2,1,0:T(8,128)S(1)}, f32[2,64,128]{2,1,0:T(8,128)S(1)}, u32[]{:S(2)}, u32[]{:S(2)}) collective-permute-start(f32[2,64,128]{2,1,0:T(8,128)S(1)} %add.59), channel_id=1, source_target_pairs={{0,1},{1,0},{2,3},{3,2},{4,5},{5,4},{6,7},{7,6},{8,9},{9,8},{10,11... | collective-permute-start | bytes 196616 | tf_op jit(solution)/shard_map/ppermute | solution.py:309
  48.3 1.3 %collective-permute-start.19 = (f32[2,64,128]{2,1,0:T(8,128)S(1)}, f32[2,64,128]{2,1,0:T(8,128)S(1)}, u32[]{:S(2)}, u32[]{:S(2)}) collective-permute-start(f32[2,64,128]{2,1,0:T(8,128)S(1)} %add.63), channel_id=1, source_target_pairs={{0,1},{1,0},{2,3},{3,2},{4,5},{5,4},{6,7},{7,6},{8,9},{9,8},{10,11... | collective-permute-start | bytes 196616 | tf_op jit(solution)/shard_map/ppermute | solution.py:309

commit v6 on v5

--- a/solution.py
+++ b/solution.py
@@ -7,7 +7,7 @@
 from jax.experimental.pallas import tpu as pltpu
 from jax.sharding import PartitionSpec as P
 
-CHUNKS = 4
+CHUNKS = 3
 WAYS = 4
 CHAINS = 1
 
@@ -69,8 +69,7 @@
     sino_hbm,
     mine_ref,
     other_ref,
-    col_ref,
-    pair_ref,
+    stage,
     turned_ref,
     index_ref,
     rows_ref,
@@ -79,13 +78,11 @@
     map_ref,
     start_ref,
     sino_ref,
-    stage,
     lhs,
     acc,
     sums,
     sems,
     small_sems,
-    *cols,
 ):
     count_blocks, width, _ = blocks_ref.shape
     total_rows = map_ref.shape[0]
@@ -119,8 +116,6 @@
         copy(k).start()
     acc[...] = jnp.zeros_like(acc)
     sums[...] = jnp.zeros_like(sums)
-    for one in cols:
-        one[...] = jnp.zeros_like(one)
     lhs[...] = jnp.zeros_like(lhs)
     for one in small:
         one.wait()
@@ -142,16 +137,10 @@
             index_ref[0, j] = position
             index_ref[1, j] = patch
             places.append(at8(position))
-            block = stage[j]
+            block = stage[j].T
             high = block.astype(bf16)
-            low = block - high.astype(f32)
-            pair_ref[j, :width, :] = high
-            pair_ref[j, width:, :] = low.astype(bf16)
-            other = block.T
-            high = other.astype(bf16)
-            turned = jnp.concatenate([high, (other - high.astype(f32)).astype(bf16)], axis=0)
+            turned = jnp.concatenate([high, (block - high.astype(f32)).astype(bf16)], axis=0)
             turned_ref[j] = turned
-            cols[j % WAYS][at8(patch), :] += jnp.sum(block.reshape(width // 8, 8, width), axis=0)
             terms.append(
                 product(lhs[pl.ds(pl.multiple_of(patch * 16, 16), 16), :], turned)
             )
@@ -162,6 +151,21 @@
     write_halves(acc, slices, core, half, mine_ref, other_ref)
     for ref, side in ((mine_ref, core), (other_ref, 1 - core)):
         ref[slices] = sums[pl.ds(side * half * 8, half, stride=8), :]
+
+
+def prepare_kernel(index_ref, stage, col_ref, pair_ref, *cols):
+    count_blocks, width, _ = stage.shape
+    patches = col_ref.shape[0]
+    for one in cols:
+        one[...] = jnp.zeros_like(one)
+    for j in range(count_blocks):
+        block = stage[j]
+        high = block.astype(bf16)
+        pair_ref[j, :width, :] = high
+        pair_ref[j, width:, :] = (block - high.astype(f32)).astype(bf16)
+        cols[j % WAYS][at8(index_ref[1, j]), :] += jnp.sum(
+            block.reshape(width // 8, 8, width), axis=0
+        )
     for p in range(patches):
         total = cols[0][at8(p), :]
         for one in cols[1:]:
@@ -333,7 +337,7 @@
     swapped = distances[1::-1] + distances[2:]
 
     def sum_over_nodes(mine, other):
-        cut = 2
+        cut = mine.shape[0] - 2
         values = [
             m + exchange(o, 1, nodes)
             for m, o in ((mine[:cut], other[:cut]), (mine[cut:], other[cut:]))
@@ -347,18 +351,17 @@
     acc_shape = pltpu.VMEM((total_rows * 8 + 8, width), f32)
     patch_shape = pltpu.VMEM((patches * 8 + 8, width), f32)
 
-    mine, other, col, pair, turned, index = pl.pallas_call(
+    mine, other, stage, turned, index = pl.pallas_call(
         functools.partial(first_kernel, 0, slices),
         out_shape=(
             array(slices + 1, half, width),
             array(slices + 1, half, width),
-            array(patches, width),
-            pltpu.VMEM((count_blocks, 2 * width, width), bf16),
+            pltpu.VMEM(blocks.shape, f32),
             pltpu.VMEM((count_blocks, 2 * width, width), bf16),
             pltpu.SMEM((2, count_blocks), jnp.int32),
         ),
         in_specs=[hbm] * 2 + [pl.BlockSpec(memory_space=pl.ANY)] + [hbm] * 4,
-        out_specs=(vmem,) * 5 + (smem,),
+        out_specs=(vmem,) * 4 + (smem,),
         scratch_shapes=[
             pltpu.SMEM(block_row.shape, jnp.int32),
             pltpu.SMEM(block_patch.shape, jnp.int32),
@@ -366,14 +369,12 @@
             pltpu.SMEM(row_map.shape, jnp.int32),
             pltpu.VMEM(start.shape, f32),
             pltpu.VMEM(sinogram.shape, f32),
-            pltpu.VMEM(blocks.shape, f32),
             pltpu.VMEM((patches * 16 + 16, width), f32),
             acc_shape,
             acc_shape,
             pltpu.SemaphoreType.DMA((CHUNKS,)),
             pltpu.SemaphoreType.DMA((6,)),
-        ]
-        + [patch_shape] * WAYS,
+        ],
         compiler_params=params,
         name="first",
     )(
@@ -381,6 +382,25 @@
         in_hbm(block_patch),
         block_count,
         *map(in_hbm, (row_map, blocks, start, sinogram)),
+    )
+
+    col, pair = pl.pallas_call(
+        prepare_kernel,
+        out_shape=(
+            array(patches, width),
+            pltpu.VMEM((count_blocks, 2 * width, width), bf16),
+        ),
+        in_specs=[smem, vmem],
+        out_specs=(vmem,) * 2,
+        scratch_shapes=[patch_shape] * WAYS,
+        compiler_params=pltpu.CompilerParams(vmem_limit_bytes=8 * 1024 * 1024),
+        cost_estimate=pl.CostEstimate(
+            flops=0, bytes_accessed=2 * blocks.size * 4, transcendentals=0
+        ),
+        name="prepare",
+    )(
+        pltpu.with_memory_space_constraint(index, pltpu.SMEM),
+        pltpu.with_memory_space_constraint(stage, pltpu.VMEM),
     )
 
     def held():

time: 51.6 us -> 51.5 us (level)
  waiting for transfers between devices: 20.5 us -> 19.4 us
  Pallas kernels: 7.88 us -> 8.82 us
    ppermute x20, waiting for transfers between devices: 20.5 us -> 19.4 us  [exchange(): lax.ppermute(value, 'node', [(i, i ^ distance) for i in range(nodes)])]
    pallas_call x0 -> x1, Pallas kernels: none -> 0.89 us  [body(): pl.pallas_call(prepare_kernel, out_shape=(array(patches, width), pltpu.VM...]
  transfers between devices with their start and end apart: 20 -> 20, of which waited for: 15 -> 15; matrix products, arithmetic and copies ran while one was open for 0% -> 0% of each run, Pallas kernels for 0% -> 2%
where the time goes in v6:
time: 51.5 us; the launch traced here: 51.4 us
  starting transfers between devices  21.5 us (42%)
  waiting for transfers between devices  19.4 us (38%)
  Pallas kernels  8.82 us (17%)
  between operations  1.46 us (3%)
    ppermute x20, starting transfers between devices, exchange(): lax.ppermute(value, 'node', [(i, i ^ distance) for i in range(nodes)])  21.5 us
    ppermute x20, waiting for transfers between devices, exchange(): lax.ppermute(value, 'node', [(i, i ^ distance) for i in range(nodes)])  19.4 us
    pallas_call x1, Pallas kernels, body(): pl.pallas_call(functools.partial(first_kernel, 0, slices), out_shape=(arr...  4.08 us
    pallas_call x1, Pallas kernels, body(): pl.pallas_call(functools.partial(middle_kernel, chain * slices, slices),...  2.15 us
    pallas_call x1, Pallas kernels, body(): pl.pallas_call(functools.partial(last_kernel, chain * slices, slices), ou...  1.69 us
  transfers between devices with their start and end apart: 20, of which 15 were waited for; matrix products, arithmetic and copies ran while one was open for 0% of the time, Pallas kernels for 2%

profile of v6, /device:TPU:0, one launch (start us, length us, event | category | flops | bytes accessed | tf_op | source)
XLA Modules:
  0.0 51.4 jit_solution(3879214468780535464)
XLA Ops:
  1.3 4.1 %first.1 = (f32[5,64,128]{2,1,0:T(8,128)S(1)}, f32[5,64,128]{2,1,0:T(8,128)S(1)}, f32[96,128,128]{2,1,0:T(8,128)S(1)}, bf16[96,256,128]{2,1,0:T(8,128)(2,1)S(1)}, s32[2,96]{1,0:T(2,128)S(4)}) custom-call(s32[96]{0:T(128)} %rows_hbm.1, s32[96]{0:T(128)} %patch_hbm.1, s32[1]{0:T(128)S(6)} %copy.9.count_hbm, s32[128]{0:T(128)} %map_hbm.1, ...), custom_call_target="tpu_custom_call" | custom-call | tf_op jit(solution)/shard_map/first/pallas_call | solution.py:354
  5.4 0.5 collective-permute-start
  6.0 0.9 %collective-permute-done = f32[3,64,128]{2,1,0:T(8,128)S(1)} collective-permute-done((f32[3,64,128]{2,1,0:T(8,128)S(1)}, f32[3,64,128]{2,1,0:T(8,128)S(1)}, u32[]{:S(2)}, u32[]{:S(2)}) %collective-permute-start) | collective-permute-done | bytes 98336 | tf_op jit(solution)/shard_map/ppermute | solution.py:313
  6.9 3.0 %collective-permute-start.1 = (f32[3,64,128]{2,1,0:T(8,128)S(1)}, f32[3,64,128]{2,1,0:T(8,128)S(1)}, u32[]{:S(2)}, u32[]{:S(2)}) collective-permute-start(f32[3,64,128]{2,1,0:T(8,128)S(1)} %slice_add_fusion), channel_id=1, source_target_pairs={{0,2},{1,3},{2,0},{3,1},{4,6},{5,7},{6,4},{7,5},{8,10},{9,11},{10,... | collective-permute-start | bytes 294920 | tf_op jit(solution)/shard_map/ppermute | solution.py:313
  9.8 1.6 %collective-permute-start.5 = (f32[2,64,128]{2,1,0:T(8,128)S(1)}, f32[2,64,128]{2,1,0:T(8,128)S(1)}, u32[]{:S(2)}, u32[]{:S(2)}) collective-permute-start(f32[2,64,128]{2,1,0:T(8,128)S(1)} %slice_add_fusion.3), channel_id=1, source_target_pairs={{0,4},{1,5},{2,6},{3,7},{4,0},{5,1},{6,2},{7,3},{8,12},{9,13},{10,... | collective-permute-start | bytes 196616 | tf_op jit(solution)/shard_map/ppermute | solution.py:313
  11.5 1.4 %collective-permute-done.1 = f32[3,64,128]{2,1,0:T(8,128)S(1)} collective-permute-done((f32[3,64,128]{2,1,0:T(8,128)S(1)}, f32[3,64,128]{2,1,0:T(8,128)S(1)}, u32[]{:S(2)}, u32[]{:S(2)}) %collective-permute-start.1) | collective-permute-done | bytes 98336 | tf_op jit(solution)/shard_map/ppermute | solution.py:313
  12.9 1.8 %collective-permute-start.2 = (f32[3,64,128]{2,1,0:T(8,128)S(1)}, f32[3,64,128]{2,1,0:T(8,128)S(1)}, u32[]{:S(2)}, u32[]{:S(2)}) collective-permute-start(f32[3,64,128]{2,1,0:T(8,128)S(1)} %add.49), channel_id=1, source_target_pairs={{0,4},{1,5},{2,6},{3,7},{4,0},{5,1},{6,2},{7,3},{8,12},{9,13},{10,... | collective-permute-start | bytes 294920 | tf_op jit(solution)/shard_map/ppermute | solution.py:313
  14.8 1.6 %collective-permute-start.6 = (f32[2,64,128]{2,1,0:T(8,128)S(1)}, f32[2,64,128]{2,1,0:T(8,128)S(1)}, u32[]{:S(2)}, u32[]{:S(2)}) collective-permute-start(f32[2,64,128]{2,1,0:T(8,128)S(1)} %add.53), channel_id=1, source_target_pairs={{0,2},{1,3},{2,0},{3,1},{4,6},{5,7},{6,4},{7,5},{8,10},{9,11},{10,... | collective-permute-start | bytes 196616 | tf_op jit(solution)/shard_map/ppermute | solution.py:313
  16.4 1.2 %collective-permute-done.2 = f32[3,64,128]{2,1,0:T(8,128)S(1)} collective-permute-done((f32[3,64,128]{2,1,0:T(8,128)S(1)}, f32[3,64,128]{2,1,0:T(8,128)S(1)}, u32[]{:S(2)}, u32[]{:S(2)}) %collective-permute-start.2) | collective-permute-done | bytes 98336 | tf_op jit(solution)/shard_map/ppermute | solution.py:313
  17.6 2.9 %collective-permute-start.3 = (f32[3,64,128]{2,1,0:T(8,128)S(1)}, f32[3,64,128]{2,1,0:T(8,128)S(1)}, u32[]{:S(2)}, u32[]{:S(2)}) collective-permute-start(f32[3,64,128]{2,1,0:T(8,128)S(1)} %add.50), channel_id=1, source_target_pairs={{0,8},{1,9},{2,10},{3,11},{4,12},{5,13},{6,14},{7,15},{8,0},{9,1},... | collective-permute-start | bytes 294920 | tf_op jit(solution)/shard_map/ppermute | solution.py:313
  20.5 1.3 %collective-permute-start.7 = (f32[2,64,128]{2,1,0:T(8,128)S(1)}, f32[2,64,128]{2,1,0:T(8,128)S(1)}, u32[]{:S(2)}, u32[]{:S(2)}) collective-permute-start(f32[2,64,128]{2,1,0:T(8,128)S(1)} %add.54), channel_id=1, source_target_pairs={{0,8},{1,9},{2,10},{3,11},{4,12},{5,13},{6,14},{7,15},{8,0},{9,1},... | collective-permute-start | bytes 196616 | tf_op jit(solution)/shard_map/ppermute | solution.py:313
  21.8 0.9 %prepare.1 = (f32[8,128]{1,0:T(8,128)S(1)}, bf16[96,256,128]{2,1,0:T(8,128)(2,1)S(1)}) custom-call(s32[2,96]{1,0:T(2,128)S(4)} %get-tuple-element.13.index_ref, f32[96,128,128]{2,1,0:T(8,128)S(1)} %get-tuple-element.14.stage), custom_call_target="tpu_custom_call" | custom-call | bytes 12582912 | tf_op jit(solution)/shard_map/prepare/pallas_call | solution.py:387
  22.7 4.2 %collective-permute-done.7 = f32[2,64,128]{2,1,0:T(8,128)S(1)} collective-permute-done((f32[2,64,128]{2,1,0:T(8,128)S(1)}, f32[2,64,128]{2,1,0:T(8,128)S(1)}, u32[]{:S(2)}, u32[]{:S(2)}) %collective-permute-start.7) | collective-permute-done | bytes 65568 | tf_op jit(solution)/shard_map/ppermute | solution.py:313
  27.0 0.5 %collective-permute-start.8 = (f32[3,64,128]{2,1,0:T(8,128)S(1)}, f32[3,64,128]{2,1,0:T(8,128)S(1)}, u32[]{:S(2)}, u32[]{:S(2)}) collective-permute-start(f32[3,64,128]{2,1,0:T(8,128)S(1)} %add.51), channel_id=1, source_target_pairs={{0,1},{1,0},{2,3},{3,2},{4,5},{5,4},{6,7},{7,6},{8,9},{9,8},{10,11... | collective-permute-start | bytes 294920 | tf_op jit(solution)/shard_map/ppermute | solution.py:313
  27.6 0.6 %collective-permute-done.9 = f32[2,64,128]{2,1,0:T(8,128)S(1)} collective-permute-done((f32[2,64,128]{2,1,0:T(8,128)S(1)}, f32[2,64,128]{2,1,0:T(8,128)S(1)}, u32[]{:S(2)}, u32[]{:S(2)}) %collective-permute-start.9) | collective-permute-done | bytes 65568 | tf_op jit(solution)/shard_map/ppermute | solution.py:313
  28.5 2.2 %middle.1 = (f32[4,64,128]{2,1,0:T(8,128)S(1)}, f32[4,64,128]{2,1,0:T(8,128)S(1)}, f32[4,1024]{1,0:T(4,128)S(1)}, f32[128,128]{1,0:T(8,128)S(1)}) custom-call(s32[2,96]{1,0:T(2,128)S(4)} %get-tuple-element.13.index_ref, bf16[96,256,128]{2,1,0:T(8,128)(2,1)S(1)} %get-tuple-element.15.pair_ref, bf16[96,256,128]{2,1,0:T(8,128)(2,1)S(1)} %get-tuple-element.16.turned_ref, ...), custom_call_target="tpu_custom_call" | custom-call | tf_op jit(solution)/shard_map/middle/pallas_call | solution.py:417
  30.7 0.4 collective-permute-start.10
  31.3 0.7 %collective-permute-done.10 = f32[2,64,128]{2,1,0:T(8,128)S(1)} collective-permute-done((f32[2,64,128]{2,1,0:T(8,128)S(1)}, f32[2,64,128]{2,1,0:T(8,128)S(1)}, u32[]{:S(2)}, u32[]{:S(2)}) %collective-permute-start.10) | collective-permute-done | bytes 65568 | tf_op jit(solution)/shard_map/ppermute | solution.py:313
  32.4 1.6 %collective-permute-start.11 = (f32[2,64,128]{2,1,0:T(8,128)S(1)}, f32[2,64,128]{2,1,0:T(8,128)S(1)}, u32[]{:S(2)}, u32[]{:S(2)}) collective-permute-start(f32[2,64,128]{2,1,0:T(8,128)S(1)} %get-tuple-element.24), channel_id=1, source_target_pairs={{0,2},{1,3},{2,0},{3,1},{4,6},{5,7},{6,4},{7,5},{8,10},{9,11},{10,... | collective-permute-start | bytes 196616 | tf_op jit(solution)/shard_map/ppermute | solution.py:313
  34.0 0.5 %collective-permute-start.15 = (f32[2,64,128]{2,1,0:T(8,128)S(1)}, f32[2,64,128]{2,1,0:T(8,128)S(1)}, u32[]{:S(2)}, u32[]{:S(2)}) collective-permute-start(f32[2,64,128]{2,1,0:T(8,128)S(1)} %get-tuple-element.25), channel_id=1, source_target_pairs={{0,4},{1,5},{2,6},{3,7},{4,0},{5,1},{6,2},{7,3},{8,12},{9,13},{10,... | collective-permute-start | bytes 196616 | tf_op jit(solution)/shard_map/ppermute | solution.py:313
  34.5 2.2 %collective-permute-done.11 = f32[2,64,128]{2,1,0:T(8,128)S(1)} collective-permute-done((f32[2,64,128]{2,1,0:T(8,128)S(1)}, f32[2,64,128]{2,1,0:T(8,128)S(1)}, u32[]{:S(2)}, u32[]{:S(2)}) %collective-permute-start.11) | collective-permute-done | bytes 65568 | tf_op jit(solution)/shard_map/ppermute | solution.py:313
  36.7 0.7 %collective-permute-start.12 = (f32[2,64,128]{2,1,0:T(8,128)S(1)}, f32[2,64,128]{2,1,0:T(8,128)S(1)}, u32[]{:S(2)}, u32[]{:S(2)}) collective-permute-start(f32[2,64,128]{2,1,0:T(8,128)S(1)} %add.57), channel_id=1, source_target_pairs={{0,4},{1,5},{2,6},{3,7},{4,0},{5,1},{6,2},{7,3},{8,12},{9,13},{10,... | collective-permute-start | bytes 196616 | tf_op jit(solution)/shard_map/ppermute | solution.py:313
  37.4 0.8 %collective-permute-done.15 = f32[2,64,128]{2,1,0:T(8,128)S(1)} collective-permute-done((f32[2,64,128]{2,1,0:T(8,128)S(1)}, f32[2,64,128]{2,1,0:T(8,128)S(1)}, u32[]{:S(2)}, u32[]{:S(2)}) %collective-permute-start.15) | collective-permute-done | bytes 65568 | tf_op jit(solution)/shard_map/ppermute | solution.py:313
  38.3 0.7 %collective-permute-start.16 = (f32[2,64,128]{2,1,0:T(8,128)S(1)}, f32[2,64,128]{2,1,0:T(8,128)S(1)}, u32[]{:S(2)}, u32[]{:S(2)}) collective-permute-start(f32[2,64,128]{2,1,0:T(8,128)S(1)} %add.61), channel_id=1, source_target_pairs={{0,2},{1,3},{2,0},{3,1},{4,6},{5,7},{6,4},{7,5},{8,10},{9,11},{10,... | collective-permute-start | bytes 196616 | tf_op jit(solution)/shard_map/ppermute | solution.py:313
  38.9 2.2 %collective-permute-done.12 = f32[2,64,128]{2,1,0:T(8,128)S(1)} collective-permute-done((f32[2,64,128]{2,1,0:T(8,128)S(1)}, f32[2,64,128]{2,1,0:T(8,128)S(1)}, u32[]{:S(2)}, u32[]{:S(2)}) %collective-permute-start.12) | collective-permute-done | bytes 65568 | tf_op jit(solution)/shard_map/ppermute | solution.py:313
  41.1 1.8 %collective-permute-start.13 = (f32[2,64,128]{2,1,0:T(8,128)S(1)}, f32[2,64,128]{2,1,0:T(8,128)S(1)}, u32[]{:S(2)}, u32[]{:S(2)}) collective-permute-start(f32[2,64,128]{2,1,0:T(8,128)S(1)} %add.58), channel_id=1, source_target_pairs={{0,8},{1,9},{2,10},{3,11},{4,12},{5,13},{6,14},{7,15},{8,0},{9,1},... | collective-permute-start | bytes 196616 | tf_op jit(solution)/shard_map/ppermute | solution.py:313
  42.9 2.1 %collective-permute-start.17 = (f32[2,64,128]{2,1,0:T(8,128)S(1)}, f32[2,64,128]{2,1,0:T(8,128)S(1)}, u32[]{:S(2)}, u32[]{:S(2)}) collective-permute-start(f32[2,64,128]{2,1,0:T(8,128)S(1)} %add.62), channel_id=1, source_target_pairs={{0,8},{1,9},{2,10},{3,11},{4,12},{5,13},{6,14},{7,15},{8,0},{9,1},... | collective-permute-start | bytes 196616 | tf_op jit(solution)/shard_map/ppermute | solution.py:313
  45.0 2.7 %collective-permute-done.13 = f32[2,64,128]{2,1,0:T(8,128)S(1)} collective-permute-done((f32[2,64,128]{2,1,0:T(8,128)S(1)}, f32[2,64,128]{2,1,0:T(8,128)S(1)}, u32[]{:S(2)}, u32[]{:S(2)}) %collective-permute-start.13) | collective-permute-done | bytes 65568 | tf_op jit(solution)/shard_map/ppermute | solution.py:313
  47.7 0.6 %collective-permute-done.17 = f32[2,64,128]{2,1,0:T(8,128)S(1)} collective-permute-done((f32[2,64,128]{2,1,0:T(8,128)S(1)}, f32[2,64,128]{2,1,0:T(8,128)S(1)}, u32[]{:S(2)}, u32[]{:S(2)}) %collective-permute-start.17) | collective-permute-done | bytes 65568 | tf_op jit(solution)/shard_map/ppermute | solution.py:313
  48.5 0.5 %collective-permute-done.18 = f32[2,64,128]{2,1,0:T(8,128)S(1)} collective-permute-done((f32[2,64,128]{2,1,0:T(8,128)S(1)}, f32[2,64,128]{2,1,0:T(8,128)S(1)}, u32[]{:S(2)}, u32[]{:S(2)}) %collective-permute-start.18) | collective-permute-done | bytes 65568 | tf_op jit(solution)/shard_map/ppermute | solution.py:313
  49.0 0.7 %collective-permute-done.19 = f32[2,64,128]{2,1,0:T(8,128)S(1)} collective-permute-done((f32[2,64,128]{2,1,0:T(8,128)S(1)}, f32[2,64,128]{2,1,0:T(8,128)S(1)}, u32[]{:S(2)}, u32[]{:S(2)}) %collective-permute-start.19) | collective-permute-done | bytes 65568 | tf_op jit(solution)/shard_map/ppermute | solution.py:313
  49.7 1.7 %last.1 = (f32[4,1024]{1,0:T(4,128)}, f32[4,1024]{1,0:T(4,128)}) custom-call(s32[2,96]{1,0:T(2,128)S(4)} %get-tuple-element.13.index_ref, bf16[96,256,128]{2,1,0:T(8,128)(2,1)S(1)} %get-tuple-element.15.pair_ref, f32[4,64,128]{2,1,0:T(8,128)S(1)} %pad_maximum_fusion.2.mine_ref, f32[4,64,128]{2,1,0:T(8,128)S(1)} %pad_maximum_fusion.3.other_ref, ...), custom_call_target="tpu_custom_call" | custom-call | tf_op jit(solution)/shard_map/last/pallas_call | solution.py:442
  (38 shorter events, 1.3 us)
Async XLA Ops:
  1.3 27.3 %copy-start = (f32[4,1024]{1,0:T(4,128)S(1)}, f32[4,1024]{1,0:T(4,128)}, u32[]{:S(2)}) copy-start(f32[4,1024]{1,0:T(4,128)} %start_ref.1) | copy-start | bytes 49156
  1.3 27.3 %copy-start.1 = (f32[4,1024]{1,0:T(4,128)S(1)}, f32[4,1024]{1,0:T(4,128)}, u32[]{:S(2)}) copy-start(f32[4,1024]{1,0:T(4,128)} %sino_ref.1) | copy-start | bytes 49156
  5.4 1.4 %collective-permute-start = (f32[3,64,128]{2,1,0:T(8,128)S(1)}, f32[3,64,128]{2,1,0:T(8,128)S(1)}, u32[]{:S(2)}, u32[]{:S(2)}) collective-permute-start(f32[3,64,128]{2,1,0:T(8,128)S(1)} %slice.25), channel_id=1, source_target_pairs={{0,1},{1,0},{2,3},{3,2},{4,5},{5,4},{6,7},{7,6},{8,9},{9,8},{10,11... | collective-permute-start | bytes 294920 | tf_op jit(solution)/shard_map/ppermute | solution.py:313
  5.9 3.9 %collective-permute-start.4 = (f32[2,64,128]{2,1,0:T(8,128)S(1)}, f32[2,64,128]{2,1,0:T(8,128)S(1)}, u32[]{:S(2)}, u32[]{:S(2)}) collective-permute-start(f32[2,64,128]{2,1,0:T(8,128)S(1)} %slice.27), channel_id=1, source_target_pairs={{0,1},{1,0},{2,3},{3,2},{4,5},{5,4},{6,7},{7,6},{8,9},{9,8},{10,11... | collective-permute-start | bytes 196616 | tf_op jit(solution)/shard_map/ppermute | solution.py:313
  6.9 6.1 %collective-permute-start.1 = (f32[3,64,128]{2,1,0:T(8,128)S(1)}, f32[3,64,128]{2,1,0:T(8,128)S(1)}, u32[]{:S(2)}, u32[]{:S(2)}) collective-permute-start(f32[3,64,128]{2,1,0:T(8,128)S(1)} %slice_add_fusion), channel_id=1, source_target_pairs={{0,2},{1,3},{2,0},{3,1},{4,6},{5,7},{6,4},{7,5},{8,10},{9,11},{10,... | collective-permute-start | bytes 294920 | tf_op jit(solution)/shard_map/ppermute | solution.py:313
  9.8 5.0 %collective-permute-start.5 = (f32[2,64,128]{2,1,0:T(8,128)S(1)}, f32[2,64,128]{2,1,0:T(8,128)S(1)}, u32[]{:S(2)}, u32[]{:S(2)}) collective-permute-start(f32[2,64,128]{2,1,0:T(8,128)S(1)} %slice_add_fusion.3), channel_id=1, source_target_pairs={{0,4},{1,5},{2,6},{3,7},{4,0},{5,1},{6,2},{7,3},{8,12},{9,13},{10,... | collective-permute-start | bytes 196616 | tf_op jit(solution)/shard_map/ppermute | solution.py:313
  12.9 4.7 %collective-permute-start.2 = (f32[3,64,128]{2,1,0:T(8,128)S(1)}, f32[3,64,128]{2,1,0:T(8,128)S(1)}, u32[]{:S(2)}, u32[]{:S(2)}) collective-permute-start(f32[3,64,128]{2,1,0:T(8,128)S(1)} %add.49), channel_id=1, source_target_pairs={{0,4},{1,5},{2,6},{3,7},{4,0},{5,1},{6,2},{7,3},{8,12},{9,13},{10,... | collective-permute-start | bytes 294920 | tf_op jit(solution)/shard_map/ppermute | solution.py:313
  14.8 5.7 %collective-permute-start.6 = (f32[2,64,128]{2,1,0:T(8,128)S(1)}, f32[2,64,128]{2,1,0:T(8,128)S(1)}, u32[]{:S(2)}, u32[]{:S(2)}) collective-permute-start(f32[2,64,128]{2,1,0:T(8,128)S(1)} %add.53), channel_id=1, source_target_pairs={{0,2},{1,3},{2,0},{3,1},{4,6},{5,7},{6,4},{7,5},{8,10},{9,11},{10,... | collective-permute-start | bytes 196616 | tf_op jit(solution)/shard_map/ppermute | solution.py:313
  17.6 9.3 %collective-permute-start.3 = (f32[3,64,128]{2,1,0:T(8,128)S(1)}, f32[3,64,128]{2,1,0:T(8,128)S(1)}, u32[]{:S(2)}, u32[]{:S(2)}) collective-permute-start(f32[3,64,128]{2,1,0:T(8,128)S(1)} %add.50), channel_id=1, source_target_pairs={{0,8},{1,9},{2,10},{3,11},{4,12},{5,13},{6,14},{7,15},{8,0},{9,1},... | collective-permute-start | bytes 294920 | tf_op jit(solution)/shard_map/ppermute | solution.py:313
  20.5 6.4 %collective-permute-start.7 = (f32[2,64,128]{2,1,0:T(8,128)S(1)}, f32[2,64,128]{2,1,0:T(8,128)S(1)}, u32[]{:S(2)}, u32[]{:S(2)}) collective-permute-start(f32[2,64,128]{2,1,0:T(8,128)S(1)} %add.54), channel_id=1, source_target_pairs={{0,8},{1,9},{2,10},{3,11},{4,12},{5,13},{6,14},{7,15},{8,0},{9,1},... | collective-permute-start | bytes 196616 | tf_op jit(solution)/shard_map/ppermute | solution.py:313
  26.9 1.3 %collective-permute-start.9 = (f32[2,64,128]{2,1,0:T(8,128)S(1)}, f32[2,64,128]{2,1,0:T(8,128)S(1)}, u32[]{:S(2)}, u32[]{:S(2)}) collective-permute-start(f32[2,64,128]{2,1,0:T(8,128)S(1)} %add.55), channel_id=1, source_target_pairs={{0,1},{1,0},{2,3},{3,2},{4,5},{5,4},{6,7},{7,6},{8,9},{9,8},{10,11... | collective-permute-start | bytes 196616 | tf_op jit(solution)/shard_map/ppermute | solution.py:313
  27.0 1.5 %collective-permute-start.8 = (f32[3,64,128]{2,1,0:T(8,128)S(1)}, f32[3,64,128]{2,1,0:T(8,128)S(1)}, u32[]{:S(2)}, u32[]{:S(2)}) collective-permute-start(f32[3,64,128]{2,1,0:T(8,128)S(1)} %add.51), channel_id=1, source_target_pairs={{0,1},{1,0},{2,3},{3,2},{4,5},{5,4},{6,7},{7,6},{8,9},{9,8},{10,11... | collective-permute-start | bytes 294920 | tf_op jit(solution)/shard_map/ppermute | solution.py:313
  30.7 1.3 %collective-permute-start.10 = (f32[2,64,128]{2,1,0:T(8,128)S(1)}, f32[2,64,128]{2,1,0:T(8,128)S(1)}, u32[]{:S(2)}, u32[]{:S(2)}) collective-permute-start(f32[2,64,128]{2,1,0:T(8,128)S(1)} %get-tuple-element.26), channel_id=1, source_target_pairs={{0,1},{1,0},{2,3},{3,2},{4,5},{5,4},{6,7},{7,6},{8,9},{9,8},{10,11... | collective-permute-start | bytes 196616 | tf_op jit(solution)/shard_map/ppermute | solution.py:313
  31.1 1.3 %collective-permute-start.14 = (f32[2,64,128]{2,1,0:T(8,128)S(1)}, f32[2,64,128]{2,1,0:T(8,128)S(1)}, u32[]{:S(2)}, u32[]{:S(2)}) collective-permute-start(f32[2,64,128]{2,1,0:T(8,128)S(1)} %get-tuple-element.27), channel_id=1, source_target_pairs={{0,1},{1,0},{2,3},{3,2},{4,5},{5,4},{6,7},{7,6},{8,9},{9,8},{10,11... | collective-permute-start | bytes 196616 | tf_op jit(solution)/shard_map/ppermute | solution.py:313
  32.4 4.3 %collective-permute-start.11 = (f32[2,64,128]{2,1,0:T(8,128)S(1)}, f32[2,64,128]{2,1,0:T(8,128)S(1)}, u32[]{:S(2)}, u32[]{:S(2)}) collective-permute-start(f32[2,64,128]{2,1,0:T(8,128)S(1)} %get-tuple-element.24), channel_id=1, source_target_pairs={{0,2},{1,3},{2,0},{3,1},{4,6},{5,7},{6,4},{7,5},{8,10},{9,11},{10,... | collective-permute-start | bytes 196616 | tf_op jit(solution)/shard_map/ppermute | solution.py:313
  34.0 4.3 %collective-permute-start.15 = (f32[2,64,128]{2,1,0:T(8,128)S(1)}, f32[2,64,128]{2,1,0:T(8,128)S(1)}, u32[]{:S(2)}, u32[]{:S(2)}) collective-permute-start(f32[2,64,128]{2,1,0:T(8,128)S(1)} %get-tuple-element.25), channel_id=1, source_target_pairs={{0,4},{1,5},{2,6},{3,7},{4,0},{5,1},{6,2},{7,3},{8,12},{9,13},{10,... | collective-permute-start | bytes 196616 | tf_op jit(solution)/shard_map/ppermute | solution.py:313
  36.7 4.3 %collective-permute-start.12 = (f32[2,64,128]{2,1,0:T(8,128)S(1)}, f32[2,64,128]{2,1,0:T(8,128)S(1)}, u32[]{:S(2)}, u32[]{:S(2)}) collective-permute-start(f32[2,64,128]{2,1,0:T(8,128)S(1)} %add.57), channel_id=1, source_target_pairs={{0,4},{1,5},{2,6},{3,7},{4,0},{5,1},{6,2},{7,3},{8,12},{9,13},{10,... | collective-permute-start | bytes 196616 | tf_op jit(solution)/shard_map/ppermute | solution.py:313
  38.3 4.6 %collective-permute-start.16 = (f32[2,64,128]{2,1,0:T(8,128)S(1)}, f32[2,64,128]{2,1,0:T(8,128)S(1)}, u32[]{:S(2)}, u32[]{:S(2)}) collective-permute-start(f32[2,64,128]{2,1,0:T(8,128)S(1)} %add.61), channel_id=1, source_target_pairs={{0,2},{1,3},{2,0},{3,1},{4,6},{5,7},{6,4},{7,5},{8,10},{9,11},{10,... | collective-permute-start | bytes 196616 | tf_op jit(solution)/shard_map/ppermute | solution.py:313
  41.1 6.6 %collective-permute-start.13 = (f32[2,64,128]{2,1,0:T(8,128)S(1)}, f32[2,64,128]{2,1,0:T(8,128)S(1)}, u32[]{:S(2)}, u32[]{:S(2)}) collective-permute-start(f32[2,64,128]{2,1,0:T(8,128)S(1)} %add.58), channel_id=1, source_target_pairs={{0,8},{1,9},{2,10},{3,11},{4,12},{5,13},{6,14},{7,15},{8,0},{9,1},... | collective-permute-start | bytes 196616 | tf_op jit(solution)/shard_map/ppermute | solution.py:313
  42.9 5.4 %collective-permute-start.17 = (f32[2,64,128]{2,1,0:T(8,128)S(1)}, f32[2,64,128]{2,1,0:T(8,128)S(1)}, u32[]{:S(2)}, u32[]{:S(2)}) collective-permute-start(f32[2,64,128]{2,1,0:T(8,128)S(1)} %add.62), channel_id=1, source_target_pairs={{0,8},{1,9},{2,10},{3,11},{4,12},{5,13},{6,14},{7,15},{8,0},{9,1},... | collective-permute-start | bytes 196616 | tf_op jit(solution)/shard_map/ppermute | solution.py:313
  47.7 1.3 %collective-permute-start.18 = (f32[2,64,128]{2,1,0:T(8,128)S(1)}, f32[2,64,128]{2,1,0:T(8,128)S(1)}, u32[]{:S(2)}, u32[]{:S(2)}) collective-permute-start(f32[2,64,128]{2,1,0:T(8,128)S(1)} %add.59), channel_id=1, source_target_pairs={{0,1},{1,0},{2,3},{3,2},{4,5},{5,4},{6,7},{7,6},{8,9},{9,8},{10,11... | collective-permute-start | bytes 196616 | tf_op jit(solution)/shard_map/ppermute | solution.py:313
  48.4 1.3 %collective-permute-start.19 = (f32[2,64,128]{2,1,0:T(8,128)S(1)}, f32[2,64,128]{2,1,0:T(8,128)S(1)}, u32[]{:S(2)}, u32[]{:S(2)}) collective-permute-start(f32[2,64,128]{2,1,0:T(8,128)S(1)} %add.63), channel_id=1, source_target_pairs={{0,1},{1,0},{2,3},{3,2},{4,5},{5,4},{6,7},{7,6},{8,9},{9,8},{10,11... | collective-permute-start | bytes 196616 | tf_op jit(solution)/shard_map/ppermute | solution.py:313

commit v7 on v5

--- a/solution.py
+++ b/solution.py
@@ -333,7 +333,7 @@
     swapped = distances[1::-1] + distances[2:]
 
     def sum_over_nodes(mine, other):
-        cut = 2
+        cut = mine.shape[0] - 2
         values = [
             m + exchange(o, 1, nodes)
             for m, o in ((mine[:cut], other[:cut]), (mine[cut:], other[cut:]))

time: 51.6 us -> 51.6 us (level)
  no operation moved by 1% of the time
where the time goes in v7:
time: 51.6 us; the launch traced here: 51.4 us
  starting transfers between devices  21.4 us (41%)
  waiting for transfers between devices  20.3 us (39%)
  Pallas kernels  7.89 us (15%)
  between operations  1.48 us (3%)
    ppermute x20, starting transfers between devices, exchange(): lax.ppermute(value, 'node', [(i, i ^ distance) for i in range(nodes)])  21.4 us
    ppermute x20, waiting for transfers between devices, exchange(): lax.ppermute(value, 'node', [(i, i ^ distance) for i in range(nodes)])  20.3 us
    pallas_call x1, Pallas kernels, body(): pl.pallas_call(functools.partial(first_kernel, 0, slices), out_shape=(arr...  4.06 us
    pallas_call x1, Pallas kernels, body(): pl.pallas_call(functools.partial(middle_kernel, chain * slices, slices),...  2.13 us
    pallas_call x1, Pallas kernels, body(): pl.pallas_call(functools.partial(last_kernel, chain * slices, slices), ou...  1.69 us
  transfers between devices with their start and end apart: 20, of which 15 were waited for; matrix products, arithmetic and copies ran while one was open for 0% of the time, Pallas kernels for 0%

profile of v7, /device:TPU:0, one launch (start us, length us, event | category | flops | bytes accessed | tf_op | source)
XLA Modules:
  0.0 51.4 jit_solution(12105534917693191574)
XLA Ops:
  1.3 4.1 %first.1 = (f32[5,64,128]{2,1,0:T(8,128)S(1)}, f32[5,64,128]{2,1,0:T(8,128)S(1)}, f32[8,128]{1,0:T(8,128)S(1)}, bf16[96,256,128]{2,1,0:T(8,128)(2,1)S(1)}, bf16[...) custom-call(s32[96]{0:T(128)} %rows_hbm.1, s32[96]{0:T(128)} %patch_hbm.1, s32[1]{0:T(128)S(6)} %copy.9.count_hbm, ...), custom_call_target="tpu_custom_call" | custom-call | tf_op jit(solution)/shard_map/first/pallas_call | solution.py:350
  5.4 0.5 %collective-permute-start = (f32[3,64,128]{2,1,0:T(8,128)S(1)}, f32[3,64,128]{2,1,0:T(8,128)S(1)}, u32[]{:S(2)}, u32[]{:S(2)}) collective-permute-start(f32[3,64,128]{2,1,0:T(8,128)S(1)} %slice.25), channel_id=1, source_target_pairs={{0,1},{1,0},{2,3},{3,2},{4,5},{5,4},{6,7},{7,6},{8,9},{9,8},{10,11... | collective-permute-start | bytes 294920 | tf_op jit(solution)/shard_map/ppermute | solution.py:309
  6.0 0.9 %collective-permute-done = f32[3,64,128]{2,1,0:T(8,128)S(1)} collective-permute-done((f32[3,64,128]{2,1,0:T(8,128)S(1)}, f32[3,64,128]{2,1,0:T(8,128)S(1)}, u32[]{:S(2)}, u32[]{:S(2)}) %collective-permute-start) | collective-permute-done | bytes 98336 | tf_op jit(solution)/shard_map/ppermute | solution.py:309
  6.9 2.9 %collective-permute-start.1 = (f32[3,64,128]{2,1,0:T(8,128)S(1)}, f32[3,64,128]{2,1,0:T(8,128)S(1)}, u32[]{:S(2)}, u32[]{:S(2)}) collective-permute-start(f32[3,64,128]{2,1,0:T(8,128)S(1)} %slice_add_fusion), channel_id=1, source_target_pairs={{0,2},{1,3},{2,0},{3,1},{4,6},{5,7},{6,4},{7,5},{8,10},{9,11},{10,... | collective-permute-start | bytes 294920 | tf_op jit(solution)/shard_map/ppermute | solution.py:309
  9.8 1.6 %collective-permute-start.5 = (f32[2,64,128]{2,1,0:T(8,128)S(1)}, f32[2,64,128]{2,1,0:T(8,128)S(1)}, u32[]{:S(2)}, u32[]{:S(2)}) collective-permute-start(f32[2,64,128]{2,1,0:T(8,128)S(1)} %slice_add_fusion.3), channel_id=1, source_target_pairs={{0,4},{1,5},{2,6},{3,7},{4,0},{5,1},{6,2},{7,3},{8,12},{9,13},{10,... | collective-permute-start | bytes 196616 | tf_op jit(solution)/shard_map/ppermute | solution.py:309
  11.5 1.5 %collective-permute-done.1 = f32[3,64,128]{2,1,0:T(8,128)S(1)} collective-permute-done((f32[3,64,128]{2,1,0:T(8,128)S(1)}, f32[3,64,128]{2,1,0:T(8,128)S(1)}, u32[]{:S(2)}, u32[]{:S(2)}) %collective-permute-start.1) | collective-permute-done | bytes 98336 | tf_op jit(solution)/shard_map/ppermute | solution.py:309
  12.9 1.9 %collective-permute-start.2 = (f32[3,64,128]{2,1,0:T(8,128)S(1)}, f32[3,64,128]{2,1,0:T(8,128)S(1)}, u32[]{:S(2)}, u32[]{:S(2)}) collective-permute-start(f32[3,64,128]{2,1,0:T(8,128)S(1)} %add.49), channel_id=1, source_target_pairs={{0,4},{1,5},{2,6},{3,7},{4,0},{5,1},{6,2},{7,3},{8,12},{9,13},{10,... | collective-permute-start | bytes 294920 | tf_op jit(solution)/shard_map/ppermute | solution.py:309
  14.8 1.6 %collective-permute-start.6 = (f32[2,64,128]{2,1,0:T(8,128)S(1)}, f32[2,64,128]{2,1,0:T(8,128)S(1)}, u32[]{:S(2)}, u32[]{:S(2)}) collective-permute-start(f32[2,64,128]{2,1,0:T(8,128)S(1)} %add.53), channel_id=1, source_target_pairs={{0,2},{1,3},{2,0},{3,1},{4,6},{5,7},{6,4},{7,5},{8,10},{9,11},{10,... | collective-permute-start | bytes 196616 | tf_op jit(solution)/shard_map/ppermute | solution.py:309
  16.4 1.2 %collective-permute-done.2 = f32[3,64,128]{2,1,0:T(8,128)S(1)} collective-permute-done((f32[3,64,128]{2,1,0:T(8,128)S(1)}, f32[3,64,128]{2,1,0:T(8,128)S(1)}, u32[]{:S(2)}, u32[]{:S(2)}) %collective-permute-start.2) | collective-permute-done | bytes 98336 | tf_op jit(solution)/shard_map/ppermute | solution.py:309
  17.6 2.9 %collective-permute-start.3 = (f32[3,64,128]{2,1,0:T(8,128)S(1)}, f32[3,64,128]{2,1,0:T(8,128)S(1)}, u32[]{:S(2)}, u32[]{:S(2)}) collective-permute-start(f32[3,64,128]{2,1,0:T(8,128)S(1)} %add.50), channel_id=1, source_target_pairs={{0,8},{1,9},{2,10},{3,11},{4,12},{5,13},{6,14},{7,15},{8,0},{9,1},... | collective-permute-start | bytes 294920 | tf_op jit(solution)/shard_map/ppermute | solution.py:309
  20.5 1.3 %collective-permute-start.7 = (f32[2,64,128]{2,1,0:T(8,128)S(1)}, f32[2,64,128]{2,1,0:T(8,128)S(1)}, u32[]{:S(2)}, u32[]{:S(2)}) collective-permute-start(f32[2,64,128]{2,1,0:T(8,128)S(1)} %add.54), channel_id=1, source_target_pairs={{0,8},{1,9},{2,10},{3,11},{4,12},{5,13},{6,14},{7,15},{8,0},{9,1},... | collective-permute-start | bytes 196616 | tf_op jit(solution)/shard_map/ppermute | solution.py:309
  21.8 5.1 %collective-permute-done.7 = f32[2,64,128]{2,1,0:T(8,128)S(1)} collective-permute-done((f32[2,64,128]{2,1,0:T(8,128)S(1)}, f32[2,64,128]{2,1,0:T(8,128)S(1)}, u32[]{:S(2)}, u32[]{:S(2)}) %collective-permute-start.7) | collective-permute-done | bytes 65568 | tf_op jit(solution)/shard_map/ppermute | solution.py:309
  27.0 0.5 %collective-permute-start.8 = (f32[3,64,128]{2,1,0:T(8,128)S(1)}, f32[3,64,128]{2,1,0:T(8,128)S(1)}, u32[]{:S(2)}, u32[]{:S(2)}) collective-permute-start(f32[3,64,128]{2,1,0:T(8,128)S(1)} %add.51), channel_id=1, source_target_pairs={{0,1},{1,0},{2,3},{3,2},{4,5},{5,4},{6,7},{7,6},{8,9},{9,8},{10,11... | collective-permute-start | bytes 294920 | tf_op jit(solution)/shard_map/ppermute | solution.py:309
  27.6 0.6 %collective-permute-done.9 = f32[2,64,128]{2,1,0:T(8,128)S(1)} collective-permute-done((f32[2,64,128]{2,1,0:T(8,128)S(1)}, f32[2,64,128]{2,1,0:T(8,128)S(1)}, u32[]{:S(2)}, u32[]{:S(2)}) %collective-permute-start.9) | collective-permute-done | bytes 65568 | tf_op jit(solution)/shard_map/ppermute | solution.py:309
  28.5 2.1 %middle.1 = (f32[4,64,128]{2,1,0:T(8,128)S(1)}, f32[4,64,128]{2,1,0:T(8,128)S(1)}, f32[4,1024]{1,0:T(4,128)S(1)}, f32[128,128]{1,0:T(8,128)S(1)}) custom-call(s32[2,96]{1,0:T(2,128)S(4)} %get-tuple-element.12.index_ref, bf16[96,256,128]{2,1,0:T(8,128)(2,1)S(1)} %get-tuple-element.13.pair_ref, bf16[96,256,128]{2,1,0:T(8,128)(2,1)S(1)} %get-tuple-element.14.turned_ref, ...), custom_call_target="tpu_custom_call" | custom-call | tf_op jit(solution)/shard_map/middle/pallas_call | solution.py:397
  30.7 0.4 collective-permute-start.10
  31.3 0.8 %collective-permute-done.10 = f32[2,64,128]{2,1,0:T(8,128)S(1)} collective-permute-done((f32[2,64,128]{2,1,0:T(8,128)S(1)}, f32[2,64,128]{2,1,0:T(8,128)S(1)}, u32[]{:S(2)}, u32[]{:S(2)}) %collective-permute-start.10) | collective-permute-done | bytes 65568 | tf_op jit(solution)/shard_map/ppermute | solution.py:309
  32.1 0.4 collective-permute-done.14
  32.4 1.6 %collective-permute-start.11 = (f32[2,64,128]{2,1,0:T(8,128)S(1)}, f32[2,64,128]{2,1,0:T(8,128)S(1)}, u32[]{:S(2)}, u32[]{:S(2)}) collective-permute-start(f32[2,64,128]{2,1,0:T(8,128)S(1)} %get-tuple-element.22), channel_id=1, source_target_pairs={{0,2},{1,3},{2,0},{3,1},{4,6},{5,7},{6,4},{7,5},{8,10},{9,11},{10,... | collective-permute-start | bytes 196616 | tf_op jit(solution)/shard_map/ppermute | solution.py:309
  34.0 0.6 %collective-permute-start.15 = (f32[2,64,128]{2,1,0:T(8,128)S(1)}, f32[2,64,128]{2,1,0:T(8,128)S(1)}, u32[]{:S(2)}, u32[]{:S(2)}) collective-permute-start(f32[2,64,128]{2,1,0:T(8,128)S(1)} %get-tuple-element.23), channel_id=1, source_target_pairs={{0,4},{1,5},{2,6},{3,7},{4,0},{5,1},{6,2},{7,3},{8,12},{9,13},{10,... | collective-permute-start | bytes 196616 | tf_op jit(solution)/shard_map/ppermute | solution.py:309
  34.6 2.2 %collective-permute-done.11 = f32[2,64,128]{2,1,0:T(8,128)S(1)} collective-permute-done((f32[2,64,128]{2,1,0:T(8,128)S(1)}, f32[2,64,128]{2,1,0:T(8,128)S(1)}, u32[]{:S(2)}, u32[]{:S(2)}) %collective-permute-start.11) | collective-permute-done | bytes 65568 | tf_op jit(solution)/shard_map/ppermute | solution.py:309
  36.8 0.6 %collective-permute-start.12 = (f32[2,64,128]{2,1,0:T(8,128)S(1)}, f32[2,64,128]{2,1,0:T(8,128)S(1)}, u32[]{:S(2)}, u32[]{:S(2)}) collective-permute-start(f32[2,64,128]{2,1,0:T(8,128)S(1)} %add.57), channel_id=1, source_target_pairs={{0,4},{1,5},{2,6},{3,7},{4,0},{5,1},{6,2},{7,3},{8,12},{9,13},{10,... | collective-permute-start | bytes 196616 | tf_op jit(solution)/shard_map/ppermute | solution.py:309
  37.4 0.9 %collective-permute-done.15 = f32[2,64,128]{2,1,0:T(8,128)S(1)} collective-permute-done((f32[2,64,128]{2,1,0:T(8,128)S(1)}, f32[2,64,128]{2,1,0:T(8,128)S(1)}, u32[]{:S(2)}, u32[]{:S(2)}) %collective-permute-start.15) | collective-permute-done | bytes 65568 | tf_op jit(solution)/shard_map/ppermute | solution.py:309
  38.3 0.7 %collective-permute-start.16 = (f32[2,64,128]{2,1,0:T(8,128)S(1)}, f32[2,64,128]{2,1,0:T(8,128)S(1)}, u32[]{:S(2)}, u32[]{:S(2)}) collective-permute-start(f32[2,64,128]{2,1,0:T(8,128)S(1)} %add.61), channel_id=1, source_target_pairs={{0,2},{1,3},{2,0},{3,1},{4,6},{5,7},{6,4},{7,5},{8,10},{9,11},{10,... | collective-permute-start | bytes 196616 | tf_op jit(solution)/shard_map/ppermute | solution.py:309
  39.0 2.1 %collective-permute-done.12 = f32[2,64,128]{2,1,0:T(8,128)S(1)} collective-permute-done((f32[2,64,128]{2,1,0:T(8,128)S(1)}, f32[2,64,128]{2,1,0:T(8,128)S(1)}, u32[]{:S(2)}, u32[]{:S(2)}) %collective-permute-start.12) | collective-permute-done | bytes 65568 | tf_op jit(solution)/shard_map/ppermute | solution.py:309
  41.1 1.8 %collective-permute-start.13 = (f32[2,64,128]{2,1,0:T(8,128)S(1)}, f32[2,64,128]{2,1,0:T(8,128)S(1)}, u32[]{:S(2)}, u32[]{:S(2)}) collective-permute-start(f32[2,64,128]{2,1,0:T(8,128)S(1)} %add.58), channel_id=1, source_target_pairs={{0,8},{1,9},{2,10},{3,11},{4,12},{5,13},{6,14},{7,15},{8,0},{9,1},... | collective-permute-start | bytes 196616 | tf_op jit(solution)/shard_map/ppermute | solution.py:309
  42.9 2.1 %collective-permute-start.17 = (f32[2,64,128]{2,1,0:T(8,128)S(1)}, f32[2,64,128]{2,1,0:T(8,128)S(1)}, u32[]{:S(2)}, u32[]{:S(2)}) collective-permute-start(f32[2,64,128]{2,1,0:T(8,128)S(1)} %add.62), channel_id=1, source_target_pairs={{0,8},{1,9},{2,10},{3,11},{4,12},{5,13},{6,14},{7,15},{8,0},{9,1},... | collective-permute-start | bytes 196616 | tf_op jit(solution)/shard_map/ppermute | solution.py:309
  45.0 2.6 %collective-permute-done.13 = f32[2,64,128]{2,1,0:T(8,128)S(1)} collective-permute-done((f32[2,64,128]{2,1,0:T(8,128)S(1)}, f32[2,64,128]{2,1,0:T(8,128)S(1)}, u32[]{:S(2)}, u32[]{:S(2)}) %collective-permute-start.13) | collective-permute-done | bytes 65568 | tf_op jit(solution)/shard_map/ppermute | solution.py:309
  47.7 0.6 %collective-permute-done.17 = f32[2,64,128]{2,1,0:T(8,128)S(1)} collective-permute-done((f32[2,64,128]{2,1,0:T(8,128)S(1)}, f32[2,64,128]{2,1,0:T(8,128)S(1)}, u32[]{:S(2)}, u32[]{:S(2)}) %collective-permute-start.17) | collective-permute-done | bytes 65568 | tf_op jit(solution)/shard_map/ppermute | solution.py:309
  48.4 0.5 %collective-permute-done.18 = f32[2,64,128]{2,1,0:T(8,128)S(1)} collective-permute-done((f32[2,64,128]{2,1,0:T(8,128)S(1)}, f32[2,64,128]{2,1,0:T(8,128)S(1)}, u32[]{:S(2)}, u32[]{:S(2)}) %collective-permute-start.18) | collective-permute-done | bytes 65568 | tf_op jit(solution)/shard_map/ppermute | solution.py:309
  49.0 0.7 %collective-permute-done.19 = f32[2,64,128]{2,1,0:T(8,128)S(1)} collective-permute-done((f32[2,64,128]{2,1,0:T(8,128)S(1)}, f32[2,64,128]{2,1,0:T(8,128)S(1)}, u32[]{:S(2)}, u32[]{:S(2)}) %collective-permute-start.19) | collective-permute-done | bytes 65568 | tf_op jit(solution)/shard_map/ppermute | solution.py:309
  49.7 1.7 %last.1 = (f32[4,1024]{1,0:T(4,128)}, f32[4,1024]{1,0:T(4,128)}) custom-call(s32[2,96]{1,0:T(2,128)S(4)} %get-tuple-element.12.index_ref, bf16[96,256,128]{2,1,0:T(8,128)(2,1)S(1)} %get-tuple-element.13.pair_ref, f32[4,64,128]{2,1,0:T(8,128)S(1)} %pad_maximum_fusion.2.mine_ref, f32[4,64,128]{2,1,0:T(8,128)S(1)} %pad_maximum_fusion.3.other_ref, ...), custom_call_target="tpu_custom_call" | custom-call | tf_op jit(solution)/shard_map/last/pallas_call | solution.py:422
  (37 shorter events, 1.0 us)
Async XLA Ops:
  0.6 27.9 %copy-start = (f32[4,1024]{1,0:T(4,128)S(1)}, f32[4,1024]{1,0:T(4,128)}, u32[]{:S(2)}) copy-start(f32[4,1024]{1,0:T(4,128)} %start_ref.1) | copy-start | bytes 49156
  0.6 27.9 %copy-start.1 = (f32[4,1024]{1,0:T(4,128)S(1)}, f32[4,1024]{1,0:T(4,128)}, u32[]{:S(2)}) copy-start(f32[4,1024]{1,0:T(4,128)} %sino_ref.1) | copy-start | bytes 49156
  5.4 1.5 %collective-permute-start = (f32[3,64,128]{2,1,0:T(8,128)S(1)}, f32[3,64,128]{2,1,0:T(8,128)S(1)}, u32[]{:S(2)}, u32[]{:S(2)}) collective-permute-start(f32[3,64,128]{2,1,0:T(8,128)S(1)} %slice.25), channel_id=1, source_target_pairs={{0,1},{1,0},{2,3},{3,2},{4,5},{5,4},{6,7},{7,6},{8,9},{9,8},{10,11... | collective-permute-start | bytes 294920 | tf_op jit(solution)/shard_map/ppermute | solution.py:309
  5.9 3.9 %collective-permute-start.4 = (f32[2,64,128]{2,1,0:T(8,128)S(1)}, f32[2,64,128]{2,1,0:T(8,128)S(1)}, u32[]{:S(2)}, u32[]{:S(2)}) collective-permute-start(f32[2,64,128]{2,1,0:T(8,128)S(1)} %slice.27), channel_id=1, source_target_pairs={{0,1},{1,0},{2,3},{3,2},{4,5},{5,4},{6,7},{7,6},{8,9},{9,8},{10,11... | collective-permute-start | bytes 196616 | tf_op jit(solution)/shard_map/ppermute | solution.py:309
  6.9 6.0 %collective-permute-start.1 = (f32[3,64,128]{2,1,0:T(8,128)S(1)}, f32[3,64,128]{2,1,0:T(8,128)S(1)}, u32[]{:S(2)}, u32[]{:S(2)}) collective-permute-start(f32[3,64,128]{2,1,0:T(8,128)S(1)} %slice_add_fusion), channel_id=1, source_target_pairs={{0,2},{1,3},{2,0},{3,1},{4,6},{5,7},{6,4},{7,5},{8,10},{9,11},{10,... | collective-permute-start | bytes 294920 | tf_op jit(solution)/shard_map/ppermute | solution.py:309
  9.8 5.0 %collective-permute-start.5 = (f32[2,64,128]{2,1,0:T(8,128)S(1)}, f32[2,64,128]{2,1,0:T(8,128)S(1)}, u32[]{:S(2)}, u32[]{:S(2)}) collective-permute-start(f32[2,64,128]{2,1,0:T(8,128)S(1)} %slice_add_fusion.3), channel_id=1, source_target_pairs={{0,4},{1,5},{2,6},{3,7},{4,0},{5,1},{6,2},{7,3},{8,12},{9,13},{10,... | collective-permute-start | bytes 196616 | tf_op jit(solution)/shard_map/ppermute | solution.py:309
  12.9 4.7 %collective-permute-start.2 = (f32[3,64,128]{2,1,0:T(8,128)S(1)}, f32[3,64,128]{2,1,0:T(8,128)S(1)}, u32[]{:S(2)}, u32[]{:S(2)}) collective-permute-start(f32[3,64,128]{2,1,0:T(8,128)S(1)} %add.49), channel_id=1, source_target_pairs={{0,4},{1,5},{2,6},{3,7},{4,0},{5,1},{6,2},{7,3},{8,12},{9,13},{10,... | collective-permute-start | bytes 294920 | tf_op jit(solution)/shard_map/ppermute | solution.py:309
  14.8 5.7 %collective-permute-start.6 = (f32[2,64,128]{2,1,0:T(8,128)S(1)}, f32[2,64,128]{2,1,0:T(8,128)S(1)}, u32[]{:S(2)}, u32[]{:S(2)}) collective-permute-start(f32[2,64,128]{2,1,0:T(8,128)S(1)} %add.53), channel_id=1, source_target_pairs={{0,2},{1,3},{2,0},{3,1},{4,6},{5,7},{6,4},{7,5},{8,10},{9,11},{10,... | collective-permute-start | bytes 196616 | tf_op jit(solution)/shard_map/ppermute | solution.py:309
  17.6 9.3 %collective-permute-start.3 = (f32[3,64,128]{2,1,0:T(8,128)S(1)}, f32[3,64,128]{2,1,0:T(8,128)S(1)}, u32[]{:S(2)}, u32[]{:S(2)}) collective-permute-start(f32[3,64,128]{2,1,0:T(8,128)S(1)} %add.50), channel_id=1, source_target_pairs={{0,8},{1,9},{2,10},{3,11},{4,12},{5,13},{6,14},{7,15},{8,0},{9,1},... | collective-permute-start | bytes 294920 | tf_op jit(solution)/shard_map/ppermute | solution.py:309
  20.5 6.4 %collective-permute-start.7 = (f32[2,64,128]{2,1,0:T(8,128)S(1)}, f32[2,64,128]{2,1,0:T(8,128)S(1)}, u32[]{:S(2)}, u32[]{:S(2)}) collective-permute-start(f32[2,64,128]{2,1,0:T(8,128)S(1)} %add.54), channel_id=1, source_target_pairs={{0,8},{1,9},{2,10},{3,11},{4,12},{5,13},{6,14},{7,15},{8,0},{9,1},... | collective-permute-start | bytes 196616 | tf_op jit(solution)/shard_map/ppermute | solution.py:309
  26.9 1.3 %collective-permute-start.9 = (f32[2,64,128]{2,1,0:T(8,128)S(1)}, f32[2,64,128]{2,1,0:T(8,128)S(1)}, u32[]{:S(2)}, u32[]{:S(2)}) collective-permute-start(f32[2,64,128]{2,1,0:T(8,128)S(1)} %add.55), channel_id=1, source_target_pairs={{0,1},{1,0},{2,3},{3,2},{4,5},{5,4},{6,7},{7,6},{8,9},{9,8},{10,11... | collective-permute-start | bytes 196616 | tf_op jit(solution)/shard_map/ppermute | solution.py:309
  27.0 1.5 %collective-permute-start.8 = (f32[3,64,128]{2,1,0:T(8,128)S(1)}, f32[3,64,128]{2,1,0:T(8,128)S(1)}, u32[]{:S(2)}, u32[]{:S(2)}) collective-permute-start(f32[3,64,128]{2,1,0:T(8,128)S(1)} %add.51), channel_id=1, source_target_pairs={{0,1},{1,0},{2,3},{3,2},{4,5},{5,4},{6,7},{7,6},{8,9},{9,8},{10,11... | collective-permute-start | bytes 294920 | tf_op jit(solution)/shard_map/ppermute | solution.py:309
  30.7 1.3 %collective-permute-start.10 = (f32[2,64,128]{2,1,0:T(8,128)S(1)}, f32[2,64,128]{2,1,0:T(8,128)S(1)}, u32[]{:S(2)}, u32[]{:S(2)}) collective-permute-start(f32[2,64,128]{2,1,0:T(8,128)S(1)} %get-tuple-element.24), channel_id=1, source_target_pairs={{0,1},{1,0},{2,3},{3,2},{4,5},{5,4},{6,7},{7,6},{8,9},{9,8},{10,11... | collective-permute-start | bytes 196616 | tf_op jit(solution)/shard_map/ppermute | solution.py:309
  31.2 1.3 %collective-permute-start.14 = (f32[2,64,128]{2,1,0:T(8,128)S(1)}, f32[2,64,128]{2,1,0:T(8,128)S(1)}, u32[]{:S(2)}, u32[]{:S(2)}) collective-permute-start(f32[2,64,128]{2,1,0:T(8,128)S(1)} %get-tuple-element.25), channel_id=1, source_target_pairs={{0,1},{1,0},{2,3},{3,2},{4,5},{5,4},{6,7},{7,6},{8,9},{9,8},{10,11... | collective-permute-start | bytes 196616 | tf_op jit(solution)/shard_map/ppermute | solution.py:309
  32.4 4.3 %collective-permute-start.11 = (f32[2,64,128]{2,1,0:T(8,128)S(1)}, f32[2,64,128]{2,1,0:T(8,128)S(1)}, u32[]{:S(2)}, u32[]{:S(2)}) collective-permute-start(f32[2,64,128]{2,1,0:T(8,128)S(1)} %get-tuple-element.22), channel_id=1, source_target_pairs={{0,2},{1,3},{2,0},{3,1},{4,6},{5,7},{6,4},{7,5},{8,10},{9,11},{10,... | collective-permute-start | bytes 196616 | tf_op jit(solution)/shard_map/ppermute | solution.py:309
  34.0 4.3 %collective-permute-start.15 = (f32[2,64,128]{2,1,0:T(8,128)S(1)}, f32[2,64,128]{2,1,0:T(8,128)S(1)}, u32[]{:S(2)}, u32[]{:S(2)}) collective-permute-start(f32[2,64,128]{2,1,0:T(8,128)S(1)} %get-tuple-element.23), channel_id=1, source_target_pairs={{0,4},{1,5},{2,6},{3,7},{4,0},{5,1},{6,2},{7,3},{8,12},{9,13},{10,... | collective-permute-start | bytes 196616 | tf_op jit(solution)/shard_map/ppermute | solution.py:309
  36.8 4.3 %collective-permute-start.12 = (f32[2,64,128]{2,1,0:T(8,128)S(1)}, f32[2,64,128]{2,1,0:T(8,128)S(1)}, u32[]{:S(2)}, u32[]{:S(2)}) collective-permute-start(f32[2,64,128]{2,1,0:T(8,128)S(1)} %add.57), channel_id=1, source_target_pairs={{0,4},{1,5},{2,6},{3,7},{4,0},{5,1},{6,2},{7,3},{8,12},{9,13},{10,... | collective-permute-start | bytes 196616 | tf_op jit(solution)/shard_map/ppermute | solution.py:309
  38.3 4.6 %collective-permute-start.16 = (f32[2,64,128]{2,1,0:T(8,128)S(1)}, f32[2,64,128]{2,1,0:T(8,128)S(1)}, u32[]{:S(2)}, u32[]{:S(2)}) collective-permute-start(f32[2,64,128]{2,1,0:T(8,128)S(1)} %add.61), channel_id=1, source_target_pairs={{0,2},{1,3},{2,0},{3,1},{4,6},{5,7},{6,4},{7,5},{8,10},{9,11},{10,... | collective-permute-start | bytes 196616 | tf_op jit(solution)/shard_map/ppermute | solution.py:309
  41.1 6.5 %collective-permute-start.13 = (f32[2,64,128]{2,1,0:T(8,128)S(1)}, f32[2,64,128]{2,1,0:T(8,128)S(1)}, u32[]{:S(2)}, u32[]{:S(2)}) collective-permute-start(f32[2,64,128]{2,1,0:T(8,128)S(1)} %add.58), channel_id=1, source_target_pairs={{0,8},{1,9},{2,10},{3,11},{4,12},{5,13},{6,14},{7,15},{8,0},{9,1},... | collective-permute-start | bytes 196616 | tf_op jit(solution)/shard_map/ppermute | solution.py:309
  42.9 5.4 %collective-permute-start.17 = (f32[2,64,128]{2,1,0:T(8,128)S(1)}, f32[2,64,128]{2,1,0:T(8,128)S(1)}, u32[]{:S(2)}, u32[]{:S(2)}) collective-permute-start(f32[2,64,128]{2,1,0:T(8,128)S(1)} %add.62), channel_id=1, source_target_pairs={{0,8},{1,9},{2,10},{3,11},{4,12},{5,13},{6,14},{7,15},{8,0},{9,1},... | collective-permute-start | bytes 196616 | tf_op jit(solution)/shard_map/ppermute | solution.py:309
  47.6 1.3 %collective-permute-start.18 = (f32[2,64,128]{2,1,0:T(8,128)S(1)}, f32[2,64,128]{2,1,0:T(8,128)S(1)}, u32[]{:S(2)}, u32[]{:S(2)}) collective-permute-start(f32[2,64,128]{2,1,0:T(8,128)S(1)} %add.59), channel_id=1, source_target_pairs={{0,1},{1,0},{2,3},{3,2},{4,5},{5,4},{6,7},{7,6},{8,9},{9,8},{10,11... | collective-permute-start | bytes 196616 | tf_op jit(solution)/shard_map/ppermute | solution.py:309
  48.3 1.3 %collective-permute-start.19 = (f32[2,64,128]{2,1,0:T(8,128)S(1)}, f32[2,64,128]{2,1,0:T(8,128)S(1)}, u32[]{:S(2)}, u32[]{:S(2)}) collective-permute-start(f32[2,64,128]{2,1,0:T(8,128)S(1)} %add.63), channel_id=1, source_target_pairs={{0,1},{1,0},{2,3},{3,2},{4,5},{5,4},{6,7},{7,6},{8,9},{9,8},{10,11... | collective-permute-start | bytes 196616 | tf_op jit(solution)/shard_map/ppermute | solution.py:309
